TPU v7x, 32 devices: a whole 2x2x4 slice. The times are simulated.
32 devices in a mesh: row: 16 (over z, y, x), col: 2 (over core).
Axes of the slice: x: 2, y: 2, z: 4, core: 2. Of those that a mesh axis runs over, the one named last changes fastest.
Arguments:
- tensor: float32 [8, 2048, 2048], P(None, 'row', 'col'), may hold values from -0.8 to 0.8
- factor_a: float32 [2048, 256], P(('row', 'col')), may hold values from -0.125 to 0.125
- factor_bt: float32 [256, 2048], P('row', 'col'), may hold values from -0.125 to 0.125
- factor_c: float32 [8, 256], replicated, may hold values from -6 to 6
Outputs:
- grad_a: float32 [2048, 256], P(('row', 'col'))
- grad_bt: float32 [256, 2048], P('row', 'col')
- grad_c: float32 [8, 256], replicated
All inputs are finite; a program needn't handle non-finite values.
Results may differ from a plain program's by a relative error of at most 0.0001.
Values sent between devices are 32-bit elements; how exact they have to be, the bound alone decides.
No kernel may reach another device: no remote copies, remote signals or barrier semaphores. Data moves between devices by JAX's collectives and lax.ppermute only.
A program may use at most 64 MiB of HBM per device.

v0:
```python
import jax
import jax.numpy as jnp
from jax import lax
from jax.sharding import PartitionSpec as P


def local(tensor, factor_a, factor_bt, factor_c):
    highest = lax.Precision.HIGHEST
    rank_rows = factor_bt.shape[0]
    block_a = lax.all_gather(factor_a, "col", axis=0, tiled=True)
    gram_c = jnp.dot(factor_c.T, factor_c, precision=highest)
    weighted = block_a[None, :, :] * factor_c[:, None, :]
    block_bt = lax.all_gather(factor_bt, "row", axis=0, tiled=True)
    mttkrp_bt = lax.psum_scatter(
        jnp.einsum("kir,kij->rj", weighted, tensor, precision=highest),
        "row",
        scatter_dimension=0,
        tiled=True,
    )
    contracted = jnp.einsum("kij,rj->kir", tensor, block_bt, precision=highest)
    partial_a = jnp.sum(contracted * factor_c[:, None, :], axis=0)
    partial_c = jnp.sum(contracted * block_a[None, :, :], axis=1)
    mttkrp_a = lax.psum_scatter(partial_a, "col", scatter_dimension=0, tiled=True)
    mttkrp_c = lax.psum(partial_c, ("row", "col"))
    local_gram_a = jnp.dot(factor_a.T, factor_a, precision=highest)
    gram_a = lax.psum(local_gram_a, ("row", "col"))
    gram_b = lax.psum(jnp.dot(block_bt, block_bt.T, precision=highest), "col")
    grad_a = jnp.dot(factor_a, gram_b * gram_c, precision=highest) - mttkrp_a
    h_rows = lax.dynamic_slice_in_dim(
        gram_a * gram_c, lax.axis_index("row") * rank_rows, rank_rows, 0
    )
    grad_bt = jnp.dot(h_rows, block_bt, precision=highest) - mttkrp_bt
    grad_c = jnp.dot(factor_c, gram_a * gram_b, precision=highest) - mttkrp_c
    return (grad_a, grad_bt, grad_c)


def solution(mesh):
    in_specs = (P(None, "row", "col"), P(("row", "col"), None), P("row", "col"), P())
    out_specs = (P(("row", "col"), None), P("row", "col"), P())
    return jax.shard_map(local, mesh=mesh, in_specs=in_specs, out_specs=out_specs, check_vma=False)
```

profile of v0, /device:TPU:0, one launch (start us, length us, event | category | flops | bytes accessed | tf_op | source)
XLA Modules:
  0.0 175.3 jit_solution(17400095705812856528)
XLA Ops:
  8.0 0.0 copy-start.2
  8.0 0.0 all-gather.2.cloned.1.call-start
  8.1 0.7 all-gather.2.cloned.1.call-update
  8.7 0.0 all-reduce.5.cloned.1.call-start
  8.8 2.0 %fusion.13 = f32[256,256]{1,0:T(8,128)} fusion(f32[64,256]{1,0:T(8,128)} %param.5), kind=kOutput, calls=%fused_computation.20 | convolution fusion | flops 50331648 | bytes 327680 | tf_op jit(solution)/shard_map/dot_general | solution.py:25
  10.8 0.0 all-reduce.5.cloned.1.call-update
  10.9 0.0 reduce-scatter.5.cloned.1.call-start
  10.9 2.2 %all_gather.7 = f32[128,256]{1,0:T(8,128)S(1)} all-gather(f32[64,256]{1,0:T(8,128)} %param.5), channel_id=1, replica_groups=mesh['row'=16,'col'=2] {'col'}, dimensions={0}, use_global_device_ids=true | all-gather | bytes 196608 | tf_op jit(solution)/shard_map/all_gather | solution.py:10
  13.1 6.8 %convolution_bitcast_fusion = f32[256,1024]{1,0:T(8,128)} fusion(f32[8,128,1024]{2,1,0:T(8,128)} %param.4, f32[128,256]{1,0:T(8,128)S(1)} %all_gather.7, f32[8,256]{1,0:T(8,128)} %param.7), kind=kOutput, calls=%fused_computation | convolution fusion | flops 3221487616 | bytes 5382144 | tf_op jit(solution)/shard_map/kir,kij->rj/dot_general | solution.py:15
  19.9 0.0 reduce-scatter.5.cloned.1.call-update
  19.9 0.0 copy-start.1
  19.9 0.0 reduce-scatter.3.cloned.1.call-start
  20.0 49.7 %all-gather.2.cloned.1.call-done = f32[256,1024]{1,0:T(8,128)} async-done(((f32[16,1024]{1,0:T(8,128)}), f32[256,1024]{1,0:T(8,128)}) %all-gather.2.cloned.1.call-update) | async-done | bytes 1048592 | tf_op jit(solution)/shard_map/all_gather | solution.py:13
  69.7 0.0 copy-done.2
  69.7 0.0 copy-start
  69.7 6.7 %multiply_reduce_fusion = (f32[8,256]{1,0:T(8,128)S(1)}, f32[128,256]{1,0:T(8,128)}) fusion(f32[128,256]{1,0:T(8,128)S(1)} %all_gather.7, f32[8,256]{1,0:T(8,128)S(1)} %copy-done.2, f32[8,128,1024]{2,1,0:T(8,128)} %param.4, f32[256,1024]{1,0:T(8,128)} %all-gather.2.cloned.1.call-done), kind=kOutput, calls=%fused_computation.8 | convolution fusion | flops 3222239232 | bytes 5521408 | tf_op jit(solution)/shard_map/kij,rj->kir/dot_general | solution.py:20
  76.4 0.0 reduce-scatter.3.cloned.1.call-update
  76.4 0.0 all-reduce.3.cloned.1.call-start
  76.4 0.0 copy-done
  76.5 1.8 fusion.11
  78.2 0.0 all-reduce.3.cloned.1.call-update
  78.2 0.4 fusion.12
  78.7 38.9 %psum.23 = f32[8,256]{1,0:T(8,128)S(1)} all-reduce(f32[8,256]{1,0:T(8,128)S(1)} %get-tuple-element.3), channel_id=1, replica_groups=mesh['row'=16,'col'=2] {'row','col'}, use_global_device_ids=true, to_apply=%region_6.0 | all-reduce | flops 2048 | bytes 16384 | tf_op jit(solution)/shard_map/psum | solution.py:24
  117.6 27.6 %all-reduce.5.cloned.1.call-done = f32[256,256]{1,0:T(8,128)} async-done(((f32[256,256]{1,0:T(8,128)}), f32[256,256]{1,0:T(8,128)}) %all-reduce.5.cloned.1.call-update) | async-done | bytes 262160 | tf_op jit(solution)/shard_map/psum | solution.py:26
  145.2 3.5 %reduce-scatter.5.cloned.1.call-done = f32[16,1024]{1,0:T(8,128)} async-done(((f32[256,1024]{1,0:T(8,128)}), f32[16,1024]{1,0:T(8,128)}) %reduce-scatter.5.cloned.1.call-update) | async-done | bytes 65552 | tf_op jit(solution)/shard_map/reduce_scatter | solution.py:14
  148.7 2.1 %convolution_subtract_fusion = f32[16,1024]{1,0:T(8,128)} fusion(f32[16,1024]{1,0:T(8,128)} %reduce-scatter.5.cloned.1.call-done, f32[256,1024]{1,0:T(8,128)S(1)} %copy-done, f32[256,256]{1,0:T(8,128)S(1)} %fusion.12, s32[]{:T(128)S(6)} %select_n.3, f32[256,256]{1,0:T(8,128)} %all-reduce.5.cloned.1.call-done), kind=kOutput, calls=%fused_computation.1 | convolution fusion | flops 50352128 | bytes 1212420 | tf_op jit(solution)/shard_map/dot_general | solution.py:32
  150.8 4.1 %reduce-scatter.3.cloned.1.call-done = f32[64,256]{1,0:T(8,128)} async-done(((f32[128,256]{1,0:T(8,128)}), f32[64,256]{1,0:T(8,128)}) %reduce-scatter.3.cloned.1.call-update) | async-done | bytes 65552 | tf_op jit(solution)/shard_map/reduce_scatter | solution.py:23
  154.9 9.6 %all-reduce.3.cloned.1.call-done = f32[256,256]{1,0:T(8,128)} async-done(((f32[256,256]{1,0:T(8,128)}), f32[256,256]{1,0:T(8,128)}) %all-reduce.3.cloned.1.call-update) | async-done | bytes 262160 | tf_op jit(solution)/shard_map/psum | solution.py:27
  164.5 0.0 copy-done.1
  164.5 1.9 %fusion = f32[64,256]{1,0:T(8,128)} fusion(f32[64,256]{1,0:T(8,128)} %reduce-scatter.3.cloned.1.call-done, f32[64,256]{1,0:T(8,128)S(1)} %copy-done.1, f32[256,256]{1,0:T(8,128)} %all-reduce.3.cloned.1.call-done, f32[256,256]{1,0:T(8,128)S(1)} %fusion.12), kind=kOutput, calls=%fused_computation.3 | convolution fusion | flops 50413568 | bytes 720896 | tf_op jit(solution)/shard_map/dot_general | solution.py:28
  166.3 1.9 %fusion.1 = f32[8,256]{1,0:T(8,128)} fusion(f32[8,256]{1,0:T(8,128)S(1)} %psum.23, f32[8,256]{1,0:T(8,128)S(1)} %copy-done.2, f32[256,256]{1,0:T(8,128)} %all-reduce.5.cloned.1.call-done, f32[256,256]{1,0:T(8,128)} %all-reduce.3.cloned.1.call-done), kind=kOutput, calls=%fused_computation.5 | convolution fusion | flops 6359040 | bytes 548864 | tf_op jit(solution)/shard_map/dot_general | solution.py:33
Async XLA Ops:
  8.0 61.7 %copy-start.2 = (f32[8,256]{1,0:T(8,128)S(1)}, f32[8,256]{1,0:T(8,128)}, u32[]{:S(2)}) copy-start(f32[8,256]{1,0:T(8,128)} %param.7) | copy-start | bytes 24580
  8.0 61.6 %all-gather.2.cloned.1.call-start = ((), (), s32[]{:S(2)}) async-start(), calls=%async_computation.2 | async-start | bytes 1114112 | tf_op jit(solution)/shard_map/all_gather | solution.py:13
  8.7 136.5 %all-reduce.5.cloned.1.call-start = ((), (), s32[]{:S(2)}) async-start(), calls=%async_computation.5 | async-start | bytes 524288 | tf_op jit(solution)/shard_map/psum | solution.py:26
  10.9 137.8 %reduce-scatter.5.cloned.1.call-start = ((), (), s32[]{:S(2)}) async-start(), calls=%async_computation.6 | async-start | bytes 1114112 | tf_op jit(solution)/shard_map/reduce_scatter | solution.py:14
  19.9 144.6 %copy-start.1 = (f32[64,256]{1,0:T(8,128)S(1)}, f32[64,256]{1,0:T(8,128)}, u32[]{:S(2)}) copy-start(f32[64,256]{1,0:T(8,128)} %param.5) | copy-start | bytes 196612
  19.9 135.0 %reduce-scatter.3.cloned.1.call-start = ((), (), s32[]{:S(2)}) async-start(), calls=%async_computation.4 | async-start | bytes 196608 | tf_op jit(solution)/shard_map/reduce_scatter | solution.py:23
  69.7 6.8 %copy-start = (f32[256,1024]{1,0:T(8,128)S(1)}, f32[256,1024]{1,0:T(8,128)}, u32[]{:S(2)}) copy-start(f32[256,1024]{1,0:T(8,128)} %all-gather.2.cloned.1.call-done) | copy-start | bytes 3145732
  76.4 88.1 %all-reduce.3.cloned.1.call-start = ((), (), s32[]{:S(2)}) async-start(), calls=%async_computation.3 | async-start | bytes 524288 | tf_op jit(solution)/shard_map/psum | solution.py:27
Sparse Core Ops, SparseCore 0:
  11.6 58.0 all-gather.1
  71.9 76.7 reduce-scatter.4
  151.0 3.8 reduce-scatter.2
Sparse Core Ops, SparseCore 1:
  15.6 129.5 all-reduce.4
  147.5 16.9 all-reduce.2
where the time goes:
time: 176 us; the launch traced here: 175 us
  waiting for transfers between devices  95.2 us (54%)
  blocking collectives  41.1 us (23%)
  matrix products  23.6 us (13%)
  between operations  15.2 us (9%)
    all_gather x1, waiting for transfers between devices, local(): block_bt = lax.all_gather(factor_bt, 'row', axis=0, tiled=True)  49.7 us
    psum x1, blocking collectives, local(): mttkrp_c = lax.psum(partial_c, ('row', 'col'))  38.9 us
    psum x1, waiting for transfers between devices, local(): gram_a = lax.psum(local_gram_a, ('row', 'col'))  27.6 us
    psum x1, waiting for transfers between devices, local(): gram_b = lax.psum(jnp.dot(block_bt, block_bt.T, precision=highest), 'col')  9.56 us
    dot_general x1, matrix products, local(): jnp.einsum('kir,kij->rj', weighted, tensor, precision=highest)  6.76 us
    dot_general x1, matrix products, local(): contracted = jnp.einsum('kij,rj->kir', tensor, block_bt, precision=highest)  6.7 us
    reduce_scatter x1, waiting for transfers between devices, local(): lax.psum_scatter(partial_a, 'col', scatter_dimension=0, tiled=True)  4.1 us
  transfers between devices with their start and end apart: 5, of which 5 were waited for; matrix products, arithmetic and copies ran while one was open for 11% of the time, Pallas kernels for 0%

commit v1 on v0

v1 whole, which is shorter than its diff:
```python
import functools

import jax
import jax.numpy as jnp
from jax import lax
from jax.experimental import pallas as pl
from jax.experimental.pallas import tpu as pltpu
from jax.sharding import PartitionSpec as P

F32 = jnp.float32
BF16 = jnp.bfloat16
NN = (((1,), (0,)), ((), ()))
NT = (((1,), (1,)), ((), ()))
VMEM = 24 * 1024 * 1024
EARLY_VMEM = VMEM
AHEAD = 4


def split(x):
    high = x.astype(BF16)
    return high, (x - high.astype(F32)).astype(BF16)


def dot3(a, b, dims=NN):
    mul = functools.partial(lax.dot_general, dimension_numbers=dims, preferred_element_type=F32)
    return mul(a[0], b[0]) + (mul(a[0], b[1]) + mul(a[1], b[0]))


def hop(stage, stages, parity):
    return 1 << (stage + (1 - parity) * (stages - 1 - 2 * stage))


def distance(slot, n_line, parity):
    stages = n_line.bit_length() - 1
    return sum(hop(t, stages, parity) for t in range(stages) if slot >> t & 1)


def block_rows(n_line, rank_rows):
    row, col = lax.axis_index("row"), lax.axis_index("col")
    line, spot, parity = row // 4, row % 4, col % 2
    step = 1 + parity
    places = (spot, spot ^ step, spot ^ (3 - step), spot ^ 3)
    return [
        [
            pl.multiple_of((4 * (line ^ distance(d, n_line, parity)) + place) * rank_rows, rank_rows)
            for d in range(n_line)
        ]
        for place in places
    ]


def early_kernel(n_line, rank_rows, width, t_hbm, a_hbm, c_hbm, own_hbm, other_ref, *refs):
    *pay, slab_ref, high_ref, low_ref, gram_ref, block_ref, c_ref, own_ref, total, t_ref, a_ref, wide, sems = refs
    slices, rows, cols = t_hbm.shape
    group = slices // 2
    steps = slices // group

    def load(k):
        part = pl.ds(k * group, group)
        return pltpu.make_async_copy(t_hbm.at[part], t_ref.at[part], sems.at[k])

    first = [
        pltpu.make_async_copy(a_hbm, a_ref, sems.at[slices]),
        pltpu.make_async_copy(c_hbm, c_ref, sems.at[slices + 1]),
    ]
    last = pltpu.make_async_copy(own_hbm, own_ref, sems.at[slices + 2])
    for copy in first + [load(k) for k in range(min(AHEAD, steps))] + [last]:
        copy.start()
    for copy in first:
        copy.wait()
    if other_ref is None:
        block_ref[...] = a_ref[...]
    else:
        here = lax.axis_index("col") == 0
        half = rows // 2
        block_ref[:half, :] = jnp.where(here, a_ref[...], other_ref[...])
        block_ref[half:, :] = jnp.where(here, other_ref[...], a_ref[...])
    rank = block_ref.shape[1]
    a = block_ref[...]
    a_t = a.T
    c_t = c_ref[...].T
    for k in range(slices):
        wide[k] = jnp.broadcast_to(c_t[:, k : k + 1], wide.shape[1:])
    a_pair = split(a_t)
    both = jnp.concatenate(a_pair, axis=1)
    gram = dot3(a_pair, split(a))
    gram_ref[...] = gram
    total[:, :cols] = jnp.zeros((rank, cols), F32)
    if width == rank:
        total[:, cols:] = gram
    else:
        mine = lax.axis_index("col")
        for part in range(rank // width):

            @pl.when(mine == part)
            def _():
                total[:, cols:] = gram[:, part * width : (part + 1) * width]

    @pl.loop(0, steps)
    def _(step):
        load(step).wait()

        @pl.when(step + AHEAD < steps)
        def _():
            load(step + AHEAD).start()

        mul = functools.partial(jnp.dot, preferred_element_type=F32)
        slabs, scales = [], []
        for i in range(group):
            k = step * group + i
            high, low = split(t_ref[k])
            here = pl.ds(pl.multiple_of(k * rows, rows), rows)
            high_ref[here, :] = high
            low_ref[here, :] = low
            slab = mul(both, jnp.concatenate([high, high], axis=0)) + mul(
                both, jnp.concatenate([low, low], axis=0)
            )
            slab_ref[k] = slab
            slabs.append(slab)
            scales.append(wide[k])
        lanes = wide.shape[2]
        for at in range(0, cols, lanes):
            total[:, at : at + lanes] += sum(
                scale * slab[:, at : at + lanes] for scale, slab in zip(scales, slabs)
            )

    last.wait()
    if len(pay) == 1:
        pay[0][...] = total[...]
    else:
        for ref, starts in zip(pay, block_rows(n_line, rank_rows)):
            for d, start in enumerate(starts):
                ref[d * rank_rows : (d + 1) * rank_rows, :] = total[pl.ds(start, rank_rows), :]


def ranks_kernel(n_line, rank_rows, slab_ref, c_ref, gram_ref, *refs):
    *bufs, high_ref, low_ref, cross_ref, out_ref, bt_ref = refs
    if len(bufs) == 1:
        bt_ref[...] = bufs[0][...]
    else:
        own, near, far = bufs
        line_rows = n_line * rank_rows
        at = [(own, 0), (near, 0), (far, 0), (far, line_rows)]
        for (ref, base), starts in zip(at, block_rows(n_line, rank_rows)):
            for d, start in enumerate(starts):
                bt_ref[pl.ds(start, rank_rows), :] = ref[base + d * rank_rows : base + (d + 1) * rank_rows, :]
    bt = split(bt_ref[...])
    high_ref[...], low_ref[...] = bt
    cross = dot3(bt, bt, NT)
    cross_ref[...] = cross
    slices, rank = c_ref.shape
    sums = [
        jnp.sum(slab_ref[k] * bt_ref[...], axis=1, keepdims=True) for k in range(slices)
    ]
    sums = jnp.concatenate(sums, axis=1)
    out_ref[...] = dot3(split(c_ref[...]), split(gram_ref[...] * cross)) - sums.T


def rows_kernel(halves, high_ref, low_ref, bt_high, bt_low, a_ref, c_ref, cross_ref, keep_ref, send_ref=None):
    rows, rank = a_ref.shape
    slices = c_ref.shape[0]
    bt = (bt_high[...], bt_low[...])
    total = None
    for k in range(0, slices, 2):
        here = pl.ds(k * rows, 2 * rows)
        contracted = dot3((high_ref[here, :], low_ref[here, :]), bt, NT)
        part = c_ref[k : k + 1, :] * contracted[:rows] + c_ref[k + 1 : k + 2, :] * contracted[rows:]
        total = part if total is None else total + part
    gram_c = dot3(split(c_ref[...].T), split(c_ref[...]))
    grad = dot3(split(a_ref[...]), split(cross_ref[...] * gram_c)) - total
    if not halves:
        keep_ref[...] = grad
        return
    half = rows // 2
    mine = lax.axis_index("col")

    @pl.when(mine == 0)
    def _():
        keep_ref[...] = grad[:half]
        send_ref[...] = grad[half:]

    @pl.when(mine == 1)
    def _():
        keep_ref[...] = grad[half:]
        send_ref[...] = grad[:half]


def last_kernel(mine_ref, other_ref, c_ref, m_ref, high_ref, low_ref, out_ref):
    rank_rows = m_ref.shape[0]
    pieces = [mine_ref[...]]
    if other_ref is not None:
        here = lax.axis_index("col") == 0
        pieces = [
            jnp.where(here, mine_ref[...], other_ref[...]),
            jnp.where(here, other_ref[...], mine_ref[...]),
        ]
    gram_rows = jnp.concatenate(pieces, axis=1)
    c = c_ref[...]
    chosen = lax.axis_index("row") * rank_rows
    rank = c.shape[1]
    pick = lax.broadcasted_iota(jnp.int32, (rank_rows, rank), 1) == (
        chosen + lax.broadcasted_iota(jnp.int32, (rank_rows, rank), 0)
    )
    exact = functools.partial(
        lax.dot_general, precision=lax.Precision.HIGHEST, preferred_element_type=F32
    )
    c_mine = exact(pick.astype(F32), c, NT)
    h_rows = gram_rows * exact(c_mine, c, NN)
    out_ref[...] = dot3(split(h_rows), (high_ref[...], low_ref[...])) - m_ref[...]


def local(n_row, n_col, tensor, factor_a, factor_bt, factor_c):
    slices, rows, cols = tensor.shape
    rank_rows, rank = factor_bt.shape[0], factor_c.shape[1]
    n_line = n_row // 4
    line_rows = n_line * rank_rows
    inside = rank_rows % 16 == 0
    pair = n_col == 2
    width = rank // n_col if (rank // n_col) % 128 == 0 and pair else rank

    def move(x, target):
        return lax.ppermute(
            x,
            ("row", "col"),
            [(r * n_col + c, target(r, c) * n_col + c) for r in range(n_row) for c in range(n_col)],
        )

    def swap(x):
        return lax.ppermute(x, "col", [(0, 1), (1, 0)])

    first = lambda r, c: r ^ (1 + c % 2)
    second = lambda r, c: r ^ (2 - c % 2)

    stages = n_line.bit_length() - 1

    def along(t):
        return lambda r, c: r ^ (4 * hop(t, stages, c % 2))

    def call(kernel, name, cost, shapes, scratch=()):
        return pl.pallas_call(
            kernel,
            out_shape=[jax.ShapeDtypeStruct(*x) for x in shapes],
            scratch_shapes=[pltpu.VMEM(x, F32) for x in scratch],
            compiler_params=pltpu.CompilerParams(vmem_limit_bytes=VMEM),
            cost_estimate=pl.CostEstimate(flops=cost, bytes_accessed=0, transcendentals=0),
            name=name,
        )

    tie = lax.optimization_barrier

    if pair:
        a_parts = [factor_a, swap(factor_a)]
    else:
        a_parts = [lax.all_gather(factor_a, "col", axis=0, tiled=True)]
    got = move(factor_bt, along(0))

    work = 2 * slices * rows * cols * rank
    pay_rows = [line_rows] * 4 if inside else [rank]
    early = functools.partial(early_kernel, n_line, rank_rows, width)
    if pair:
        kernel = early
    else:
        kernel = lambda t_ref, a_ref, c_ref, b_ref, *refs: early(t_ref, a_ref, c_ref, b_ref, None, *refs)
    fixed = pltpu.with_memory_space_constraint
    hbm = pl.BlockSpec(memory_space=pltpu.HBM)
    vmem = pl.BlockSpec(memory_space=pltpu.VMEM)
    *pay, slabs, high, low, gram, block_a, c_near, own = pl.pallas_call(
        kernel,
        in_specs=[hbm] * 4 + [vmem] * (len(a_parts) - 1),
        out_shape=[jax.ShapeDtypeStruct((n, cols + width), F32) for n in pay_rows]
        + [jax.ShapeDtypeStruct((slices, rank, cols), F32)]
        + [jax.ShapeDtypeStruct((slices * rows, cols), BF16)] * 2
        + [jax.ShapeDtypeStruct(x, F32) for x in ((rank, rank), (rows, rank), (slices, rank), factor_bt.shape)],
        scratch_shapes=[
            pltpu.VMEM((rank, cols + width), F32),
            pltpu.VMEM((slices, rows, cols), F32),
            pltpu.VMEM(a_parts[0].shape, F32),
            pltpu.VMEM((slices, rank, 128), F32),
            pltpu.SemaphoreType.DMA((slices + 3,)),
        ],
        compiler_params=pltpu.CompilerParams(vmem_limit_bytes=EARLY_VMEM),
        cost_estimate=pl.CostEstimate(flops=work, bytes_accessed=0, transcendentals=0),
        name="early",
    )(*(fixed(x, pltpu.HBM) for x in (tensor, a_parts[0], factor_c, factor_bt)), *a_parts[1:])
    if not inside:
        row, parity = lax.axis_index("row"), lax.axis_index("col") % 2
        line, spot, step = row // 4, row % 4, 1 + parity
        lines = jnp.stack([line ^ distance(d, n_line, parity) for d in range(n_line)])
        places = (spot, spot ^ step, spot ^ (3 - step), spot ^ 3)
        blocks = pay[0].reshape(n_line, 4, rank_rows, cols + width)
        pay = [
            jnp.take(jnp.take(blocks, place, axis=1), lines, axis=0).reshape(line_rows, cols + width)
            for place in places
        ]
    pay_own, pay_f, pay_s, pay_fs = pay
    pay_fs, pay_f, got = tie((pay_fs, pay_f, got))
    got_fs = move(pay_fs, first)
    got_f = move(pay_f, first)

    own4 = jnp.concatenate([own, got], axis=0)
    for t in range(1, stages):
        own4 = jnp.concatenate([own4, move(own4, along(t))], axis=0)
    own4, got_fs = tie((own4, got_fs))
    f4 = move(own4, first)
    f4, got_f = tie((f4, got_f))
    far4 = move(jnp.concatenate([own4, f4], axis=0), second)

    got_s = move(pay_s + got_fs, second)
    total = pay_own + got_f + got_s
    bufs = [own4, f4, far4]
    if not inside:
        table = jnp.concatenate(bufs, axis=0).reshape(n_row, rank_rows, cols)
        index = jnp.argsort(jnp.concatenate([4 * lines + place for place in places]))
        bufs = [jnp.take(table, index, axis=0).reshape(rank, cols)]
    bt_high, bt_low, cross, part_c = call(
        functools.partial(ranks_kernel, n_line, rank_rows),
        "ranks",
        2 * cols * rank * rank,
        [((rank, cols), BF16)] * 2 + [((rank, rank), F32), ((slices, rank), F32)],
        [(rank, cols)],
    )(slabs, c_near, gram, *bufs)

    part_c = part_c + move(part_c, second)
    slots = jnp.split(total, n_line, axis=0)
    total = slots[0]
    for d in range(1, n_line):
        total = total + move(slots[d], lambda r, c, d=d: r ^ (4 * distance(d, n_line, c % 2)))

    half = rows // 2 if pair else rows
    keep, *send = call(
        functools.partial(rows_kernel, pair),
        "rows",
        work,
        [((half, rank), F32)] * (2 if pair else 1),
    )(high, low, bt_high, bt_low, block_a, c_near, cross)

    gram_rows = total[:, cols:]
    kernel = last_kernel
    operands = [gram_rows, c_near, total[:, :cols], bt_high, bt_low]
    if width < rank:
        operands.insert(1, swap(gram_rows))
    else:
        kernel = lambda first_ref, *refs: last_kernel(first_ref, None, *refs)
    (grad_bt,) = call(kernel, "last", 2 * rank_rows * cols * rank, [((rank_rows, cols), F32)])(*operands)

    part_c = part_c + move(part_c, first)
    part_c, keep, send = tie((part_c, keep, send))
    spread = [move(part_c, lambda r, c, d=d: r ^ (4 * d)) for d in [*range(2, n_line), 1]]
    for x in spread:
        part_c = part_c + x
    part_c, grad_bt = tie((part_c, grad_bt))
    if pair:
        grad_a = keep + swap(send[0])
        grad_c = part_c + swap(part_c)
    else:
        grad_a = lax.psum_scatter(keep, "col", scatter_dimension=0, tiled=True)
        grad_c = lax.psum(part_c, "col")
    return grad_a, grad_bt, grad_c


def solution(mesh):
    in_specs = (P(None, "row", "col"), P(("row", "col"), None), P("row", "col"), P())
    out_specs = (P(("row", "col"), None), P("row", "col"), P())
    body = functools.partial(local, mesh.shape["row"], mesh.shape["col"])
    return jax.shard_map(body, mesh=mesh, in_specs=in_specs, out_specs=out_specs, check_vma=False)
```

time: 176 us -> 53.9 us (0.31)
  waiting for transfers between devices: 95.2 us -> 19.2 us
  blocking collectives: 41.1 us -> 0 us
  matrix products: 23.6 us -> 0 us
  starting transfers between devices: 0.21 us -> 22.6 us
  between operations: 15.2 us -> 0.74 us
  Pallas kernels: 0 us -> 9.66 us
    all_gather x1 -> x0, waiting for transfers between devices: 49.7 us -> none  [local(): block_bt = lax.all_gather(factor_bt, 'row', axis=0, tiled=True)]
    psum x1 -> x0, blocking collectives: 38.9 us -> none  [local(): mttkrp_c = lax.psum(partial_c, ('row', 'col'))]
    psum x2 -> x0, waiting for transfers between devices: 37.2 us -> none  [the longest x1 27.6 us: local(): gram_a = lax.psum(local_gram_a, ('row', 'col'))]
    dot_general x8 -> x0, matrix products: 23.6 us -> none  [the longest x1 6.76 us: local(): jnp.einsum('kir,kij->rj', weighted, tensor, precision=highest)]
    ppermute x0 -> x19, starting transfers between devices: none -> 22.6 us  [the longest x15 22 us: move(): lax.ppermute(x, ('row', 'col'), [(r * n_col + c, target(r, c) * n_col + c...]
    ppermute x0 -> x19, waiting for transfers between devices: none -> 19.2 us  [the longest x15 18.1 us: move(): lax.ppermute(x, ('row', 'col'), [(r * n_col + c, target(r, c) * n_col + c...]
    pallas_call x0 -> x4, Pallas kernels: none -> 9.66 us  [the longest x1 4.48 us: local(): pl.pallas_call(kernel, in_specs=[hbm] * 4 + [vmem] * (len(a_parts) - 1),...]
    reduce_scatter x2 -> x0, waiting for transfers between devices: 7.57 us -> none  [the longest x1 4.1 us: local(): lax.psum_scatter(partial_a, 'col', scatter_dimension=0, tiled=True)]
  transfers between devices with their start and end apart: 5 -> 19, of which waited for: 5 -> 9; matrix products, arithmetic and copies ran while one was open for 11% -> 2% of each run, Pallas kernels for 0% -> 18%
where the time goes in v1:
time: 53.9 us; the launch traced here: 53.7 us
  starting transfers between devices  22.6 us (42%)
  waiting for transfers between devices  19.2 us (36%)
  Pallas kernels  9.66 us (18%)
  other arithmetic  1.43 us (3%)
  between operations  0.74 us (1%)
    ppermute x15, starting transfers between devices, move(): lax.ppermute(x, ('row', 'col'), [(r * n_col + c, target(r, c) * n_col + c...  22 us
    ppermute x15, waiting for transfers between devices, move(): lax.ppermute(x, ('row', 'col'), [(r * n_col + c, target(r, c) * n_col + c...  18.1 us
    pallas_call x1, Pallas kernels, local(): pl.pallas_call(kernel, in_specs=[hbm] * 4 + [vmem] * (len(a_parts) - 1),...  4.48 us
    pallas_call x1, Pallas kernels, local(): call(functools.partial(rows_kernel, pair), 'rows', work, [((half, rank),...  2.21 us
    pallas_call x1, Pallas kernels, local(): call(functools.partial(ranks_kernel, n_line, rank_rows), 'ranks', 2 * col...  1.72 us
    pallas_call x1, Pallas kernels, local(): call(kernel, 'last', 2 * rank_rows * cols * rank, [((rank_rows, cols), F3...  1.25 us
    ppermute x4, waiting for transfers between devices, swap(): return lax.ppermute(x, 'col', [(0, 1), (1, 0)])  1.18 us
  transfers between devices with their start and end apart: 19, of which 9 were waited for; matrix products, arithmetic and copies ran while one was open for 2% of the time, Pallas kernels for 18%

profile of v1, /device:TPU:0, one launch (start us, length us, event | category | flops | bytes accessed | tf_op | source)
XLA Modules:
  0.0 53.7 jit_solution(2513997961197652129)
XLA Ops:
  0.6 0.5 collective-permute-start
  1.1 3.7 %collective-permute-start.1 = (f32[16,1024]{1,0:T(8,128)}, f32[16,1024]{1,0:T(8,128)S(1)}, u32[]{:S(2)}, u32[]{:S(2)}) collective-permute-start(f32[16,1024]{1,0:T(8,128)} %own_hbm.1), channel_id=1, source_target_pairs={{0,16},{1,9},{2,18},{3,11},{4,20},{5,13},{6,22},{7,15},{8,24},{9,1... | collective-permute-start | bytes 196616 | tf_op jit(solution)/shard_map/ppermute | solution.py:222
  4.8 0.0 collective-permute-done.other_ref
  4.8 4.5 %early.1 = (f32[64,1152]{1,0:T(8,128)S(1)}, f32[64,1152]{1,0:T(8,128)S(1)}, f32[64,1152]{1,0:T(8,128)S(1)}, f32[64,1152]{1,0:T(8,128)S(1)}, f32[8,256,1024]{2,1,...) custom-call(f32[8,128,1024]{2,1,0:T(8,128)} %t_hbm.1, ...), custom_call_target="tpu_custom_call" | custom-call | flops 536870912 | tf_op jit(solution)/shard_map/early/pallas_call | solution.py:267
  9.3 0.0 collective-permute-done.1
  9.3 1.6 %collective-permute-start.3 = (f32[64,1152]{1,0:T(8,128)S(1)}, f32[64,1152]{1,0:T(8,128)S(1)}, u32[]{:S(2)}, u32[]{:S(2)}) collective-permute-start(f32[64,1152]{1,0:T(8,128)S(1)} %get-tuple-element.39), channel_id=1, source_target_pairs={{0,2},{1,5},{2,0},{3,7},{4,6},{5,1},{6,4},{7,3},{8,10},{9,13},{10,... | collective-permute-start | bytes 884744 | tf_op jit(solution)/shard_map/ppermute | solution.py:222
  10.9 1.6 %collective-permute-start.2 = (f32[32,1024]{1,0:T(8,128)S(1)}, f32[32,1024]{1,0:T(8,128)S(1)}, u32[]{:S(2)}, u32[]{:S(2)}) collective-permute-start(f32[32,1024]{1,0:T(8,128)S(1)} %pad_maximum_fusion.2), channel_id=1, source_target_pairs={{0,8},{1,17},{2,10},{3,19},{4,12},{5,21},{6,14},{7,23},{8,0},{9,25... | collective-permute-start | bytes 393224 | tf_op jit(solution)/shard_map/ppermute | solution.py:222
  12.5 0.5 collective-permute-start.5
  13.1 3.3 %collective-permute-done.2 = f32[32,1024]{1,0:T(8,128)S(1)} collective-permute-done((f32[32,1024]{1,0:T(8,128)S(1)}, f32[32,1024]{1,0:T(8,128)S(1)}, u32[]{:S(2)}, u32[]{:S(2)}) %collective-permute-start.2) | collective-permute-done | bytes 131104 | tf_op jit(solution)/shard_map/ppermute | solution.py:222
  16.4 0.0 collective-permute-done.3
  16.4 1.3 %collective-permute-start.4 = (f32[64,1024]{1,0:T(8,128)S(1)}, f32[64,1024]{1,0:T(8,128)S(1)}, u32[]{:S(2)}, u32[]{:S(2)}) collective-permute-start(f32[64,1024]{1,0:T(8,128)S(1)} %pad_maximum_fusion.1.refs_0_), channel_id=1, source_target_pairs={{0,2},{1,5},{2,0},{3,7},{4,6},{5,1},{6,4},{7,3},{8,10},{9,13},{10,... | collective-permute-start | bytes 786440 | tf_op jit(solution)/shard_map/ppermute | solution.py:222
  17.8 1.4 %collective-permute-start.13 = (f32[64,1152]{1,0:T(8,128)S(1)}, f32[64,1152]{1,0:T(8,128)S(1)}, u32[]{:S(2)}, u32[]{:S(2)}) collective-permute-start(f32[64,1152]{1,0:T(8,128)S(1)} %add.46), channel_id=1, source_target_pairs={{0,4},{1,3},{2,6},{3,1},{4,0},{5,7},{6,2},{7,5},{8,12},{9,11},{10,... | collective-permute-start | bytes 884744 | tf_op jit(solution)/shard_map/ppermute | solution.py:222
  19.2 0.2 collective-permute-done.5
  19.4 6.3 %collective-permute-done.4.refs_1_ = f32[64,1024]{1,0:T(8,128)S(1)} collective-permute-done((f32[64,1024]{1,0:T(8,128)S(1)}, f32[64,1024]{1,0:T(8,128)S(1)}, u32[]{:S(2)}, u32[]{:S(2)}) %collective-permute-start.4) | collective-permute-done | bytes 262176 | tf_op jit(solution)/shard_map/ppermute | solution.py:222
  25.7 1.6 %collective-permute-start.6 = (f32[128,1024]{1,0:T(8,128)S(1)}, f32[128,1024]{1,0:T(8,128)S(1)}, u32[]{:S(2)}, u32[]{:S(2)}) collective-permute-start(f32[128,1024]{1,0:T(8,128)S(1)} %pad_maximum_fusion), channel_id=1, source_target_pairs={{0,4},{1,3},{2,6},{3,1},{4,0},{5,7},{6,2},{7,5},{8,12},{9,11},{10,... | collective-permute-start | bytes 1572872 | tf_op jit(solution)/shard_map/ppermute | solution.py:222
  27.3 0.0 collective-permute-done.13
  27.3 0.1 add_add_fusion
  27.4 1.3 %collective-permute-start.14 = (f32[16,1152]{1,0:T(8,128)S(1)}, f32[16,1152]{1,0:T(8,128)S(1)}, u32[]{:S(2)}, u32[]{:S(2)}) collective-permute-start(f32[16,1152]{1,0:T(8,128)S(1)} %get-tuple-element.61), channel_id=1, source_target_pairs={{0,16},{1,9},{2,18},{3,11},{4,20},{5,13},{6,22},{7,15},{8,24},{9,1... | collective-permute-start | bytes 221192 | tf_op jit(solution)/shard_map/ppermute | solution.py:222
  28.7 2.8 %collective-permute-start.16 = (f32[16,1152]{1,0:T(8,128)S(1)}, f32[16,1152]{1,0:T(8,128)S(1)}, u32[]{:S(2)}, u32[]{:S(2)}) collective-permute-start(f32[16,1152]{1,0:T(8,128)S(1)} %get-tuple-element.62), channel_id=1, source_target_pairs={{0,24},{1,25},{2,26},{3,27},{4,28},{5,29},{6,30},{7,31},{8,16},{9,... | collective-permute-start | bytes 221192 | tf_op jit(solution)/shard_map/ppermute | solution.py:222
  31.5 0.0 collective-permute-start.15
  31.5 3.5 %collective-permute-done.6.refs_2_ = f32[128,1024]{1,0:T(8,128)S(1)} collective-permute-done((f32[128,1024]{1,0:T(8,128)S(1)}, f32[128,1024]{1,0:T(8,128)S(1)}, u32[]{:S(2)}, u32[]{:S(2)}) %collective-permute-start.6) | collective-permute-done | bytes 524320 | tf_op jit(solution)/shard_map/ppermute | solution.py:222
  35.0 1.7 %ranks.1 = (bf16[256,1024]{1,0:T(8,128)(2,1)S(1)}, bf16[256,1024]{1,0:T(8,128)(2,1)S(1)}, f32[256,256]{1,0:T(8,128)S(1)}, f32[8,256]{1,0:T(8,128)S(1)}) custom-call(f32[8,256,1024]{2,1,0:T(8,128)S(1)} %get-tuple-element.32.slab_ref, f32[8,256]{1,0:T(8,128)S(1)} %get-tuple-element.33.c_ref, f32[256,256]{1,0:T(8,128)S(1)} %get-tuple-element.34.gram_ref, ...), custom_call_target="tpu_custom_call" | custom-call | flops 134217728 | tf_op jit(solution)/shard_map/ranks/pallas_call | solution.py:315
  36.7 1.5 %collective-permute-start.7 = (f32[8,256]{1,0:T(8,128)S(1)}, f32[8,256]{1,0:T(8,128)S(1)}, u32[]{:S(2)}, u32[]{:S(2)}) collective-permute-start(f32[8,256]{1,0:T(8,128)S(1)} %get-tuple-element.43), channel_id=1, source_target_pairs={{0,4},{1,3},{2,6},{3,1},{4,0},{5,7},{6,2},{7,5},{8,12},{9,11},{10,... | collective-permute-start | bytes 24584 | tf_op jit(solution)/shard_map/ppermute | solution.py:222
  38.2 0.0 collective-permute-done.14
  38.2 0.0 collective-permute-done.16
  38.2 0.0 collective-permute-done.15
  38.3 0.1 collective-permute-start.17
  38.3 2.0 %collective-permute-done.7 = f32[8,256]{1,0:T(8,128)S(1)} collective-permute-done((f32[8,256]{1,0:T(8,128)S(1)}, f32[8,256]{1,0:T(8,128)S(1)}, u32[]{:S(2)}, u32[]{:S(2)}) %collective-permute-start.7) | collective-permute-done | bytes 8224 | tf_op jit(solution)/shard_map/ppermute | solution.py:222
  40.4 1.2 %collective-permute-start.8 = (f32[8,256]{1,0:T(8,128)S(1)}, f32[8,256]{1,0:T(8,128)S(1)}, u32[]{:S(2)}, u32[]{:S(2)}) collective-permute-start(f32[8,256]{1,0:T(8,128)S(1)} %add.39), channel_id=1, source_target_pairs={{0,2},{1,5},{2,0},{3,7},{4,6},{5,1},{6,4},{7,3},{8,10},{9,13},{10,... | collective-permute-start | bytes 24584 | tf_op jit(solution)/shard_map/ppermute | solution.py:222
  41.6 2.2 %rows.1 = (f32[64,256]{1,0:T(8,128)S(1)}, f32[64,256]{1,0:T(8,128)S(1)}) custom-call(bf16[1024,1024]{1,0:T(8,128)(2,1)S(1)} %get-tuple-element.44.high_ref, bf16[1024,1024]{1,0:T(8,128)(2,1)S(1)} %get-tuple-element.45.low_ref, bf16[256,1024]{1,0:T(8,128)(2,1)S(1)} %get-tuple-element.46.bt_high.high_ref, ...), custom_call_target="tpu_custom_call" | custom-call | flops 536870912 | tf_op jit(solution)/shard_map/rows/pallas_call | solution.py:330
  43.8 0.2 collective-permute-done.8
  44.0 1.8 %collective-permute-start.12 = (f32[8,256]{1,0:T(8,128)S(1)}, f32[8,256]{1,0:T(8,128)S(1)}, u32[]{:S(2)}, u32[]{:S(2)}) collective-permute-start(f32[8,256]{1,0:T(8,128)S(1)} %add.40), channel_id=1, source_target_pairs={{0,8},{1,9},{2,10},{3,11},{4,12},{5,13},{6,14},{7,15},{8,0},{9,1},... | collective-permute-start | bytes 24584 | tf_op jit(solution)/shard_map/ppermute | solution.py:222
  45.8 0.9 %collective-permute-start.11 = (f32[8,256]{1,0:T(8,128)S(1)}, f32[8,256]{1,0:T(8,128)S(1)}, u32[]{:S(2)}, u32[]{:S(2)}) collective-permute-start(f32[8,256]{1,0:T(8,128)S(1)} %add.40), channel_id=1, source_target_pairs={{0,24},{1,25},{2,26},{3,27},{4,28},{5,29},{6,30},{7,31},{8,16},{9,... | collective-permute-start | bytes 24584 | tf_op jit(solution)/shard_map/ppermute | solution.py:222
  46.7 0.8 %collective-permute-start.10 = (f32[8,256]{1,0:T(8,128)S(1)}, f32[8,256]{1,0:T(8,128)S(1)}, u32[]{:S(2)}, u32[]{:S(2)}) collective-permute-start(f32[8,256]{1,0:T(8,128)S(1)} %add.40), channel_id=1, source_target_pairs={{0,16},{1,17},{2,18},{3,19},{4,20},{5,21},{6,22},{7,23},{8,24},{9,... | collective-permute-start | bytes 24584 | tf_op jit(solution)/shard_map/ppermute | solution.py:222
  47.5 0.0 collective-permute-done.17.other_ref
  47.5 1.3 %last.1 = f32[16,1024]{1,0:T(8,128)} custom-call(f32[16,128]{1,0:T(8,128)S(1)} %slice.8.mine_ref, f32[16,128]{1,0:T(8,128)S(1)} %collective-permute-done.17.other_ref, f32[8,256]{1,0:T(8,128)S(1)} %get-tuple-element.33.c_ref, f32[16,1024]{1,0:T(8,128)S(1)} %slice.9.m_ref, bf16[256,1024]{1,0:T(8,128)(2,1)S(1)} %get-tuple-element.46.bt_high.high_ref, ...), custom_call_target="tpu_custom_call" | custom-call | flops 8388608 | tf_op jit(solution)/shard_map/last/pallas_call | solution.py:344
  48.8 0.0 collective-permute-start.9
  48.8 0.0 collective-permute-done.12
  48.8 2.5 %collective-permute-done.11 = f32[8,256]{1,0:T(8,128)S(1)} collective-permute-done((f32[8,256]{1,0:T(8,128)S(1)}, f32[8,256]{1,0:T(8,128)S(1)}, u32[]{:S(2)}, u32[]{:S(2)}) %collective-permute-start.11) | collective-permute-done | bytes 8224 | tf_op jit(solution)/shard_map/ppermute | solution.py:222
  51.2 0.1 collective-permute-done.10
  51.3 0.0 collective-permute-start.18
  51.3 1.2 %collective-permute-done.18 = f32[8,256]{1,0:T(8,128)S(1)} collective-permute-done((f32[8,256]{1,0:T(8,128)S(1)}, f32[8,256]{1,0:T(8,128)S(1)}, u32[]{:S(2)}, u32[]{:S(2)}) %collective-permute-start.18) | collective-permute-done | bytes 8224 | tf_op jit(solution)/shard_map/ppermute | solution.py:229
  52.5 0.6 %add.51 = f32[8,256]{1,0:T(8,128)} add(f32[8,256]{1,0:T(8,128)S(1)} %add_add_fusion.1, f32[8,256]{1,0:T(8,128)S(1)} %collective-permute-done.18) | non-fusion elementwise | flops 2048 | bytes 24576 | tf_op jit(solution)/shard_map/add | solution.py:354
  53.1 0.0 collective-permute-done.9
  53.1 0.6 %add.41 = f32[64,256]{1,0:T(8,128)} add(f32[64,256]{1,0:T(8,128)S(1)} %get-tuple-element.52, f32[64,256]{1,0:T(8,128)S(1)} %collective-permute-done.9) | non-fusion elementwise | flops 16384 | bytes 196608 | tf_op jit(solution)/shard_map/add | solution.py:353
  (11 shorter events, 0.2 us)
Async XLA Ops:
  0.6 4.2 %collective-permute-start = (f32[64,256]{1,0:T(8,128)}, f32[64,256]{1,0:T(8,128)S(1)}, u32[]{:S(2)}, u32[]{:S(2)}) collective-permute-start(f32[64,256]{1,0:T(8,128)} %a_hbm.1), channel_id=1, source_target_pairs={{0,1},{1,0},{2,3},{3,2},{4,5},{5,4},{6,7},{7,6},{8,9},{9,8},{10,11... | collective-permute-start | bytes 196616 | tf_op jit(solution)/shard_map/ppermute | solution.py:229
  1.1 8.2 %collective-permute-start.1 = (f32[16,1024]{1,0:T(8,128)}, f32[16,1024]{1,0:T(8,128)S(1)}, u32[]{:S(2)}, u32[]{:S(2)}) collective-permute-start(f32[16,1024]{1,0:T(8,128)} %own_hbm.1), channel_id=1, source_target_pairs={{0,16},{1,9},{2,18},{3,11},{4,20},{5,13},{6,22},{7,15},{8,24},{9,1... | collective-permute-start | bytes 196616 | tf_op jit(solution)/shard_map/ppermute | solution.py:222
  9.3 7.1 %collective-permute-start.3 = (f32[64,1152]{1,0:T(8,128)S(1)}, f32[64,1152]{1,0:T(8,128)S(1)}, u32[]{:S(2)}, u32[]{:S(2)}) collective-permute-start(f32[64,1152]{1,0:T(8,128)S(1)} %get-tuple-element.39), channel_id=1, source_target_pairs={{0,2},{1,5},{2,0},{3,7},{4,6},{5,1},{6,4},{7,3},{8,10},{9,13},{10,... | collective-permute-start | bytes 884744 | tf_op jit(solution)/shard_map/ppermute | solution.py:222
  10.9 5.5 %collective-permute-start.2 = (f32[32,1024]{1,0:T(8,128)S(1)}, f32[32,1024]{1,0:T(8,128)S(1)}, u32[]{:S(2)}, u32[]{:S(2)}) collective-permute-start(f32[32,1024]{1,0:T(8,128)S(1)} %pad_maximum_fusion.2), channel_id=1, source_target_pairs={{0,8},{1,17},{2,10},{3,19},{4,12},{5,21},{6,14},{7,23},{8,0},{9,25... | collective-permute-start | bytes 393224 | tf_op jit(solution)/shard_map/ppermute | solution.py:222
  12.5 6.8 %collective-permute-start.5 = (f32[64,1152]{1,0:T(8,128)S(1)}, f32[64,1152]{1,0:T(8,128)S(1)}, u32[]{:S(2)}, u32[]{:S(2)}) collective-permute-start(f32[64,1152]{1,0:T(8,128)S(1)} %get-tuple-element.41), channel_id=1, source_target_pairs={{0,2},{1,5},{2,0},{3,7},{4,6},{5,1},{6,4},{7,3},{8,10},{9,13},{10,... | collective-permute-start | bytes 884744 | tf_op jit(solution)/shard_map/ppermute | solution.py:222
  16.4 9.2 %collective-permute-start.4 = (f32[64,1024]{1,0:T(8,128)S(1)}, f32[64,1024]{1,0:T(8,128)S(1)}, u32[]{:S(2)}, u32[]{:S(2)}) collective-permute-start(f32[64,1024]{1,0:T(8,128)S(1)} %pad_maximum_fusion.1.refs_0_), channel_id=1, source_target_pairs={{0,2},{1,5},{2,0},{3,7},{4,6},{5,1},{6,4},{7,3},{8,10},{9,13},{10,... | collective-permute-start | bytes 786440 | tf_op jit(solution)/shard_map/ppermute | solution.py:222
  17.8 9.5 %collective-permute-start.13 = (f32[64,1152]{1,0:T(8,128)S(1)}, f32[64,1152]{1,0:T(8,128)S(1)}, u32[]{:S(2)}, u32[]{:S(2)}) collective-permute-start(f32[64,1152]{1,0:T(8,128)S(1)} %add.46), channel_id=1, source_target_pairs={{0,4},{1,3},{2,6},{3,1},{4,0},{5,7},{6,2},{7,5},{8,12},{9,11},{10,... | collective-permute-start | bytes 884744 | tf_op jit(solution)/shard_map/ppermute | solution.py:222
  25.7 9.2 %collective-permute-start.6 = (f32[128,1024]{1,0:T(8,128)S(1)}, f32[128,1024]{1,0:T(8,128)S(1)}, u32[]{:S(2)}, u32[]{:S(2)}) collective-permute-start(f32[128,1024]{1,0:T(8,128)S(1)} %pad_maximum_fusion), channel_id=1, source_target_pairs={{0,4},{1,3},{2,6},{3,1},{4,0},{5,7},{6,2},{7,5},{8,12},{9,11},{10,... | collective-permute-start | bytes 1572872 | tf_op jit(solution)/shard_map/ppermute | solution.py:222
  27.4 10.8 %collective-permute-start.14 = (f32[16,1152]{1,0:T(8,128)S(1)}, f32[16,1152]{1,0:T(8,128)S(1)}, u32[]{:S(2)}, u32[]{:S(2)}) collective-permute-start(f32[16,1152]{1,0:T(8,128)S(1)} %get-tuple-element.61), channel_id=1, source_target_pairs={{0,16},{1,9},{2,18},{3,11},{4,20},{5,13},{6,22},{7,15},{8,24},{9,1... | collective-permute-start | bytes 221192 | tf_op jit(solution)/shard_map/ppermute | solution.py:222
  28.7 9.5 %collective-permute-start.16 = (f32[16,1152]{1,0:T(8,128)S(1)}, f32[16,1152]{1,0:T(8,128)S(1)}, u32[]{:S(2)}, u32[]{:S(2)}) collective-permute-start(f32[16,1152]{1,0:T(8,128)S(1)} %get-tuple-element.62), channel_id=1, source_target_pairs={{0,24},{1,25},{2,26},{3,27},{4,28},{5,29},{6,30},{7,31},{8,16},{9,... | collective-permute-start | bytes 221192 | tf_op jit(solution)/shard_map/ppermute | solution.py:222
  31.5 6.7 %collective-permute-start.15 = (f32[16,1152]{1,0:T(8,128)S(1)}, f32[16,1152]{1,0:T(8,128)S(1)}, u32[]{:S(2)}, u32[]{:S(2)}) collective-permute-start(f32[16,1152]{1,0:T(8,128)S(1)} %get-tuple-element.63), channel_id=1, source_target_pairs={{0,8},{1,17},{2,10},{3,19},{4,12},{5,21},{6,14},{7,23},{8,0},{9,25... | collective-permute-start | bytes 221192 | tf_op jit(solution)/shard_map/ppermute | solution.py:222
  36.7 3.7 %collective-permute-start.7 = (f32[8,256]{1,0:T(8,128)S(1)}, f32[8,256]{1,0:T(8,128)S(1)}, u32[]{:S(2)}, u32[]{:S(2)}) collective-permute-start(f32[8,256]{1,0:T(8,128)S(1)} %get-tuple-element.43), channel_id=1, source_target_pairs={{0,4},{1,3},{2,6},{3,1},{4,0},{5,7},{6,2},{7,5},{8,12},{9,11},{10,... | collective-permute-start | bytes 24584 | tf_op jit(solution)/shard_map/ppermute | solution.py:222
  38.3 9.2 %collective-permute-start.17 = (f32[16,128]{1,0:T(8,128)S(1)}, f32[16,128]{1,0:T(8,128)S(1)}, u32[]{:S(2)}, u32[]{:S(2)}) collective-permute-start(f32[16,128]{1,0:T(8,128)S(1)} %slice.8.mine_ref), channel_id=1, source_target_pairs={{0,1},{1,0},{2,3},{3,2},{4,5},{5,4},{6,7},{7,6},{8,9},{9,8},{10,11... | collective-permute-start | bytes 24584 | tf_op jit(solution)/shard_map/ppermute | solution.py:229
  40.4 3.7 %collective-permute-start.8 = (f32[8,256]{1,0:T(8,128)S(1)}, f32[8,256]{1,0:T(8,128)S(1)}, u32[]{:S(2)}, u32[]{:S(2)}) collective-permute-start(f32[8,256]{1,0:T(8,128)S(1)} %add.39), channel_id=1, source_target_pairs={{0,2},{1,5},{2,0},{3,7},{4,6},{5,1},{6,4},{7,3},{8,10},{9,13},{10,... | collective-permute-start | bytes 24584 | tf_op jit(solution)/shard_map/ppermute | solution.py:222
  44.0 4.8 %collective-permute-start.12 = (f32[8,256]{1,0:T(8,128)S(1)}, f32[8,256]{1,0:T(8,128)S(1)}, u32[]{:S(2)}, u32[]{:S(2)}) collective-permute-start(f32[8,256]{1,0:T(8,128)S(1)} %add.40), channel_id=1, source_target_pairs={{0,8},{1,9},{2,10},{3,11},{4,12},{5,13},{6,14},{7,15},{8,0},{9,1},... | collective-permute-start | bytes 24584 | tf_op jit(solution)/shard_map/ppermute | solution.py:222
  45.8 5.5 %collective-permute-start.11 = (f32[8,256]{1,0:T(8,128)S(1)}, f32[8,256]{1,0:T(8,128)S(1)}, u32[]{:S(2)}, u32[]{:S(2)}) collective-permute-start(f32[8,256]{1,0:T(8,128)S(1)} %add.40), channel_id=1, source_target_pairs={{0,24},{1,25},{2,26},{3,27},{4,28},{5,29},{6,30},{7,31},{8,16},{9,... | collective-permute-start | bytes 24584 | tf_op jit(solution)/shard_map/ppermute | solution.py:222
  46.7 4.6 %collective-permute-start.10 = (f32[8,256]{1,0:T(8,128)S(1)}, f32[8,256]{1,0:T(8,128)S(1)}, u32[]{:S(2)}, u32[]{:S(2)}) collective-permute-start(f32[8,256]{1,0:T(8,128)S(1)} %add.40), channel_id=1, source_target_pairs={{0,16},{1,17},{2,18},{3,19},{4,20},{5,21},{6,22},{7,23},{8,24},{9,... | collective-permute-start | bytes 24584 | tf_op jit(solution)/shard_map/ppermute | solution.py:222
  48.8 4.3 %collective-permute-start.9 = (f32[64,256]{1,0:T(8,128)S(1)}, f32[64,256]{1,0:T(8,128)S(1)}, u32[]{:S(2)}, u32[]{:S(2)}) collective-permute-start(f32[64,256]{1,0:T(8,128)S(1)} %get-tuple-element.53), channel_id=1, source_target_pairs={{0,1},{1,0},{2,3},{3,2},{4,5},{5,4},{6,7},{7,6},{8,9},{9,8},{10,11... | collective-permute-start | bytes 196616 | tf_op jit(solution)/shard_map/ppermute | solution.py:229
  51.3 1.2 %collective-permute-start.18 = (f32[8,256]{1,0:T(8,128)S(1)}, f32[8,256]{1,0:T(8,128)S(1)}, u32[]{:S(2)}, u32[]{:S(2)}) collective-permute-start(f32[8,256]{1,0:T(8,128)S(1)} %add_add_fusion.1), channel_id=1, source_target_pairs={{0,1},{1,0},{2,3},{3,2},{4,5},{5,4},{6,7},{7,6},{8,9},{9,8},{10,11... | collective-permute-start | bytes 24584 | tf_op jit(solution)/shard_map/ppermute | solution.py:229

commit v2 on v1

--- a/solution.py
+++ b/solution.py
@@ -14,6 +14,7 @@
 VMEM = 24 * 1024 * 1024
 EARLY_VMEM = VMEM
 AHEAD = 4
+WEIGHT = 200
 
 
 def split(x):
@@ -133,27 +134,39 @@
                 ref[d * rank_rows : (d + 1) * rank_rows, :] = total[pl.ds(start, rank_rows), :]
 
 
-def ranks_kernel(n_line, rank_rows, slab_ref, c_ref, gram_ref, *refs):
-    *bufs, high_ref, low_ref, cross_ref, out_ref, bt_ref = refs
-    if len(bufs) == 1:
-        bt_ref[...] = bufs[0][...]
-    else:
-        own, near, far = bufs
-        line_rows = n_line * rank_rows
-        at = [(own, 0), (near, 0), (far, 0), (far, line_rows)]
-        for (ref, base), starts in zip(at, block_rows(n_line, rank_rows)):
-            for d, start in enumerate(starts):
-                bt_ref[pl.ds(start, rank_rows), :] = ref[base + d * rank_rows : base + (d + 1) * rank_rows, :]
-    bt = split(bt_ref[...])
-    high_ref[...], low_ref[...] = bt
+def put_ranks(slab_ref, ref, starts, count, high_ref, low_ref, sums_ref):
+    for d, start in enumerate(starts):
+        block = ref[d * count : (d + 1) * count, :]
+        here = pl.ds(start, count)
+        high_ref[here, :], low_ref[here, :] = split(block)
+        sums_ref[here, :] = jnp.concatenate(
+            [
+                jnp.sum(slab_ref[k, here, :] * block, axis=1, keepdims=True)
+                for k in range(slab_ref.shape[0])
+            ],
+            axis=1,
+        )
+
+
+def near_kernel(n_line, rank_rows, slab_ref, *refs):
+    *bufs, high_ref, low_ref, sums_ref = refs
+    for ref, starts in zip(bufs, block_rows(n_line, rank_rows)):
+        put_ranks(slab_ref, ref, starts, rank_rows, high_ref, low_ref, sums_ref)
+
+
+def ranks_kernel(n_line, rank_rows, slab_ref, c_ref, gram_ref, buf_ref, *refs):
+    *sofar, high_ref, low_ref, cross_ref, out_ref, sums_ref = refs
+    if sofar:
+        for ref, out in zip(sofar, (high_ref, low_ref, sums_ref)):
+            out[...] = ref[...]
+        starts, count = block_rows(n_line, rank_rows)[3], rank_rows
+    else:
+        starts, count = [0], buf_ref.shape[0]
+    put_ranks(slab_ref, buf_ref, starts, count, high_ref, low_ref, sums_ref)
+    bt = (high_ref[...], low_ref[...])
     cross = dot3(bt, bt, NT)
     cross_ref[...] = cross
-    slices, rank = c_ref.shape
-    sums = [
-        jnp.sum(slab_ref[k] * bt_ref[...], axis=1, keepdims=True) for k in range(slices)
-    ]
-    sums = jnp.concatenate(sums, axis=1)
-    out_ref[...] = dot3(split(c_ref[...]), split(gram_ref[...] * cross)) - sums.T
+    out_ref[...] = dot3(split(c_ref[...]), split(gram_ref[...] * cross)) - sums_ref[...].T
 
 
 def rows_kernel(halves, high_ref, low_ref, bt_high, bt_low, a_ref, c_ref, cross_ref, keep_ref, send_ref=None):
@@ -185,15 +198,24 @@
         send_ref[...] = grad[:half]
 
 
-def last_kernel(mine_ref, other_ref, c_ref, m_ref, high_ref, low_ref, out_ref):
+def sum_kernel(a_ref, b_ref, out_ref):
+    out_ref[...] = a_ref[...] + b_ref[...]
+
+
+def last_kernel(pair, halves, *refs):
+    gram_refs, refs = refs[: 1 + halves], refs[1 + halves :]
+    c_ref, m_ref, high_ref, low_ref, *refs = refs
+    if pair:
+        keep_ref, back_ref, *parts, out_ref, a_out, c_out = refs
+        a_out[...] = keep_ref[...] + back_ref[...]
+        c_out[...] = sum(ref[...] for ref in parts[1:]) + parts[0][...]
+    else:
+        (out_ref,) = refs
     rank_rows = m_ref.shape[0]
-    pieces = [mine_ref[...]]
-    if other_ref is not None:
+    pieces = [ref[...] for ref in gram_refs]
+    if halves:
         here = lax.axis_index("col") == 0
-        pieces = [
-            jnp.where(here, mine_ref[...], other_ref[...]),
-            jnp.where(here, other_ref[...], mine_ref[...]),
-        ]
+        pieces = [jnp.where(here, *pieces), jnp.where(here, *pieces[::-1])]
     gram_rows = jnp.concatenate(pieces, axis=1)
     c = c_ref[...]
     chosen = lax.axis_index("row") * rank_rows
@@ -252,7 +274,8 @@
         a_parts = [factor_a, swap(factor_a)]
     else:
         a_parts = [lax.all_gather(factor_a, "col", axis=0, tiled=True)]
-    got = move(factor_bt, along(0))
+    apart = [lambda r, c, d=d: r ^ (4 * distance(d, n_line, c % 2)) for d in range(n_line)]
+    got = [move(factor_bt, apart[d]) for d in range(1, n_line)]
 
     work = 2 * slices * rows * cols * rank
     pay_rows = [line_rows] * 4 if inside else [rank]
@@ -293,38 +316,49 @@
             for place in places
         ]
     pay_own, pay_f, pay_s, pay_fs = pay
-    pay_fs, pay_f, got = tie((pay_fs, pay_f, got))
+    got_f = move(pay_f, first)
     got_fs = move(pay_fs, first)
-    got_f = move(pay_f, first)
-
-    own4 = jnp.concatenate([own, got], axis=0)
-    for t in range(1, stages):
-        own4 = jnp.concatenate([own4, move(own4, along(t))], axis=0)
-    own4, got_fs = tie((own4, got_fs))
+
+    own4 = jnp.concatenate([own, *got], axis=0)
     f4 = move(own4, first)
-    f4, got_f = tie((f4, got_f))
-    far4 = move(jnp.concatenate([own4, f4], axis=0), second)
-
-    got_s = move(pay_s + got_fs, second)
-    total = pay_own + got_f + got_s
-    bufs = [own4, f4, far4]
-    if not inside:
-        table = jnp.concatenate(bufs, axis=0).reshape(n_row, rank_rows, cols)
+    s4 = move(own4, second)
+    f4, s4 = tie((f4, s4))
+    fs4 = move(f4, second)
+    if inside:
+        sofar = call(
+            functools.partial(near_kernel, n_line, rank_rows),
+            "near",
+            WEIGHT * cols * rank * rank,
+            [((rank, cols), BF16)] * 2 + [((rank, slices), F32)],
+        )(slabs, own4, f4, s4)
+        got_fs, _ = tie((got_fs, sofar[2]))
+        last_ranks = fs4
+    else:
+        sofar = []
+        table = jnp.concatenate([own4, f4, s4, fs4], axis=0).reshape(n_row, rank_rows, cols)
         index = jnp.argsort(jnp.concatenate([4 * lines + place for place in places]))
-        bufs = [jnp.take(table, index, axis=0).reshape(rank, cols)]
+        last_ranks = jnp.take(table, index, axis=0).reshape(rank, cols)
     bt_high, bt_low, cross, part_c = call(
         functools.partial(ranks_kernel, n_line, rank_rows),
         "ranks",
-        2 * cols * rank * rank,
+        WEIGHT * cols * rank * rank,
         [((rank, cols), BF16)] * 2 + [((rank, rank), F32), ((slices, rank), F32)],
-        [(rank, cols)],
-    )(slabs, c_near, gram, *bufs)
-
-    part_c = part_c + move(part_c, second)
+        [(rank, slices)],
+    )(slabs, c_near, gram, last_ranks, *sofar)
+
+    got_s = move(pay_s + got_fs, second)
+
+    (mark,) = call(sum_kernel, "mark", WEIGHT * work, [(part_c.shape, F32)])(part_c, part_c)
+    part_c = part_c + swap(part_c) if pair else lax.psum(part_c, "col")
+    (part_c,) = call(sum_kernel, "sum", WEIGHT * work, [(part_c.shape, F32)])(part_c, move(part_c, second))
+    pay_own, _ = tie((pay_own, mark))
+    total = pay_own + got_f + got_s
     slots = jnp.split(total, n_line, axis=0)
     total = slots[0]
     for d in range(1, n_line):
-        total = total + move(slots[d], lambda r, c, d=d: r ^ (4 * distance(d, n_line, c % 2)))
+        total = total + move(slots[d], apart[d])
+    cross, _ = tie((cross, part_c))
+    part_c = part_c + move(part_c, first)
 
     half = rows // 2 if pair else rows
     keep, *send = call(
@@ -334,28 +368,21 @@
         [((half, rank), F32)] * (2 if pair else 1),
     )(high, low, bt_high, bt_low, block_a, c_near, cross)
 
+    part_c = [part_c] + [move(part_c, lambda r, c, d=d: r ^ (4 * d)) for d in reversed(range(1, n_line))]
     gram_rows = total[:, cols:]
-    kernel = last_kernel
-    operands = [gram_rows, c_near, total[:, :cols], bt_high, bt_low]
-    if width < rank:
-        operands.insert(1, swap(gram_rows))
-    else:
-        kernel = lambda first_ref, *refs: last_kernel(first_ref, None, *refs)
-    (grad_bt,) = call(kernel, "last", 2 * rank_rows * cols * rank, [((rank_rows, cols), F32)])(*operands)
-
-    part_c = part_c + move(part_c, first)
-    part_c, keep, send = tie((part_c, keep, send))
-    spread = [move(part_c, lambda r, c, d=d: r ^ (4 * d)) for d in [*range(2, n_line), 1]]
-    for x in spread:
-        part_c = part_c + x
-    part_c, grad_bt = tie((part_c, grad_bt))
-    if pair:
-        grad_a = keep + swap(send[0])
-        grad_c = part_c + swap(part_c)
-    else:
-        grad_a = lax.psum_scatter(keep, "col", scatter_dimension=0, tiled=True)
-        grad_c = lax.psum(part_c, "col")
-    return grad_a, grad_bt, grad_c
+    grams = [gram_rows, swap(gram_rows)] if width < rank else [gram_rows]
+    operands = [*grams, c_near, total[:, :cols], bt_high, bt_low]
+    shapes = [((rank_rows, cols), F32)]
+    if pair:
+        operands += [keep, swap(send[0]), *part_c]
+        shapes += [(keep.shape, F32), (factor_c.shape, F32)]
+    grad_bt, *rest = call(
+        functools.partial(last_kernel, pair, len(grams) - 1), "last", rank_rows * cols * rank, shapes
+    )(*operands)
+    if pair:
+        return rest[0], grad_bt, rest[1]
+    grad_a = lax.psum_scatter(keep, "col", scatter_dimension=0, tiled=True)
+    return grad_a, grad_bt, sum(part_c[1:], part_c[0])
 
 
 def solution(mesh):

time: 53.9 us -> 49.9 us (0.926)
  waiting for transfers between devices: 19.2 us -> 14.4 us
  starting transfers between devices: 22.6 us -> 24.8 us
  other arithmetic: 1.43 us -> 0.12 us
    ppermute x15 -> x17, waiting for transfers between devices: 18.1 us -> 13.2 us  [move(): lax.ppermute(x, ('row', 'col'), [(r * n_col + c, target(r, c) * n_col + c...]
    ppermute x15 -> x17, starting transfers between devices: 22 us -> 24.2 us  [move(): lax.ppermute(x, ('row', 'col'), [(r * n_col + c, target(r, c) * n_col + c...]
    add x5 -> x2, other arithmetic: 1.27 us -> 0.03 us  [the longest x1 0.02 us: local(): total = total + move(slots[d], apart[d])]
    pallas_call x2 -> x4, Pallas kernels: 2.98 us -> 2.88 us  [the longest x1 1.26 us: local(): call(functools.partial(last_kernel, pair, len(grams) - 1), 'last', rank_r...]
  transfers between devices with their start and end apart: 19 -> 21, of which waited for: 9 -> 8; matrix products, arithmetic and copies ran while one was open for 2% -> 0% of each run, Pallas kernels for 18% -> 17%
where the time goes in v2:
time: 49.9 us; the launch traced here: 49.7 us
  starting transfers between devices  24.8 us (50%)
  waiting for transfers between devices  14.4 us (29%)
  Pallas kernels  9.56 us (19%)
  between operations  0.76 us (2%)
    ppermute x17, starting transfers between devices, move(): lax.ppermute(x, ('row', 'col'), [(r * n_col + c, target(r, c) * n_col + c...  24.2 us
    ppermute x17, waiting for transfers between devices, move(): lax.ppermute(x, ('row', 'col'), [(r * n_col + c, target(r, c) * n_col + c...  13.2 us
    pallas_call x1, Pallas kernels, local(): pl.pallas_call(kernel, in_specs=[hbm] * 4 + [vmem] * (len(a_parts) - 1),...  4.48 us
    pallas_call x1, Pallas kernels, local(): call(functools.partial(rows_kernel, pair), 'rows', work, [((half, rank),...  2.2 us
    pallas_call x1, Pallas kernels, local(): call(functools.partial(last_kernel, pair, len(grams) - 1), 'last', rank_r...  1.26 us
    ppermute x4, waiting for transfers between devices, swap(): return lax.ppermute(x, 'col', [(0, 1), (1, 0)])  1.2 us
  transfers between devices with their start and end apart: 21, of which 8 were waited for; matrix products, arithmetic and copies ran while one was open for 0% of the time, Pallas kernels for 17%

profile of v2, /device:TPU:0, one launch (start us, length us, event | category | flops | bytes accessed | tf_op | source)
XLA Modules:
  0.0 49.7 jit_solution(11412167317992447965)
XLA Ops:
  0.6 0.5 %collective-permute-start = (f32[64,256]{1,0:T(8,128)}, f32[64,256]{1,0:T(8,128)S(1)}, u32[]{:S(2)}, u32[]{:S(2)}) collective-permute-start(f32[64,256]{1,0:T(8,128)} %a_hbm.1), channel_id=1, source_target_pairs={{0,1},{1,0},{2,3},{3,2},{4,5},{5,4},{6,7},{7,6},{8,9},{9,8},{10,11... | collective-permute-start | bytes 196616 | tf_op jit(solution)/shard_map/ppermute | solution.py:251
  1.1 3.7 %collective-permute-start.3 = (f32[16,1024]{1,0:T(8,128)}, f32[16,1024]{1,0:T(8,128)S(1)}, u32[]{:S(2)}, u32[]{:S(2)}) collective-permute-start(f32[16,1024]{1,0:T(8,128)} %own_hbm.1), channel_id=1, source_target_pairs={{0,16},{1,9},{2,18},{3,11},{4,20},{5,13},{6,22},{7,15},{8,24},{9,1... | collective-permute-start | bytes 196616 | tf_op jit(solution)/shard_map/ppermute | solution.py:244
  4.8 1.6 %collective-permute-start.4 = (f32[16,1024]{1,0:T(8,128)}, f32[16,1024]{1,0:T(8,128)S(1)}, u32[]{:S(2)}, u32[]{:S(2)}) collective-permute-start(f32[16,1024]{1,0:T(8,128)} %own_hbm.1), channel_id=1, source_target_pairs={{0,8},{1,17},{2,10},{3,19},{4,12},{5,21},{6,14},{7,23},{8,0},{9,25... | collective-permute-start | bytes 196616 | tf_op jit(solution)/shard_map/ppermute | solution.py:244
  6.4 0.0 collective-permute-start.5
  6.4 0.0 collective-permute-done.other_ref
  6.4 4.5 %early.1 = (f32[64,1152]{1,0:T(8,128)S(1)}, f32[64,1152]{1,0:T(8,128)S(1)}, f32[64,1152]{1,0:T(8,128)S(1)}, f32[64,1152]{1,0:T(8,128)S(1)}, f32[8,256,1024]{2,1,...) custom-call(f32[8,128,1024]{2,1,0:T(8,128)} %t_hbm.1, ...), custom_call_target="tpu_custom_call" | custom-call | flops 536870912 | tf_op jit(solution)/shard_map/early/pallas_call | solution.py:290
  10.9 0.0 collective-permute-done.3
  10.9 0.0 collective-permute-done.4
  10.9 1.7 %collective-permute-done.5 = f32[16,1024]{1,0:T(8,128)S(1)} collective-permute-done((f32[16,1024]{1,0:T(8,128)}, f32[16,1024]{1,0:T(8,128)S(1)}, u32[]{:S(2)}, u32[]{:S(2)}) %collective-permute-start.5) | collective-permute-done | bytes 65568 | tf_op jit(solution)/shard_map/ppermute | solution.py:244
  12.7 1.5 %collective-permute-start.6 = (f32[64,1024]{1,0:T(8,128)S(1)}, f32[64,1024]{1,0:T(8,128)S(1)}, u32[]{:S(2)}, u32[]{:S(2)}) collective-permute-start(f32[64,1024]{1,0:T(8,128)S(1)} %constant_dynamic-update-slice_fusion.refs_0_), channel_id=1, source_target_pairs={{0,2},{1,5},{2,0},{3,7},{4,6},{5,1},{6,4},{7,3},{8,10},{9,13},{10,... | collective-permute-start | bytes 786440 | tf_op jit(solution)/shard_map/ppermute | solution.py:244
  14.2 1.5 %collective-permute-start.7 = (f32[64,1024]{1,0:T(8,128)S(1)}, f32[64,1024]{1,0:T(8,128)S(1)}, u32[]{:S(2)}, u32[]{:S(2)}) collective-permute-start(f32[64,1024]{1,0:T(8,128)S(1)} %constant_dynamic-update-slice_fusion.refs_0_), channel_id=1, source_target_pairs={{0,4},{1,3},{2,6},{3,1},{4,0},{5,7},{6,2},{7,5},{8,12},{9,11},{10,... | collective-permute-start | bytes 786440 | tf_op jit(solution)/shard_map/ppermute | solution.py:244
  15.7 0.5 %collective-permute-start.2 = (f32[64,1152]{1,0:T(8,128)S(1)}, f32[64,1152]{1,0:T(8,128)S(1)}, u32[]{:S(2)}, u32[]{:S(2)}) collective-permute-start(f32[64,1152]{1,0:T(8,128)S(1)} %get-tuple-element.33), channel_id=1, source_target_pairs={{0,2},{1,5},{2,0},{3,7},{4,6},{5,1},{6,4},{7,3},{8,10},{9,13},{10,... | collective-permute-start | bytes 884744 | tf_op jit(solution)/shard_map/ppermute | solution.py:244
  16.2 1.5 %collective-permute-start.1 = (f32[64,1152]{1,0:T(8,128)S(1)}, f32[64,1152]{1,0:T(8,128)S(1)}, u32[]{:S(2)}, u32[]{:S(2)}) collective-permute-start(f32[64,1152]{1,0:T(8,128)S(1)} %get-tuple-element.31), channel_id=1, source_target_pairs={{0,2},{1,5},{2,0},{3,7},{4,6},{5,1},{6,4},{7,3},{8,10},{9,13},{10,... | collective-permute-start | bytes 884744 | tf_op jit(solution)/shard_map/ppermute | solution.py:244
  17.7 3.2 %collective-permute-done.6.refs_1_ = f32[64,1024]{1,0:T(8,128)S(1)} collective-permute-done((f32[64,1024]{1,0:T(8,128)S(1)}, f32[64,1024]{1,0:T(8,128)S(1)}, u32[]{:S(2)}, u32[]{:S(2)}) %collective-permute-start.6) | collective-permute-done | bytes 262176 | tf_op jit(solution)/shard_map/ppermute | solution.py:244
  20.9 2.5 %collective-permute-done.7.refs_2_ = f32[64,1024]{1,0:T(8,128)S(1)} collective-permute-done((f32[64,1024]{1,0:T(8,128)S(1)}, f32[64,1024]{1,0:T(8,128)S(1)}, u32[]{:S(2)}, u32[]{:S(2)}) %collective-permute-start.7) | collective-permute-done | bytes 262176 | tf_op jit(solution)/shard_map/ppermute | solution.py:244
  23.4 1.5 %collective-permute-start.13 = (f32[64,1024]{1,0:T(8,128)S(1)}, f32[64,1024]{1,0:T(8,128)S(1)}, u32[]{:S(2)}, u32[]{:S(2)}) collective-permute-start(f32[64,1024]{1,0:T(8,128)S(1)} %collective-permute-done.6.refs_1_), channel_id=1, source_target_pairs={{0,4},{1,3},{2,6},{3,1},{4,0},{5,7},{6,2},{7,5},{8,12},{9,11},{10,... | collective-permute-start | bytes 786440 | tf_op jit(solution)/shard_map/ppermute | solution.py:244
  24.9 0.6 %near.1 = (bf16[256,1024]{1,0:T(8,128)(2,1)S(1)}, bf16[256,1024]{1,0:T(8,128)(2,1)S(1)}, f32[256,8]{1,0:T(8,128)S(1)}) custom-call(f32[8,256,1024]{2,1,0:T(8,128)S(1)} %get-tuple-element.34.slab_ref, f32[64,1024]{1,0:T(8,128)S(1)} %constant_dynamic-update-slice_fusion.refs_0_, f32[64,1024]{1,0:T(8,128)S(1)} %collective-permute-done.6.refs_1_, ...), custom_call_target="tpu_custom_call" | custom-call | flops 13421772800 | tf_op jit(solution)/shard_map/near/pallas_call | solution.py:328
  25.6 0.0 collective-permute-done.2
  25.6 1.5 %collective-permute-start.8 = (f32[64,1152]{1,0:T(8,128)S(1)}, f32[64,1152]{1,0:T(8,128)S(1)}, u32[]{:S(2)}, u32[]{:S(2)}) collective-permute-start(f32[64,1152]{1,0:T(8,128)S(1)} %add.25), channel_id=1, source_target_pairs={{0,4},{1,3},{2,6},{3,1},{4,0},{5,7},{6,2},{7,5},{8,12},{9,11},{10,... | collective-permute-start | bytes 884744 | tf_op jit(solution)/shard_map/ppermute | solution.py:244
  27.1 2.7 %collective-permute-done.13.buf_ref = f32[64,1024]{1,0:T(8,128)S(1)} collective-permute-done((f32[64,1024]{1,0:T(8,128)S(1)}, f32[64,1024]{1,0:T(8,128)S(1)}, u32[]{:S(2)}, u32[]{:S(2)}) %collective-permute-start.13) | collective-permute-done | bytes 262176 | tf_op jit(solution)/shard_map/ppermute | solution.py:244
  29.8 1.0 %ranks.1 = (bf16[256,1024]{1,0:T(8,128)(2,1)S(1)}, bf16[256,1024]{1,0:T(8,128)(2,1)S(1)}, f32[256,256]{1,0:T(8,128)S(1)}, f32[8,256]{1,0:T(8,128)S(1)}) custom-call(f32[8,256,1024]{2,1,0:T(8,128)S(1)} %get-tuple-element.34.slab_ref, f32[8,256]{1,0:T(8,128)S(1)} %get-tuple-element.40.c_ref.refs_2_, f32[256,256]{1,0:T(8,128)S(1)} %get-tuple-element.41.gram_ref, ...), custom_call_target="tpu_custom_call" | custom-call | flops 13421772800 | tf_op jit(solution)/shard_map/ranks/pallas_call | solution.py:341
  30.8 0.0 collective-permute-start.14
  30.8 1.2 %collective-permute-done.14 = f32[8,256]{1,0:T(8,128)S(1)} collective-permute-done((f32[8,256]{1,0:T(8,128)S(1)}, f32[8,256]{1,0:T(8,128)S(1)}, u32[]{:S(2)}, u32[]{:S(2)}) %collective-permute-start.14) | collective-permute-done | bytes 8224 | tf_op jit(solution)/shard_map/ppermute | solution.py:251
  32.0 1.5 %collective-permute-start.15 = (f32[8,256]{1,0:T(8,128)S(1)}, f32[8,256]{1,0:T(8,128)S(1)}, u32[]{:S(2)}, u32[]{:S(2)}) collective-permute-start(f32[8,256]{1,0:T(8,128)S(1)} %add.30.a_ref), channel_id=1, source_target_pairs={{0,4},{1,3},{2,6},{3,1},{4,0},{5,7},{6,2},{7,5},{8,12},{9,11},{10,... | collective-permute-start | bytes 24584 | tf_op jit(solution)/shard_map/ppermute | solution.py:244
  33.5 0.0 collective-permute-done.1
  33.5 0.0 collective-permute-done.8
  33.5 0.1 add_add_fusion
  33.6 2.3 %collective-permute-start.11 = (f32[16,1152]{1,0:T(8,128)S(1)}, f32[16,1152]{1,0:T(8,128)S(1)}, u32[]{:S(2)}, u32[]{:S(2)}) collective-permute-start(f32[16,1152]{1,0:T(8,128)S(1)} %get-tuple-element.58), channel_id=1, source_target_pairs={{0,24},{1,25},{2,26},{3,27},{4,28},{5,29},{6,30},{7,31},{8,16},{9,... | collective-permute-start | bytes 221192 | tf_op jit(solution)/shard_map/ppermute | solution.py:244
  35.8 0.7 %collective-permute-start.10 = (f32[16,1152]{1,0:T(8,128)S(1)}, f32[16,1152]{1,0:T(8,128)S(1)}, u32[]{:S(2)}, u32[]{:S(2)}) collective-permute-start(f32[16,1152]{1,0:T(8,128)S(1)} %get-tuple-element.59), channel_id=1, source_target_pairs={{0,8},{1,17},{2,10},{3,19},{4,12},{5,21},{6,14},{7,23},{8,0},{9,25... | collective-permute-start | bytes 221192 | tf_op jit(solution)/shard_map/ppermute | solution.py:244
  36.5 1.5 %collective-permute-start.9 = (f32[16,1152]{1,0:T(8,128)S(1)}, f32[16,1152]{1,0:T(8,128)S(1)}, u32[]{:S(2)}, u32[]{:S(2)}) collective-permute-start(f32[16,1152]{1,0:T(8,128)S(1)} %get-tuple-element.57), channel_id=1, source_target_pairs={{0,16},{1,9},{2,18},{3,11},{4,20},{5,13},{6,22},{7,15},{8,24},{9,1... | collective-permute-start | bytes 221192 | tf_op jit(solution)/shard_map/ppermute | solution.py:244
  38.0 0.0 collective-permute-done.15.b_ref
  38.0 0.5 %collective-permute-start.17 = (f32[8,256]{1,0:T(8,128)S(1)}, f32[8,256]{1,0:T(8,128)S(1)}, u32[]{:S(2)}, u32[]{:S(2)}) collective-permute-start(f32[8,256]{1,0:T(8,128)S(1)} %sum.1), channel_id=1, source_target_pairs={{0,2},{1,5},{2,0},{3,7},{4,6},{5,1},{6,4},{7,3},{8,10},{9,13},{10,... | collective-permute-start | bytes 24584 | tf_op jit(solution)/shard_map/ppermute | solution.py:244
  38.6 2.2 %rows.1 = (f32[64,256]{1,0:T(8,128)S(1)}, f32[64,256]{1,0:T(8,128)S(1)}) custom-call(bf16[1024,1024]{1,0:T(8,128)(2,1)S(1)} %get-tuple-element.46.high_ref, bf16[1024,1024]{1,0:T(8,128)(2,1)S(1)} %get-tuple-element.47.low_ref, bf16[256,1024]{1,0:T(8,128)(2,1)S(1)} %get-tuple-element.44.bt_high.refs_4_, ...), custom_call_target="tpu_custom_call" | custom-call | flops 536870912 | tf_op jit(solution)/shard_map/rows/pallas_call | solution.py:364
  40.8 0.1 collective-permute-start.16
  40.9 0.8 %collective-permute-done.17 = f32[8,256]{1,0:T(8,128)S(1)} collective-permute-done((f32[8,256]{1,0:T(8,128)S(1)}, f32[8,256]{1,0:T(8,128)S(1)}, u32[]{:S(2)}, u32[]{:S(2)}) %collective-permute-start.17) | collective-permute-done | bytes 8224 | tf_op jit(solution)/shard_map/ppermute | solution.py:244
  41.7 2.2 %collective-permute-start.18 = (f32[8,256]{1,0:T(8,128)S(1)}, f32[8,256]{1,0:T(8,128)S(1)}, u32[]{:S(2)}, u32[]{:S(2)}) collective-permute-start(f32[8,256]{1,0:T(8,128)S(1)} %add.31.refs_8_), channel_id=1, source_target_pairs={{0,24},{1,25},{2,26},{3,27},{4,28},{5,29},{6,30},{7,31},{8,16},{9,... | collective-permute-start | bytes 24584 | tf_op jit(solution)/shard_map/ppermute | solution.py:244
  43.9 0.0 collective-permute-done.11
  43.9 0.0 collective-permute-start.19
  43.9 0.0 collective-permute-done.10
  43.9 2.1 %collective-permute-start.20 = (f32[8,256]{1,0:T(8,128)S(1)}, f32[8,256]{1,0:T(8,128)S(1)}, u32[]{:S(2)}, u32[]{:S(2)}) collective-permute-start(f32[8,256]{1,0:T(8,128)S(1)} %add.31.refs_8_), channel_id=1, source_target_pairs={{0,8},{1,9},{2,10},{3,11},{4,12},{5,13},{6,14},{7,15},{8,0},{9,1},... | collective-permute-start | bytes 24584 | tf_op jit(solution)/shard_map/ppermute | solution.py:244
  46.1 0.0 collective-permute-done.9
  46.1 0.1 collective-permute-start.12
  46.2 0.9 %collective-permute-done.18.refs_9_ = f32[8,256]{1,0:T(8,128)S(1)} collective-permute-done((f32[8,256]{1,0:T(8,128)S(1)}, f32[8,256]{1,0:T(8,128)S(1)}, u32[]{:S(2)}, u32[]{:S(2)}) %collective-permute-start.18) | collective-permute-done | bytes 8224 | tf_op jit(solution)/shard_map/ppermute | solution.py:244
  47.1 1.3 %collective-permute-done.19.refs_10_ = f32[8,256]{1,0:T(8,128)S(1)} collective-permute-done((f32[8,256]{1,0:T(8,128)S(1)}, f32[8,256]{1,0:T(8,128)S(1)}, u32[]{:S(2)}, u32[]{:S(2)}) %collective-permute-start.19) | collective-permute-done | bytes 8224 | tf_op jit(solution)/shard_map/ppermute | solution.py:244
  48.5 0.0 collective-permute-done.20.refs_11_
  48.5 0.0 collective-permute-done.16.refs_7_
  48.5 0.0 collective-permute-done.12.refs_1_
  48.5 1.3 %last.1 = (f32[16,1024]{1,0:T(8,128)}, f32[64,256]{1,0:T(8,128)}, f32[8,256]{1,0:T(8,128)}) custom-call(f32[16,128]{1,0:T(8,128)S(1)} %slice.8.refs_0_, f32[16,128]{1,0:T(8,128)S(1)} %collective-permute-done.12.refs_1_, f32[8,256]{1,0:T(8,128)S(1)} %get-tuple-element.40.c_ref.refs_2_, f32[16,1024]{1,0:T(8,128)S(1)} %slice.9.refs_3_, ...), custom_call_target="tpu_custom_call" | custom-call | flops 4194304 | tf_op jit(solution)/shard_map/last/pallas_call | solution.py:379
  (12 shorter events, 0.1 us)
Async XLA Ops:
  0.6 5.8 %collective-permute-start = (f32[64,256]{1,0:T(8,128)}, f32[64,256]{1,0:T(8,128)S(1)}, u32[]{:S(2)}, u32[]{:S(2)}) collective-permute-start(f32[64,256]{1,0:T(8,128)} %a_hbm.1), channel_id=1, source_target_pairs={{0,1},{1,0},{2,3},{3,2},{4,5},{5,4},{6,7},{7,6},{8,9},{9,8},{10,11... | collective-permute-start | bytes 196616 | tf_op jit(solution)/shard_map/ppermute | solution.py:251
  1.1 9.8 %collective-permute-start.3 = (f32[16,1024]{1,0:T(8,128)}, f32[16,1024]{1,0:T(8,128)S(1)}, u32[]{:S(2)}, u32[]{:S(2)}) collective-permute-start(f32[16,1024]{1,0:T(8,128)} %own_hbm.1), channel_id=1, source_target_pairs={{0,16},{1,9},{2,18},{3,11},{4,20},{5,13},{6,22},{7,15},{8,24},{9,1... | collective-permute-start | bytes 196616 | tf_op jit(solution)/shard_map/ppermute | solution.py:244
  4.8 6.1 %collective-permute-start.4 = (f32[16,1024]{1,0:T(8,128)}, f32[16,1024]{1,0:T(8,128)S(1)}, u32[]{:S(2)}, u32[]{:S(2)}) collective-permute-start(f32[16,1024]{1,0:T(8,128)} %own_hbm.1), channel_id=1, source_target_pairs={{0,8},{1,17},{2,10},{3,19},{4,12},{5,21},{6,14},{7,23},{8,0},{9,25... | collective-permute-start | bytes 196616 | tf_op jit(solution)/shard_map/ppermute | solution.py:244
  6.4 6.3 %collective-permute-start.5 = (f32[16,1024]{1,0:T(8,128)}, f32[16,1024]{1,0:T(8,128)S(1)}, u32[]{:S(2)}, u32[]{:S(2)}) collective-permute-start(f32[16,1024]{1,0:T(8,128)} %own_hbm.1), channel_id=1, source_target_pairs={{0,24},{1,25},{2,26},{3,27},{4,28},{5,29},{6,30},{7,31},{8,16},{9,... | collective-permute-start | bytes 196616 | tf_op jit(solution)/shard_map/ppermute | solution.py:244
  12.7 8.3 %collective-permute-start.6 = (f32[64,1024]{1,0:T(8,128)S(1)}, f32[64,1024]{1,0:T(8,128)S(1)}, u32[]{:S(2)}, u32[]{:S(2)}) collective-permute-start(f32[64,1024]{1,0:T(8,128)S(1)} %constant_dynamic-update-slice_fusion.refs_0_), channel_id=1, source_target_pairs={{0,2},{1,5},{2,0},{3,7},{4,6},{5,1},{6,4},{7,3},{8,10},{9,13},{10,... | collective-permute-start | bytes 786440 | tf_op jit(solution)/shard_map/ppermute | solution.py:244
  14.2 9.2 %collective-permute-start.7 = (f32[64,1024]{1,0:T(8,128)S(1)}, f32[64,1024]{1,0:T(8,128)S(1)}, u32[]{:S(2)}, u32[]{:S(2)}) collective-permute-start(f32[64,1024]{1,0:T(8,128)S(1)} %constant_dynamic-update-slice_fusion.refs_0_), channel_id=1, source_target_pairs={{0,4},{1,3},{2,6},{3,1},{4,0},{5,7},{6,2},{7,5},{8,12},{9,11},{10,... | collective-permute-start | bytes 786440 | tf_op jit(solution)/shard_map/ppermute | solution.py:244
  15.7 9.9 %collective-permute-start.2 = (f32[64,1152]{1,0:T(8,128)S(1)}, f32[64,1152]{1,0:T(8,128)S(1)}, u32[]{:S(2)}, u32[]{:S(2)}) collective-permute-start(f32[64,1152]{1,0:T(8,128)S(1)} %get-tuple-element.33), channel_id=1, source_target_pairs={{0,2},{1,5},{2,0},{3,7},{4,6},{5,1},{6,4},{7,3},{8,10},{9,13},{10,... | collective-permute-start | bytes 884744 | tf_op jit(solution)/shard_map/ppermute | solution.py:244
  16.2 17.3 %collective-permute-start.1 = (f32[64,1152]{1,0:T(8,128)S(1)}, f32[64,1152]{1,0:T(8,128)S(1)}, u32[]{:S(2)}, u32[]{:S(2)}) collective-permute-start(f32[64,1152]{1,0:T(8,128)S(1)} %get-tuple-element.31), channel_id=1, source_target_pairs={{0,2},{1,5},{2,0},{3,7},{4,6},{5,1},{6,4},{7,3},{8,10},{9,13},{10,... | collective-permute-start | bytes 884744 | tf_op jit(solution)/shard_map/ppermute | solution.py:244
  23.4 6.4 %collective-permute-start.13 = (f32[64,1024]{1,0:T(8,128)S(1)}, f32[64,1024]{1,0:T(8,128)S(1)}, u32[]{:S(2)}, u32[]{:S(2)}) collective-permute-start(f32[64,1024]{1,0:T(8,128)S(1)} %collective-permute-done.6.refs_1_), channel_id=1, source_target_pairs={{0,4},{1,3},{2,6},{3,1},{4,0},{5,7},{6,2},{7,5},{8,12},{9,11},{10,... | collective-permute-start | bytes 786440 | tf_op jit(solution)/shard_map/ppermute | solution.py:244
  25.6 7.9 %collective-permute-start.8 = (f32[64,1152]{1,0:T(8,128)S(1)}, f32[64,1152]{1,0:T(8,128)S(1)}, u32[]{:S(2)}, u32[]{:S(2)}) collective-permute-start(f32[64,1152]{1,0:T(8,128)S(1)} %add.25), channel_id=1, source_target_pairs={{0,4},{1,3},{2,6},{3,1},{4,0},{5,7},{6,2},{7,5},{8,12},{9,11},{10,... | collective-permute-start | bytes 884744 | tf_op jit(solution)/shard_map/ppermute | solution.py:244
  30.8 1.2 %collective-permute-start.14 = (f32[8,256]{1,0:T(8,128)S(1)}, f32[8,256]{1,0:T(8,128)S(1)}, u32[]{:S(2)}, u32[]{:S(2)}) collective-permute-start(f32[8,256]{1,0:T(8,128)S(1)} %get-tuple-element.50), channel_id=1, source_target_pairs={{0,1},{1,0},{2,3},{3,2},{4,5},{5,4},{6,7},{7,6},{8,9},{9,8},{10,11... | collective-permute-start | bytes 24584 | tf_op jit(solution)/shard_map/ppermute | solution.py:251
  32.0 6.1 %collective-permute-start.15 = (f32[8,256]{1,0:T(8,128)S(1)}, f32[8,256]{1,0:T(8,128)S(1)}, u32[]{:S(2)}, u32[]{:S(2)}) collective-permute-start(f32[8,256]{1,0:T(8,128)S(1)} %add.30.a_ref), channel_id=1, source_target_pairs={{0,4},{1,3},{2,6},{3,1},{4,0},{5,7},{6,2},{7,5},{8,12},{9,11},{10,... | collective-permute-start | bytes 24584 | tf_op jit(solution)/shard_map/ppermute | solution.py:244
  33.6 10.4 %collective-permute-start.11 = (f32[16,1152]{1,0:T(8,128)S(1)}, f32[16,1152]{1,0:T(8,128)S(1)}, u32[]{:S(2)}, u32[]{:S(2)}) collective-permute-start(f32[16,1152]{1,0:T(8,128)S(1)} %get-tuple-element.58), channel_id=1, source_target_pairs={{0,24},{1,25},{2,26},{3,27},{4,28},{5,29},{6,30},{7,31},{8,16},{9,... | collective-permute-start | bytes 221192 | tf_op jit(solution)/shard_map/ppermute | solution.py:244
  35.8 8.1 %collective-permute-start.10 = (f32[16,1152]{1,0:T(8,128)S(1)}, f32[16,1152]{1,0:T(8,128)S(1)}, u32[]{:S(2)}, u32[]{:S(2)}) collective-permute-start(f32[16,1152]{1,0:T(8,128)S(1)} %get-tuple-element.59), channel_id=1, source_target_pairs={{0,8},{1,17},{2,10},{3,19},{4,12},{5,21},{6,14},{7,23},{8,0},{9,25... | collective-permute-start | bytes 221192 | tf_op jit(solution)/shard_map/ppermute | solution.py:244
  36.5 9.6 %collective-permute-start.9 = (f32[16,1152]{1,0:T(8,128)S(1)}, f32[16,1152]{1,0:T(8,128)S(1)}, u32[]{:S(2)}, u32[]{:S(2)}) collective-permute-start(f32[16,1152]{1,0:T(8,128)S(1)} %get-tuple-element.57), channel_id=1, source_target_pairs={{0,16},{1,9},{2,18},{3,11},{4,20},{5,13},{6,22},{7,15},{8,24},{9,1... | collective-permute-start | bytes 221192 | tf_op jit(solution)/shard_map/ppermute | solution.py:244
  38.0 3.7 %collective-permute-start.17 = (f32[8,256]{1,0:T(8,128)S(1)}, f32[8,256]{1,0:T(8,128)S(1)}, u32[]{:S(2)}, u32[]{:S(2)}) collective-permute-start(f32[8,256]{1,0:T(8,128)S(1)} %sum.1), channel_id=1, source_target_pairs={{0,2},{1,5},{2,0},{3,7},{4,6},{5,1},{6,4},{7,3},{8,10},{9,13},{10,... | collective-permute-start | bytes 24584 | tf_op jit(solution)/shard_map/ppermute | solution.py:244
  40.8 7.7 %collective-permute-start.16 = (f32[64,256]{1,0:T(8,128)S(1)}, f32[64,256]{1,0:T(8,128)S(1)}, u32[]{:S(2)}, u32[]{:S(2)}) collective-permute-start(f32[64,256]{1,0:T(8,128)S(1)} %get-tuple-element.53), channel_id=1, source_target_pairs={{0,1},{1,0},{2,3},{3,2},{4,5},{5,4},{6,7},{7,6},{8,9},{9,8},{10,11... | collective-permute-start | bytes 196616 | tf_op jit(solution)/shard_map/ppermute | solution.py:251
  41.7 5.4 %collective-permute-start.18 = (f32[8,256]{1,0:T(8,128)S(1)}, f32[8,256]{1,0:T(8,128)S(1)}, u32[]{:S(2)}, u32[]{:S(2)}) collective-permute-start(f32[8,256]{1,0:T(8,128)S(1)} %add.31.refs_8_), channel_id=1, source_target_pairs={{0,24},{1,25},{2,26},{3,27},{4,28},{5,29},{6,30},{7,31},{8,16},{9,... | collective-permute-start | bytes 24584 | tf_op jit(solution)/shard_map/ppermute | solution.py:244
  43.9 4.6 %collective-permute-start.19 = (f32[8,256]{1,0:T(8,128)S(1)}, f32[8,256]{1,0:T(8,128)S(1)}, u32[]{:S(2)}, u32[]{:S(2)}) collective-permute-start(f32[8,256]{1,0:T(8,128)S(1)} %add.31.refs_8_), channel_id=1, source_target_pairs={{0,16},{1,17},{2,18},{3,19},{4,20},{5,21},{6,22},{7,23},{8,24},{9,... | collective-permute-start | bytes 24584 | tf_op jit(solution)/shard_map/ppermute | solution.py:244
  43.9 4.5 %collective-permute-start.20 = (f32[8,256]{1,0:T(8,128)S(1)}, f32[8,256]{1,0:T(8,128)S(1)}, u32[]{:S(2)}, u32[]{:S(2)}) collective-permute-start(f32[8,256]{1,0:T(8,128)S(1)} %add.31.refs_8_), channel_id=1, source_target_pairs={{0,8},{1,9},{2,10},{3,11},{4,12},{5,13},{6,14},{7,15},{8,0},{9,1},... | collective-permute-start | bytes 24584 | tf_op jit(solution)/shard_map/ppermute | solution.py:244
  46.1 2.4 %collective-permute-start.12 = (f32[16,128]{1,0:T(8,128)S(1)}, f32[16,128]{1,0:T(8,128)S(1)}, u32[]{:S(2)}, u32[]{:S(2)}) collective-permute-start(f32[16,128]{1,0:T(8,128)S(1)} %slice.8.refs_0_), channel_id=1, source_target_pairs={{0,1},{1,0},{2,3},{3,2},{4,5},{5,4},{6,7},{7,6},{8,9},{9,8},{10,11... | collective-permute-start | bytes 24584 | tf_op jit(solution)/shard_map/ppermute | solution.py:251

commit v3 on v2

--- a/solution.py
+++ b/solution.py
@@ -27,13 +27,10 @@
     return mul(a[0], b[0]) + (mul(a[0], b[1]) + mul(a[1], b[0]))
 
 
-def hop(stage, stages, parity):
-    return 1 << (stage + (1 - parity) * (stages - 1 - 2 * stage))
-
-
 def distance(slot, n_line, parity):
-    stages = n_line.bit_length() - 1
-    return sum(hop(t, stages, parity) for t in range(stages) if slot >> t & 1)
+    if slot in (0, n_line - 1):
+        return min(slot, 1)
+    return (slot + 1) ^ parity
 
 
 def block_rows(n_line, rank_rows):
@@ -252,11 +249,6 @@
 
     first = lambda r, c: r ^ (1 + c % 2)
     second = lambda r, c: r ^ (2 - c % 2)
-
-    stages = n_line.bit_length() - 1
-
-    def along(t):
-        return lambda r, c: r ^ (4 * hop(t, stages, c % 2))
 
     def call(kernel, name, cost, shapes, scratch=()):
         return pl.pallas_call(

time: 49.9 us -> 49.1 us (0.984)
  waiting for transfers between devices: 14.4 us -> 13.3 us
    ppermute x17, waiting for transfers between devices: 13.2 us -> 12.5 us  [move(): lax.ppermute(x, ('row', 'col'), [(r * n_col + c, target(r, c) * n_col + c...]
where the time goes in v3:
time: 49.1 us; the launch traced here: 48.9 us
  starting transfers between devices  25.1 us (51%)
  waiting for transfers between devices  13.3 us (27%)
  Pallas kernels  9.58 us (20%)
  between operations  0.75 us (2%)
    ppermute x17, starting transfers between devices, move(): lax.ppermute(x, ('row', 'col'), [(r * n_col + c, target(r, c) * n_col + c...  24 us
    ppermute x17, waiting for transfers between devices, move(): lax.ppermute(x, ('row', 'col'), [(r * n_col + c, target(r, c) * n_col + c...  12.5 us
    pallas_call x1, Pallas kernels, local(): pl.pallas_call(kernel, in_specs=[hbm] * 4 + [vmem] * (len(a_parts) - 1),...  4.48 us
    pallas_call x1, Pallas kernels, local(): call(functools.partial(rows_kernel, pair), 'rows', work, [((half, rank),...  2.21 us
    pallas_call x1, Pallas kernels, local(): call(functools.partial(last_kernel, pair, len(grams) - 1), 'last', rank_r...  1.26 us
    ppermute x4, starting transfers between devices, swap(): return lax.ppermute(x, 'col', [(0, 1), (1, 0)])  1.09 us
  transfers between devices with their start and end apart: 21, of which 8 were waited for; matrix products, arithmetic and copies ran while one was open for 0% of the time, Pallas kernels for 17%

profile of v3, /device:TPU:0, one launch (start us, length us, event | category | flops | bytes accessed | tf_op | source)
XLA Modules:
  0.0 48.9 jit_solution(11551304097435202664)
XLA Ops:
  0.6 0.5 %collective-permute-start = (f32[64,256]{1,0:T(8,128)}, f32[64,256]{1,0:T(8,128)S(1)}, u32[]{:S(2)}, u32[]{:S(2)}) collective-permute-start(f32[64,256]{1,0:T(8,128)} %a_hbm.1), channel_id=1, source_target_pairs={{0,1},{1,0},{2,3},{3,2},{4,5},{5,4},{6,7},{7,6},{8,9},{9,8},{10,11... | collective-permute-start | bytes 196616 | tf_op jit(solution)/shard_map/ppermute | solution.py:248
  1.1 3.7 %collective-permute-start.3 = (f32[16,1024]{1,0:T(8,128)}, f32[16,1024]{1,0:T(8,128)S(1)}, u32[]{:S(2)}, u32[]{:S(2)}) collective-permute-start(f32[16,1024]{1,0:T(8,128)} %own_hbm.1), channel_id=1, source_target_pairs={{0,16},{1,25},{2,18},{3,27},{4,20},{5,29},{6,22},{7,31},{8,24},{9,... | collective-permute-start | bytes 196616 | tf_op jit(solution)/shard_map/ppermute | solution.py:241
  4.8 1.3 %collective-permute-start.4 = (f32[16,1024]{1,0:T(8,128)}, f32[16,1024]{1,0:T(8,128)S(1)}, u32[]{:S(2)}, u32[]{:S(2)}) collective-permute-start(f32[16,1024]{1,0:T(8,128)} %own_hbm.1), channel_id=1, source_target_pairs={{0,24},{1,17},{2,26},{3,19},{4,28},{5,21},{6,30},{7,23},{8,16},{9,... | collective-permute-start | bytes 196616 | tf_op jit(solution)/shard_map/ppermute | solution.py:241
  6.2 0.2 collective-permute-start.5
  6.4 0.0 collective-permute-done.other_ref
  6.4 4.5 %early.1 = (f32[64,1152]{1,0:T(8,128)S(1)}, f32[64,1152]{1,0:T(8,128)S(1)}, f32[64,1152]{1,0:T(8,128)S(1)}, f32[64,1152]{1,0:T(8,128)S(1)}, f32[8,256,1024]{2,1,...) custom-call(f32[8,128,1024]{2,1,0:T(8,128)} %t_hbm.1, ...), custom_call_target="tpu_custom_call" | custom-call | flops 536870912 | tf_op jit(solution)/shard_map/early/pallas_call | solution.py:282
  10.9 0.0 collective-permute-done.3
  10.9 0.5 collective-permute-done.4
  11.4 0.7 %collective-permute-done.5 = f32[16,1024]{1,0:T(8,128)S(1)} collective-permute-done((f32[16,1024]{1,0:T(8,128)}, f32[16,1024]{1,0:T(8,128)S(1)}, u32[]{:S(2)}, u32[]{:S(2)}) %collective-permute-start.5) | collective-permute-done | bytes 65568 | tf_op jit(solution)/shard_map/ppermute | solution.py:241
  12.1 1.5 %collective-permute-start.6 = (f32[64,1024]{1,0:T(8,128)S(1)}, f32[64,1024]{1,0:T(8,128)S(1)}, u32[]{:S(2)}, u32[]{:S(2)}) collective-permute-start(f32[64,1024]{1,0:T(8,128)S(1)} %constant_dynamic-update-slice_fusion.refs_0_), channel_id=1, source_target_pairs={{0,2},{1,5},{2,0},{3,7},{4,6},{5,1},{6,4},{7,3},{8,10},{9,13},{10,... | collective-permute-start | bytes 786440 | tf_op jit(solution)/shard_map/ppermute | solution.py:241
  13.6 1.5 %collective-permute-start.7 = (f32[64,1024]{1,0:T(8,128)S(1)}, f32[64,1024]{1,0:T(8,128)S(1)}, u32[]{:S(2)}, u32[]{:S(2)}) collective-permute-start(f32[64,1024]{1,0:T(8,128)S(1)} %constant_dynamic-update-slice_fusion.refs_0_), channel_id=1, source_target_pairs={{0,4},{1,3},{2,6},{3,1},{4,0},{5,7},{6,2},{7,5},{8,12},{9,11},{10,... | collective-permute-start | bytes 786440 | tf_op jit(solution)/shard_map/ppermute | solution.py:241
  15.1 0.5 %collective-permute-start.2 = (f32[64,1152]{1,0:T(8,128)S(1)}, f32[64,1152]{1,0:T(8,128)S(1)}, u32[]{:S(2)}, u32[]{:S(2)}) collective-permute-start(f32[64,1152]{1,0:T(8,128)S(1)} %get-tuple-element.33), channel_id=1, source_target_pairs={{0,2},{1,5},{2,0},{3,7},{4,6},{5,1},{6,4},{7,3},{8,10},{9,13},{10,... | collective-permute-start | bytes 884744 | tf_op jit(solution)/shard_map/ppermute | solution.py:241
  15.6 1.5 %collective-permute-start.1 = (f32[64,1152]{1,0:T(8,128)S(1)}, f32[64,1152]{1,0:T(8,128)S(1)}, u32[]{:S(2)}, u32[]{:S(2)}) collective-permute-start(f32[64,1152]{1,0:T(8,128)S(1)} %get-tuple-element.31), channel_id=1, source_target_pairs={{0,2},{1,5},{2,0},{3,7},{4,6},{5,1},{6,4},{7,3},{8,10},{9,13},{10,... | collective-permute-start | bytes 884744 | tf_op jit(solution)/shard_map/ppermute | solution.py:241
  17.1 4.1 %collective-permute-done.6.refs_1_ = f32[64,1024]{1,0:T(8,128)S(1)} collective-permute-done((f32[64,1024]{1,0:T(8,128)S(1)}, f32[64,1024]{1,0:T(8,128)S(1)}, u32[]{:S(2)}, u32[]{:S(2)}) %collective-permute-start.6) | collective-permute-done | bytes 262176 | tf_op jit(solution)/shard_map/ppermute | solution.py:241
  21.2 1.6 %collective-permute-done.7.refs_2_ = f32[64,1024]{1,0:T(8,128)S(1)} collective-permute-done((f32[64,1024]{1,0:T(8,128)S(1)}, f32[64,1024]{1,0:T(8,128)S(1)}, u32[]{:S(2)}, u32[]{:S(2)}) %collective-permute-start.7) | collective-permute-done | bytes 262176 | tf_op jit(solution)/shard_map/ppermute | solution.py:241
  22.8 1.5 %collective-permute-start.13 = (f32[64,1024]{1,0:T(8,128)S(1)}, f32[64,1024]{1,0:T(8,128)S(1)}, u32[]{:S(2)}, u32[]{:S(2)}) collective-permute-start(f32[64,1024]{1,0:T(8,128)S(1)} %collective-permute-done.6.refs_1_), channel_id=1, source_target_pairs={{0,4},{1,3},{2,6},{3,1},{4,0},{5,7},{6,2},{7,5},{8,12},{9,11},{10,... | collective-permute-start | bytes 786440 | tf_op jit(solution)/shard_map/ppermute | solution.py:241
  24.4 0.6 %near.1 = (bf16[256,1024]{1,0:T(8,128)(2,1)S(1)}, bf16[256,1024]{1,0:T(8,128)(2,1)S(1)}, f32[256,8]{1,0:T(8,128)S(1)}) custom-call(f32[8,256,1024]{2,1,0:T(8,128)S(1)} %get-tuple-element.34.slab_ref, f32[64,1024]{1,0:T(8,128)S(1)} %constant_dynamic-update-slice_fusion.refs_0_, f32[64,1024]{1,0:T(8,128)S(1)} %collective-permute-done.6.refs_1_, ...), custom_call_target="tpu_custom_call" | custom-call | flops 13421772800 | tf_op jit(solution)/shard_map/near/pallas_call | solution.py:320
  25.0 0.0 collective-permute-done.2
  25.0 1.4 %collective-permute-start.8 = (f32[64,1152]{1,0:T(8,128)S(1)}, f32[64,1152]{1,0:T(8,128)S(1)}, u32[]{:S(2)}, u32[]{:S(2)}) collective-permute-start(f32[64,1152]{1,0:T(8,128)S(1)} %add.25), channel_id=1, source_target_pairs={{0,4},{1,3},{2,6},{3,1},{4,0},{5,7},{6,2},{7,5},{8,12},{9,11},{10,... | collective-permute-start | bytes 884744 | tf_op jit(solution)/shard_map/ppermute | solution.py:241
  26.4 2.8 %collective-permute-done.13.buf_ref = f32[64,1024]{1,0:T(8,128)S(1)} collective-permute-done((f32[64,1024]{1,0:T(8,128)S(1)}, f32[64,1024]{1,0:T(8,128)S(1)}, u32[]{:S(2)}, u32[]{:S(2)}) %collective-permute-start.13) | collective-permute-done | bytes 262176 | tf_op jit(solution)/shard_map/ppermute | solution.py:241
  29.2 1.0 %ranks.1 = (bf16[256,1024]{1,0:T(8,128)(2,1)S(1)}, bf16[256,1024]{1,0:T(8,128)(2,1)S(1)}, f32[256,256]{1,0:T(8,128)S(1)}, f32[8,256]{1,0:T(8,128)S(1)}) custom-call(f32[8,256,1024]{2,1,0:T(8,128)S(1)} %get-tuple-element.34.slab_ref, f32[8,256]{1,0:T(8,128)S(1)} %get-tuple-element.40.c_ref.refs_2_, f32[256,256]{1,0:T(8,128)S(1)} %get-tuple-element.41.gram_ref, ...), custom_call_target="tpu_custom_call" | custom-call | flops 13421772800 | tf_op jit(solution)/shard_map/ranks/pallas_call | solution.py:333
  30.2 0.4 collective-permute-start.14
  30.7 0.8 %collective-permute-done.14 = f32[8,256]{1,0:T(8,128)S(1)} collective-permute-done((f32[8,256]{1,0:T(8,128)S(1)}, f32[8,256]{1,0:T(8,128)S(1)}, u32[]{:S(2)}, u32[]{:S(2)}) %collective-permute-start.14) | collective-permute-done | bytes 8224 | tf_op jit(solution)/shard_map/ppermute | solution.py:248
  31.5 1.4 %collective-permute-start.15 = (f32[8,256]{1,0:T(8,128)S(1)}, f32[8,256]{1,0:T(8,128)S(1)}, u32[]{:S(2)}, u32[]{:S(2)}) collective-permute-start(f32[8,256]{1,0:T(8,128)S(1)} %add.30.a_ref), channel_id=1, source_target_pairs={{0,4},{1,3},{2,6},{3,1},{4,0},{5,7},{6,2},{7,5},{8,12},{9,11},{10,... | collective-permute-start | bytes 24584 | tf_op jit(solution)/shard_map/ppermute | solution.py:241
  32.9 0.0 collective-permute-done.1
  32.9 0.0 collective-permute-done.8
  32.9 0.1 add_add_fusion
  33.0 1.0 %collective-permute-start.11 = (f32[16,1152]{1,0:T(8,128)S(1)}, f32[16,1152]{1,0:T(8,128)S(1)}, u32[]{:S(2)}, u32[]{:S(2)}) collective-permute-start(f32[16,1152]{1,0:T(8,128)S(1)} %get-tuple-element.58), channel_id=1, source_target_pairs={{0,8},{1,9},{2,10},{3,11},{4,12},{5,13},{6,14},{7,15},{8,0},{9,1},... | collective-permute-start | bytes 221192 | tf_op jit(solution)/shard_map/ppermute | solution.py:241
  34.0 2.5 %collective-permute-start.10 = (f32[16,1152]{1,0:T(8,128)S(1)}, f32[16,1152]{1,0:T(8,128)S(1)}, u32[]{:S(2)}, u32[]{:S(2)}) collective-permute-start(f32[16,1152]{1,0:T(8,128)S(1)} %get-tuple-element.59), channel_id=1, source_target_pairs={{0,24},{1,17},{2,26},{3,19},{4,28},{5,21},{6,30},{7,23},{8,16},{9,... | collective-permute-start | bytes 221192 | tf_op jit(solution)/shard_map/ppermute | solution.py:241
  36.5 0.0 collective-permute-start.9
  36.5 0.0 collective-permute-done.15.b_ref
  36.6 1.4 %collective-permute-start.17 = (f32[8,256]{1,0:T(8,128)S(1)}, f32[8,256]{1,0:T(8,128)S(1)}, u32[]{:S(2)}, u32[]{:S(2)}) collective-permute-start(f32[8,256]{1,0:T(8,128)S(1)} %sum.1), channel_id=1, source_target_pairs={{0,2},{1,5},{2,0},{3,7},{4,6},{5,1},{6,4},{7,3},{8,10},{9,13},{10,... | collective-permute-start | bytes 24584 | tf_op jit(solution)/shard_map/ppermute | solution.py:241
  37.9 2.2 %rows.1 = (f32[64,256]{1,0:T(8,128)S(1)}, f32[64,256]{1,0:T(8,128)S(1)}) custom-call(bf16[1024,1024]{1,0:T(8,128)(2,1)S(1)} %get-tuple-element.46.high_ref, bf16[1024,1024]{1,0:T(8,128)(2,1)S(1)} %get-tuple-element.47.low_ref, bf16[256,1024]{1,0:T(8,128)(2,1)S(1)} %get-tuple-element.44.bt_high.refs_4_, ...), custom_call_target="tpu_custom_call" | custom-call | flops 536870912 | tf_op jit(solution)/shard_map/rows/pallas_call | solution.py:356
  40.2 0.1 collective-permute-start.16
  40.2 0.0 collective-permute-done.17
  40.3 2.8 %collective-permute-start.18 = (f32[8,256]{1,0:T(8,128)S(1)}, f32[8,256]{1,0:T(8,128)S(1)}, u32[]{:S(2)}, u32[]{:S(2)}) collective-permute-start(f32[8,256]{1,0:T(8,128)S(1)} %add.31.refs_8_), channel_id=1, source_target_pairs={{0,24},{1,25},{2,26},{3,27},{4,28},{5,29},{6,30},{7,31},{8,16},{9,... | collective-permute-start | bytes 24584 | tf_op jit(solution)/shard_map/ppermute | solution.py:241
  43.1 0.0 collective-permute-done.11
  43.1 0.7 %collective-permute-start.19 = (f32[8,256]{1,0:T(8,128)S(1)}, f32[8,256]{1,0:T(8,128)S(1)}, u32[]{:S(2)}, u32[]{:S(2)}) collective-permute-start(f32[8,256]{1,0:T(8,128)S(1)} %add.31.refs_8_), channel_id=1, source_target_pairs={{0,16},{1,17},{2,18},{3,19},{4,20},{5,21},{6,22},{7,23},{8,24},{9,... | collective-permute-start | bytes 24584 | tf_op jit(solution)/shard_map/ppermute | solution.py:241
  43.8 0.0 collective-permute-done.10
  43.8 1.0 %collective-permute-start.20 = (f32[8,256]{1,0:T(8,128)S(1)}, f32[8,256]{1,0:T(8,128)S(1)}, u32[]{:S(2)}, u32[]{:S(2)}) collective-permute-start(f32[8,256]{1,0:T(8,128)S(1)} %add.31.refs_8_), channel_id=1, source_target_pairs={{0,8},{1,9},{2,10},{3,11},{4,12},{5,13},{6,14},{7,15},{8,0},{9,1},... | collective-permute-start | bytes 24584 | tf_op jit(solution)/shard_map/ppermute | solution.py:241
  44.7 0.0 collective-permute-done.9
  44.8 0.1 collective-permute-start.12
  44.9 0.9 %collective-permute-done.18.refs_9_ = f32[8,256]{1,0:T(8,128)S(1)} collective-permute-done((f32[8,256]{1,0:T(8,128)S(1)}, f32[8,256]{1,0:T(8,128)S(1)}, u32[]{:S(2)}, u32[]{:S(2)}) %collective-permute-start.18) | collective-permute-done | bytes 8224 | tf_op jit(solution)/shard_map/ppermute | solution.py:241
  45.8 1.9 %collective-permute-done.19.refs_10_ = f32[8,256]{1,0:T(8,128)S(1)} collective-permute-done((f32[8,256]{1,0:T(8,128)S(1)}, f32[8,256]{1,0:T(8,128)S(1)}, u32[]{:S(2)}, u32[]{:S(2)}) %collective-permute-start.19) | collective-permute-done | bytes 8224 | tf_op jit(solution)/shard_map/ppermute | solution.py:241
  47.6 0.0 collective-permute-done.20.refs_11_
  47.7 0.0 collective-permute-done.16.refs_7_
  47.7 0.0 collective-permute-done.12.refs_1_
  47.7 1.3 %last.1 = (f32[16,1024]{1,0:T(8,128)}, f32[64,256]{1,0:T(8,128)}, f32[8,256]{1,0:T(8,128)}) custom-call(f32[16,128]{1,0:T(8,128)S(1)} %slice.8.refs_0_, f32[16,128]{1,0:T(8,128)S(1)} %collective-permute-done.12.refs_1_, f32[8,256]{1,0:T(8,128)S(1)} %get-tuple-element.40.c_ref.refs_2_, f32[16,1024]{1,0:T(8,128)S(1)} %slice.9.refs_3_, ...), custom_call_target="tpu_custom_call" | custom-call | flops 4194304 | tf_op jit(solution)/shard_map/last/pallas_call | solution.py:371
  (12 shorter events, 0.1 us)
Async XLA Ops:
  0.6 5.8 %collective-permute-start = (f32[64,256]{1,0:T(8,128)}, f32[64,256]{1,0:T(8,128)S(1)}, u32[]{:S(2)}, u32[]{:S(2)}) collective-permute-start(f32[64,256]{1,0:T(8,128)} %a_hbm.1), channel_id=1, source_target_pairs={{0,1},{1,0},{2,3},{3,2},{4,5},{5,4},{6,7},{7,6},{8,9},{9,8},{10,11... | collective-permute-start | bytes 196616 | tf_op jit(solution)/shard_map/ppermute | solution.py:248
  1.1 9.8 %collective-permute-start.3 = (f32[16,1024]{1,0:T(8,128)}, f32[16,1024]{1,0:T(8,128)S(1)}, u32[]{:S(2)}, u32[]{:S(2)}) collective-permute-start(f32[16,1024]{1,0:T(8,128)} %own_hbm.1), channel_id=1, source_target_pairs={{0,16},{1,25},{2,18},{3,27},{4,20},{5,29},{6,22},{7,31},{8,24},{9,... | collective-permute-start | bytes 196616 | tf_op jit(solution)/shard_map/ppermute | solution.py:241
  4.8 6.6 %collective-permute-start.4 = (f32[16,1024]{1,0:T(8,128)}, f32[16,1024]{1,0:T(8,128)S(1)}, u32[]{:S(2)}, u32[]{:S(2)}) collective-permute-start(f32[16,1024]{1,0:T(8,128)} %own_hbm.1), channel_id=1, source_target_pairs={{0,24},{1,17},{2,26},{3,19},{4,28},{5,21},{6,30},{7,23},{8,16},{9,... | collective-permute-start | bytes 196616 | tf_op jit(solution)/shard_map/ppermute | solution.py:241
  6.2 5.9 %collective-permute-start.5 = (f32[16,1024]{1,0:T(8,128)}, f32[16,1024]{1,0:T(8,128)S(1)}, u32[]{:S(2)}, u32[]{:S(2)}) collective-permute-start(f32[16,1024]{1,0:T(8,128)} %own_hbm.1), channel_id=1, source_target_pairs={{0,8},{1,9},{2,10},{3,11},{4,12},{5,13},{6,14},{7,15},{8,0},{9,1},... | collective-permute-start | bytes 196616 | tf_op jit(solution)/shard_map/ppermute | solution.py:241
  12.1 9.1 %collective-permute-start.6 = (f32[64,1024]{1,0:T(8,128)S(1)}, f32[64,1024]{1,0:T(8,128)S(1)}, u32[]{:S(2)}, u32[]{:S(2)}) collective-permute-start(f32[64,1024]{1,0:T(8,128)S(1)} %constant_dynamic-update-slice_fusion.refs_0_), channel_id=1, source_target_pairs={{0,2},{1,5},{2,0},{3,7},{4,6},{5,1},{6,4},{7,3},{8,10},{9,13},{10,... | collective-permute-start | bytes 786440 | tf_op jit(solution)/shard_map/ppermute | solution.py:241
  13.6 9.2 %collective-permute-start.7 = (f32[64,1024]{1,0:T(8,128)S(1)}, f32[64,1024]{1,0:T(8,128)S(1)}, u32[]{:S(2)}, u32[]{:S(2)}) collective-permute-start(f32[64,1024]{1,0:T(8,128)S(1)} %constant_dynamic-update-slice_fusion.refs_0_), channel_id=1, source_target_pairs={{0,4},{1,3},{2,6},{3,1},{4,0},{5,7},{6,2},{7,5},{8,12},{9,11},{10,... | collective-permute-start | bytes 786440 | tf_op jit(solution)/shard_map/ppermute | solution.py:241
  15.1 9.9 %collective-permute-start.2 = (f32[64,1152]{1,0:T(8,128)S(1)}, f32[64,1152]{1,0:T(8,128)S(1)}, u32[]{:S(2)}, u32[]{:S(2)}) collective-permute-start(f32[64,1152]{1,0:T(8,128)S(1)} %get-tuple-element.33), channel_id=1, source_target_pairs={{0,2},{1,5},{2,0},{3,7},{4,6},{5,1},{6,4},{7,3},{8,10},{9,13},{10,... | collective-permute-start | bytes 884744 | tf_op jit(solution)/shard_map/ppermute | solution.py:241
  15.6 17.3 %collective-permute-start.1 = (f32[64,1152]{1,0:T(8,128)S(1)}, f32[64,1152]{1,0:T(8,128)S(1)}, u32[]{:S(2)}, u32[]{:S(2)}) collective-permute-start(f32[64,1152]{1,0:T(8,128)S(1)} %get-tuple-element.31), channel_id=1, source_target_pairs={{0,2},{1,5},{2,0},{3,7},{4,6},{5,1},{6,4},{7,3},{8,10},{9,13},{10,... | collective-permute-start | bytes 884744 | tf_op jit(solution)/shard_map/ppermute | solution.py:241
  22.8 6.4 %collective-permute-start.13 = (f32[64,1024]{1,0:T(8,128)S(1)}, f32[64,1024]{1,0:T(8,128)S(1)}, u32[]{:S(2)}, u32[]{:S(2)}) collective-permute-start(f32[64,1024]{1,0:T(8,128)S(1)} %collective-permute-done.6.refs_1_), channel_id=1, source_target_pairs={{0,4},{1,3},{2,6},{3,1},{4,0},{5,7},{6,2},{7,5},{8,12},{9,11},{10,... | collective-permute-start | bytes 786440 | tf_op jit(solution)/shard_map/ppermute | solution.py:241
  25.0 7.9 %collective-permute-start.8 = (f32[64,1152]{1,0:T(8,128)S(1)}, f32[64,1152]{1,0:T(8,128)S(1)}, u32[]{:S(2)}, u32[]{:S(2)}) collective-permute-start(f32[64,1152]{1,0:T(8,128)S(1)} %add.25), channel_id=1, source_target_pairs={{0,4},{1,3},{2,6},{3,1},{4,0},{5,7},{6,2},{7,5},{8,12},{9,11},{10,... | collective-permute-start | bytes 884744 | tf_op jit(solution)/shard_map/ppermute | solution.py:241
  30.2 1.3 %collective-permute-start.14 = (f32[8,256]{1,0:T(8,128)S(1)}, f32[8,256]{1,0:T(8,128)S(1)}, u32[]{:S(2)}, u32[]{:S(2)}) collective-permute-start(f32[8,256]{1,0:T(8,128)S(1)} %get-tuple-element.50), channel_id=1, source_target_pairs={{0,1},{1,0},{2,3},{3,2},{4,5},{5,4},{6,7},{7,6},{8,9},{9,8},{10,11... | collective-permute-start | bytes 24584 | tf_op jit(solution)/shard_map/ppermute | solution.py:248
  31.5 5.1 %collective-permute-start.15 = (f32[8,256]{1,0:T(8,128)S(1)}, f32[8,256]{1,0:T(8,128)S(1)}, u32[]{:S(2)}, u32[]{:S(2)}) collective-permute-start(f32[8,256]{1,0:T(8,128)S(1)} %add.30.a_ref), channel_id=1, source_target_pairs={{0,4},{1,3},{2,6},{3,1},{4,0},{5,7},{6,2},{7,5},{8,12},{9,11},{10,... | collective-permute-start | bytes 24584 | tf_op jit(solution)/shard_map/ppermute | solution.py:241
  33.0 10.1 %collective-permute-start.11 = (f32[16,1152]{1,0:T(8,128)S(1)}, f32[16,1152]{1,0:T(8,128)S(1)}, u32[]{:S(2)}, u32[]{:S(2)}) collective-permute-start(f32[16,1152]{1,0:T(8,128)S(1)} %get-tuple-element.58), channel_id=1, source_target_pairs={{0,8},{1,9},{2,10},{3,11},{4,12},{5,13},{6,14},{7,15},{8,0},{9,1},... | collective-permute-start | bytes 221192 | tf_op jit(solution)/shard_map/ppermute | solution.py:241
  34.0 9.7 %collective-permute-start.10 = (f32[16,1152]{1,0:T(8,128)S(1)}, f32[16,1152]{1,0:T(8,128)S(1)}, u32[]{:S(2)}, u32[]{:S(2)}) collective-permute-start(f32[16,1152]{1,0:T(8,128)S(1)} %get-tuple-element.59), channel_id=1, source_target_pairs={{0,24},{1,17},{2,26},{3,19},{4,28},{5,21},{6,30},{7,23},{8,16},{9,... | collective-permute-start | bytes 221192 | tf_op jit(solution)/shard_map/ppermute | solution.py:241
  36.5 8.2 %collective-permute-start.9 = (f32[16,1152]{1,0:T(8,128)S(1)}, f32[16,1152]{1,0:T(8,128)S(1)}, u32[]{:S(2)}, u32[]{:S(2)}) collective-permute-start(f32[16,1152]{1,0:T(8,128)S(1)} %get-tuple-element.57), channel_id=1, source_target_pairs={{0,16},{1,25},{2,18},{3,27},{4,20},{5,29},{6,22},{7,31},{8,24},{9,... | collective-permute-start | bytes 221192 | tf_op jit(solution)/shard_map/ppermute | solution.py:241
  36.6 3.7 %collective-permute-start.17 = (f32[8,256]{1,0:T(8,128)S(1)}, f32[8,256]{1,0:T(8,128)S(1)}, u32[]{:S(2)}, u32[]{:S(2)}) collective-permute-start(f32[8,256]{1,0:T(8,128)S(1)} %sum.1), channel_id=1, source_target_pairs={{0,2},{1,5},{2,0},{3,7},{4,6},{5,1},{6,4},{7,3},{8,10},{9,13},{10,... | collective-permute-start | bytes 24584 | tf_op jit(solution)/shard_map/ppermute | solution.py:241
  40.2 7.5 %collective-permute-start.16 = (f32[64,256]{1,0:T(8,128)S(1)}, f32[64,256]{1,0:T(8,128)S(1)}, u32[]{:S(2)}, u32[]{:S(2)}) collective-permute-start(f32[64,256]{1,0:T(8,128)S(1)} %get-tuple-element.53), channel_id=1, source_target_pairs={{0,1},{1,0},{2,3},{3,2},{4,5},{5,4},{6,7},{7,6},{8,9},{9,8},{10,11... | collective-permute-start | bytes 196616 | tf_op jit(solution)/shard_map/ppermute | solution.py:248
  40.3 5.5 %collective-permute-start.18 = (f32[8,256]{1,0:T(8,128)S(1)}, f32[8,256]{1,0:T(8,128)S(1)}, u32[]{:S(2)}, u32[]{:S(2)}) collective-permute-start(f32[8,256]{1,0:T(8,128)S(1)} %add.31.refs_8_), channel_id=1, source_target_pairs={{0,24},{1,25},{2,26},{3,27},{4,28},{5,29},{6,30},{7,31},{8,16},{9,... | collective-permute-start | bytes 24584 | tf_op jit(solution)/shard_map/ppermute | solution.py:241
  43.1 4.6 %collective-permute-start.19 = (f32[8,256]{1,0:T(8,128)S(1)}, f32[8,256]{1,0:T(8,128)S(1)}, u32[]{:S(2)}, u32[]{:S(2)}) collective-permute-start(f32[8,256]{1,0:T(8,128)S(1)} %add.31.refs_8_), channel_id=1, source_target_pairs={{0,16},{1,17},{2,18},{3,19},{4,20},{5,21},{6,22},{7,23},{8,24},{9,... | collective-permute-start | bytes 24584 | tf_op jit(solution)/shard_map/ppermute | solution.py:241
  43.8 3.9 %collective-permute-start.20 = (f32[8,256]{1,0:T(8,128)S(1)}, f32[8,256]{1,0:T(8,128)S(1)}, u32[]{:S(2)}, u32[]{:S(2)}) collective-permute-start(f32[8,256]{1,0:T(8,128)S(1)} %add.31.refs_8_), channel_id=1, source_target_pairs={{0,8},{1,9},{2,10},{3,11},{4,12},{5,13},{6,14},{7,15},{8,0},{9,1},... | collective-permute-start | bytes 24584 | tf_op jit(solution)/shard_map/ppermute | solution.py:241
  44.8 2.9 %collective-permute-start.12 = (f32[16,128]{1,0:T(8,128)S(1)}, f32[16,128]{1,0:T(8,128)S(1)}, u32[]{:S(2)}, u32[]{:S(2)}) collective-permute-start(f32[16,128]{1,0:T(8,128)S(1)} %slice.8.refs_0_), channel_id=1, source_target_pairs={{0,1},{1,0},{2,3},{3,2},{4,5},{5,4},{6,7},{7,6},{8,9},{9,8},{10,11... | collective-permute-start | bytes 24584 | tf_op jit(solution)/shard_map/ppermute | solution.py:248

commit v4 on v3

--- a/solution.py
+++ b/solution.py
@@ -347,7 +347,7 @@
     total = pay_own + got_f + got_s
     slots = jnp.split(total, n_line, axis=0)
     total = slots[0]
-    for d in range(1, n_line):
+    for d in reversed(range(1, n_line)):
         total = total + move(slots[d], apart[d])
     cross, _ = tie((cross, part_c))
     part_c = part_c + move(part_c, first)

time: 49.1 us -> 49 us (level)
  starting transfers between devices: 25.1 us -> 25.6 us
  waiting for transfers between devices: 13.3 us -> 12.8 us
where the time goes in v4:
time: 49 us; the launch traced here: 48.9 us
  starting transfers between devices  25.6 us (52%)
  waiting for transfers between devices  12.8 us (26%)
  Pallas kernels  9.57 us (20%)
  between operations  0.76 us (2%)
    ppermute x17, starting transfers between devices, move(): lax.ppermute(x, ('row', 'col'), [(r * n_col + c, target(r, c) * n_col + c...  24.5 us
    ppermute x17, waiting for transfers between devices, move(): lax.ppermute(x, ('row', 'col'), [(r * n_col + c, target(r, c) * n_col + c...  12 us
    pallas_call x1, Pallas kernels, local(): pl.pallas_call(kernel, in_specs=[hbm] * 4 + [vmem] * (len(a_parts) - 1),...  4.48 us
    pallas_call x1, Pallas kernels, local(): call(functools.partial(rows_kernel, pair), 'rows', work, [((half, rank),...  2.2 us
    pallas_call x1, Pallas kernels, local(): call(functools.partial(last_kernel, pair, len(grams) - 1), 'last', rank_r...  1.26 us
    ppermute x4, starting transfers between devices, swap(): return lax.ppermute(x, 'col', [(0, 1), (1, 0)])  1.09 us
    pallas_call x1, Pallas kernels, local(): call(functools.partial(ranks_kernel, n_line, rank_rows), 'ranks', WEIGHT...  0.98 us
  transfers between devices with their start and end apart: 21, of which 8 were waited for; matrix products, arithmetic and copies ran while one was open for 0% of the time, Pallas kernels for 17%

profile of v4, /device:TPU:0, one launch (start us, length us, event | category | flops | bytes accessed | tf_op | source)
XLA Modules:
  0.0 48.9 jit_solution(14670948102602372888)
XLA Ops:
  0.6 0.5 %collective-permute-start = (f32[64,256]{1,0:T(8,128)}, f32[64,256]{1,0:T(8,128)S(1)}, u32[]{:S(2)}, u32[]{:S(2)}) collective-permute-start(f32[64,256]{1,0:T(8,128)} %a_hbm.1), channel_id=1, source_target_pairs={{0,1},{1,0},{2,3},{3,2},{4,5},{5,4},{6,7},{7,6},{8,9},{9,8},{10,11... | collective-permute-start | bytes 196616 | tf_op jit(solution)/shard_map/ppermute | solution.py:248
  1.1 3.7 %collective-permute-start.3 = (f32[16,1024]{1,0:T(8,128)}, f32[16,1024]{1,0:T(8,128)S(1)}, u32[]{:S(2)}, u32[]{:S(2)}) collective-permute-start(f32[16,1024]{1,0:T(8,128)} %own_hbm.1), channel_id=1, source_target_pairs={{0,16},{1,25},{2,18},{3,27},{4,20},{5,29},{6,22},{7,31},{8,24},{9,... | collective-permute-start | bytes 196616 | tf_op jit(solution)/shard_map/ppermute | solution.py:241
  4.8 1.3 %collective-permute-start.4 = (f32[16,1024]{1,0:T(8,128)}, f32[16,1024]{1,0:T(8,128)S(1)}, u32[]{:S(2)}, u32[]{:S(2)}) collective-permute-start(f32[16,1024]{1,0:T(8,128)} %own_hbm.1), channel_id=1, source_target_pairs={{0,24},{1,17},{2,26},{3,19},{4,28},{5,21},{6,30},{7,23},{8,16},{9,... | collective-permute-start | bytes 196616 | tf_op jit(solution)/shard_map/ppermute | solution.py:241
  6.2 0.2 collective-permute-start.5
  6.4 0.0 collective-permute-done.other_ref
  6.4 4.5 %early.1 = (f32[64,1152]{1,0:T(8,128)S(1)}, f32[64,1152]{1,0:T(8,128)S(1)}, f32[64,1152]{1,0:T(8,128)S(1)}, f32[64,1152]{1,0:T(8,128)S(1)}, f32[8,256,1024]{2,1,...) custom-call(f32[8,128,1024]{2,1,0:T(8,128)} %t_hbm.1, ...), custom_call_target="tpu_custom_call" | custom-call | flops 536870912 | tf_op jit(solution)/shard_map/early/pallas_call | solution.py:282
  10.9 0.0 collective-permute-done.3
  10.9 0.5 collective-permute-done.4
  11.4 0.7 %collective-permute-done.5 = f32[16,1024]{1,0:T(8,128)S(1)} collective-permute-done((f32[16,1024]{1,0:T(8,128)}, f32[16,1024]{1,0:T(8,128)S(1)}, u32[]{:S(2)}, u32[]{:S(2)}) %collective-permute-start.5) | collective-permute-done | bytes 65568 | tf_op jit(solution)/shard_map/ppermute | solution.py:241
  12.1 1.5 %collective-permute-start.6 = (f32[64,1024]{1,0:T(8,128)S(1)}, f32[64,1024]{1,0:T(8,128)S(1)}, u32[]{:S(2)}, u32[]{:S(2)}) collective-permute-start(f32[64,1024]{1,0:T(8,128)S(1)} %constant_dynamic-update-slice_fusion.refs_0_), channel_id=1, source_target_pairs={{0,2},{1,5},{2,0},{3,7},{4,6},{5,1},{6,4},{7,3},{8,10},{9,13},{10,... | collective-permute-start | bytes 786440 | tf_op jit(solution)/shard_map/ppermute | solution.py:241
  13.6 1.5 %collective-permute-start.7 = (f32[64,1024]{1,0:T(8,128)S(1)}, f32[64,1024]{1,0:T(8,128)S(1)}, u32[]{:S(2)}, u32[]{:S(2)}) collective-permute-start(f32[64,1024]{1,0:T(8,128)S(1)} %constant_dynamic-update-slice_fusion.refs_0_), channel_id=1, source_target_pairs={{0,4},{1,3},{2,6},{3,1},{4,0},{5,7},{6,2},{7,5},{8,12},{9,11},{10,... | collective-permute-start | bytes 786440 | tf_op jit(solution)/shard_map/ppermute | solution.py:241
  15.1 0.5 %collective-permute-start.2 = (f32[64,1152]{1,0:T(8,128)S(1)}, f32[64,1152]{1,0:T(8,128)S(1)}, u32[]{:S(2)}, u32[]{:S(2)}) collective-permute-start(f32[64,1152]{1,0:T(8,128)S(1)} %get-tuple-element.33), channel_id=1, source_target_pairs={{0,2},{1,5},{2,0},{3,7},{4,6},{5,1},{6,4},{7,3},{8,10},{9,13},{10,... | collective-permute-start | bytes 884744 | tf_op jit(solution)/shard_map/ppermute | solution.py:241
  15.6 1.5 %collective-permute-start.1 = (f32[64,1152]{1,0:T(8,128)S(1)}, f32[64,1152]{1,0:T(8,128)S(1)}, u32[]{:S(2)}, u32[]{:S(2)}) collective-permute-start(f32[64,1152]{1,0:T(8,128)S(1)} %get-tuple-element.31), channel_id=1, source_target_pairs={{0,2},{1,5},{2,0},{3,7},{4,6},{5,1},{6,4},{7,3},{8,10},{9,13},{10,... | collective-permute-start | bytes 884744 | tf_op jit(solution)/shard_map/ppermute | solution.py:241
  17.1 4.1 %collective-permute-done.6.refs_1_ = f32[64,1024]{1,0:T(8,128)S(1)} collective-permute-done((f32[64,1024]{1,0:T(8,128)S(1)}, f32[64,1024]{1,0:T(8,128)S(1)}, u32[]{:S(2)}, u32[]{:S(2)}) %collective-permute-start.6) | collective-permute-done | bytes 262176 | tf_op jit(solution)/shard_map/ppermute | solution.py:241
  21.2 1.6 %collective-permute-done.7.refs_2_ = f32[64,1024]{1,0:T(8,128)S(1)} collective-permute-done((f32[64,1024]{1,0:T(8,128)S(1)}, f32[64,1024]{1,0:T(8,128)S(1)}, u32[]{:S(2)}, u32[]{:S(2)}) %collective-permute-start.7) | collective-permute-done | bytes 262176 | tf_op jit(solution)/shard_map/ppermute | solution.py:241
  22.8 1.5 %collective-permute-start.13 = (f32[64,1024]{1,0:T(8,128)S(1)}, f32[64,1024]{1,0:T(8,128)S(1)}, u32[]{:S(2)}, u32[]{:S(2)}) collective-permute-start(f32[64,1024]{1,0:T(8,128)S(1)} %collective-permute-done.6.refs_1_), channel_id=1, source_target_pairs={{0,4},{1,3},{2,6},{3,1},{4,0},{5,7},{6,2},{7,5},{8,12},{9,11},{10,... | collective-permute-start | bytes 786440 | tf_op jit(solution)/shard_map/ppermute | solution.py:241
  24.4 0.6 %near.1 = (bf16[256,1024]{1,0:T(8,128)(2,1)S(1)}, bf16[256,1024]{1,0:T(8,128)(2,1)S(1)}, f32[256,8]{1,0:T(8,128)S(1)}) custom-call(f32[8,256,1024]{2,1,0:T(8,128)S(1)} %get-tuple-element.34.slab_ref, f32[64,1024]{1,0:T(8,128)S(1)} %constant_dynamic-update-slice_fusion.refs_0_, f32[64,1024]{1,0:T(8,128)S(1)} %collective-permute-done.6.refs_1_, ...), custom_call_target="tpu_custom_call" | custom-call | flops 13421772800 | tf_op jit(solution)/shard_map/near/pallas_call | solution.py:320
  25.0 0.0 collective-permute-done.2
  25.0 1.4 %collective-permute-start.8 = (f32[64,1152]{1,0:T(8,128)S(1)}, f32[64,1152]{1,0:T(8,128)S(1)}, u32[]{:S(2)}, u32[]{:S(2)}) collective-permute-start(f32[64,1152]{1,0:T(8,128)S(1)} %add.25), channel_id=1, source_target_pairs={{0,4},{1,3},{2,6},{3,1},{4,0},{5,7},{6,2},{7,5},{8,12},{9,11},{10,... | collective-permute-start | bytes 884744 | tf_op jit(solution)/shard_map/ppermute | solution.py:241
  26.4 2.8 %collective-permute-done.13.buf_ref = f32[64,1024]{1,0:T(8,128)S(1)} collective-permute-done((f32[64,1024]{1,0:T(8,128)S(1)}, f32[64,1024]{1,0:T(8,128)S(1)}, u32[]{:S(2)}, u32[]{:S(2)}) %collective-permute-start.13) | collective-permute-done | bytes 262176 | tf_op jit(solution)/shard_map/ppermute | solution.py:241
  29.2 1.0 %ranks.1 = (bf16[256,1024]{1,0:T(8,128)(2,1)S(1)}, bf16[256,1024]{1,0:T(8,128)(2,1)S(1)}, f32[256,256]{1,0:T(8,128)S(1)}, f32[8,256]{1,0:T(8,128)S(1)}) custom-call(f32[8,256,1024]{2,1,0:T(8,128)S(1)} %get-tuple-element.34.slab_ref, f32[8,256]{1,0:T(8,128)S(1)} %get-tuple-element.40.c_ref.refs_2_, f32[256,256]{1,0:T(8,128)S(1)} %get-tuple-element.41.gram_ref, ...), custom_call_target="tpu_custom_call" | custom-call | flops 13421772800 | tf_op jit(solution)/shard_map/ranks/pallas_call | solution.py:333
  30.2 0.4 collective-permute-start.14
  30.7 0.8 %collective-permute-done.14 = f32[8,256]{1,0:T(8,128)S(1)} collective-permute-done((f32[8,256]{1,0:T(8,128)S(1)}, f32[8,256]{1,0:T(8,128)S(1)}, u32[]{:S(2)}, u32[]{:S(2)}) %collective-permute-start.14) | collective-permute-done | bytes 8224 | tf_op jit(solution)/shard_map/ppermute | solution.py:248
  31.5 1.4 %collective-permute-start.15 = (f32[8,256]{1,0:T(8,128)S(1)}, f32[8,256]{1,0:T(8,128)S(1)}, u32[]{:S(2)}, u32[]{:S(2)}) collective-permute-start(f32[8,256]{1,0:T(8,128)S(1)} %add.30.a_ref), channel_id=1, source_target_pairs={{0,4},{1,3},{2,6},{3,1},{4,0},{5,7},{6,2},{7,5},{8,12},{9,11},{10,... | collective-permute-start | bytes 24584 | tf_op jit(solution)/shard_map/ppermute | solution.py:241
  32.9 0.0 collective-permute-done.1
  32.9 0.0 collective-permute-done.8
  32.9 0.1 add_add_fusion
  33.0 2.1 %collective-permute-start.11 = (f32[16,1152]{1,0:T(8,128)S(1)}, f32[16,1152]{1,0:T(8,128)S(1)}, u32[]{:S(2)}, u32[]{:S(2)}) collective-permute-start(f32[16,1152]{1,0:T(8,128)S(1)} %get-tuple-element.58), channel_id=1, source_target_pairs={{0,16},{1,25},{2,18},{3,27},{4,20},{5,29},{6,22},{7,31},{8,24},{9,... | collective-permute-start | bytes 221192 | tf_op jit(solution)/shard_map/ppermute | solution.py:241
  35.1 1.3 %collective-permute-start.10 = (f32[16,1152]{1,0:T(8,128)S(1)}, f32[16,1152]{1,0:T(8,128)S(1)}, u32[]{:S(2)}, u32[]{:S(2)}) collective-permute-start(f32[16,1152]{1,0:T(8,128)S(1)} %get-tuple-element.59), channel_id=1, source_target_pairs={{0,24},{1,17},{2,26},{3,19},{4,28},{5,21},{6,30},{7,23},{8,16},{9,... | collective-permute-start | bytes 221192 | tf_op jit(solution)/shard_map/ppermute | solution.py:241
  36.4 0.2 collective-permute-start.9
  36.5 0.0 collective-permute-done.15.b_ref
  36.6 1.4 %collective-permute-start.17 = (f32[8,256]{1,0:T(8,128)S(1)}, f32[8,256]{1,0:T(8,128)S(1)}, u32[]{:S(2)}, u32[]{:S(2)}) collective-permute-start(f32[8,256]{1,0:T(8,128)S(1)} %sum.1), channel_id=1, source_target_pairs={{0,2},{1,5},{2,0},{3,7},{4,6},{5,1},{6,4},{7,3},{8,10},{9,13},{10,... | collective-permute-start | bytes 24584 | tf_op jit(solution)/shard_map/ppermute | solution.py:241
  38.0 2.2 %rows.1 = (f32[64,256]{1,0:T(8,128)S(1)}, f32[64,256]{1,0:T(8,128)S(1)}) custom-call(bf16[1024,1024]{1,0:T(8,128)(2,1)S(1)} %get-tuple-element.46.high_ref, bf16[1024,1024]{1,0:T(8,128)(2,1)S(1)} %get-tuple-element.47.low_ref, bf16[256,1024]{1,0:T(8,128)(2,1)S(1)} %get-tuple-element.44.bt_high.refs_4_, ...), custom_call_target="tpu_custom_call" | custom-call | flops 536870912 | tf_op jit(solution)/shard_map/rows/pallas_call | solution.py:356
  40.2 0.1 collective-permute-start.16
  40.3 0.0 collective-permute-done.17
  40.3 2.8 %collective-permute-start.18 = (f32[8,256]{1,0:T(8,128)S(1)}, f32[8,256]{1,0:T(8,128)S(1)}, u32[]{:S(2)}, u32[]{:S(2)}) collective-permute-start(f32[8,256]{1,0:T(8,128)S(1)} %add.31.refs_8_), channel_id=1, source_target_pairs={{0,24},{1,25},{2,26},{3,27},{4,28},{5,29},{6,30},{7,31},{8,16},{9,... | collective-permute-start | bytes 24584 | tf_op jit(solution)/shard_map/ppermute | solution.py:241
  43.1 0.0 collective-permute-done.11
  43.1 0.7 %collective-permute-start.19 = (f32[8,256]{1,0:T(8,128)S(1)}, f32[8,256]{1,0:T(8,128)S(1)}, u32[]{:S(2)}, u32[]{:S(2)}) collective-permute-start(f32[8,256]{1,0:T(8,128)S(1)} %add.31.refs_8_), channel_id=1, source_target_pairs={{0,16},{1,17},{2,18},{3,19},{4,20},{5,21},{6,22},{7,23},{8,24},{9,... | collective-permute-start | bytes 24584 | tf_op jit(solution)/shard_map/ppermute | solution.py:241
  43.8 0.0 collective-permute-done.10
  43.8 1.4 %collective-permute-start.20 = (f32[8,256]{1,0:T(8,128)S(1)}, f32[8,256]{1,0:T(8,128)S(1)}, u32[]{:S(2)}, u32[]{:S(2)}) collective-permute-start(f32[8,256]{1,0:T(8,128)S(1)} %add.31.refs_8_), channel_id=1, source_target_pairs={{0,8},{1,9},{2,10},{3,11},{4,12},{5,13},{6,14},{7,15},{8,0},{9,1},... | collective-permute-start | bytes 24584 | tf_op jit(solution)/shard_map/ppermute | solution.py:241
  45.2 0.0 collective-permute-done.9
  45.2 0.1 collective-permute-start.12
  45.3 0.5 %collective-permute-done.18.refs_9_ = f32[8,256]{1,0:T(8,128)S(1)} collective-permute-done((f32[8,256]{1,0:T(8,128)S(1)}, f32[8,256]{1,0:T(8,128)S(1)}, u32[]{:S(2)}, u32[]{:S(2)}) %collective-permute-start.18) | collective-permute-done | bytes 8224 | tf_op jit(solution)/shard_map/ppermute | solution.py:241
  45.8 1.8 %collective-permute-done.19.refs_10_ = f32[8,256]{1,0:T(8,128)S(1)} collective-permute-done((f32[8,256]{1,0:T(8,128)S(1)}, f32[8,256]{1,0:T(8,128)S(1)}, u32[]{:S(2)}, u32[]{:S(2)}) %collective-permute-start.19) | collective-permute-done | bytes 8224 | tf_op jit(solution)/shard_map/ppermute | solution.py:241
  47.6 0.0 collective-permute-done.20.refs_11_
  47.6 0.0 collective-permute-done.16.refs_7_
  47.6 0.0 collective-permute-done.12.refs_1_
  47.6 1.3 %last.1 = (f32[16,1024]{1,0:T(8,128)}, f32[64,256]{1,0:T(8,128)}, f32[8,256]{1,0:T(8,128)}) custom-call(f32[16,128]{1,0:T(8,128)S(1)} %slice.8.refs_0_, f32[16,128]{1,0:T(8,128)S(1)} %collective-permute-done.12.refs_1_, f32[8,256]{1,0:T(8,128)S(1)} %get-tuple-element.40.c_ref.refs_2_, f32[16,1024]{1,0:T(8,128)S(1)} %slice.9.refs_3_, ...), custom_call_target="tpu_custom_call" | custom-call | flops 4194304 | tf_op jit(solution)/shard_map/last/pallas_call | solution.py:371
  (12 shorter events, 0.1 us)
Async XLA Ops:
  0.6 5.8 %collective-permute-start = (f32[64,256]{1,0:T(8,128)}, f32[64,256]{1,0:T(8,128)S(1)}, u32[]{:S(2)}, u32[]{:S(2)}) collective-permute-start(f32[64,256]{1,0:T(8,128)} %a_hbm.1), channel_id=1, source_target_pairs={{0,1},{1,0},{2,3},{3,2},{4,5},{5,4},{6,7},{7,6},{8,9},{9,8},{10,11... | collective-permute-start | bytes 196616 | tf_op jit(solution)/shard_map/ppermute | solution.py:248
  1.1 9.8 %collective-permute-start.3 = (f32[16,1024]{1,0:T(8,128)}, f32[16,1024]{1,0:T(8,128)S(1)}, u32[]{:S(2)}, u32[]{:S(2)}) collective-permute-start(f32[16,1024]{1,0:T(8,128)} %own_hbm.1), channel_id=1, source_target_pairs={{0,16},{1,25},{2,18},{3,27},{4,20},{5,29},{6,22},{7,31},{8,24},{9,... | collective-permute-start | bytes 196616 | tf_op jit(solution)/shard_map/ppermute | solution.py:241
  4.8 6.6 %collective-permute-start.4 = (f32[16,1024]{1,0:T(8,128)}, f32[16,1024]{1,0:T(8,128)S(1)}, u32[]{:S(2)}, u32[]{:S(2)}) collective-permute-start(f32[16,1024]{1,0:T(8,128)} %own_hbm.1), channel_id=1, source_target_pairs={{0,24},{1,17},{2,26},{3,19},{4,28},{5,21},{6,30},{7,23},{8,16},{9,... | collective-permute-start | bytes 196616 | tf_op jit(solution)/shard_map/ppermute | solution.py:241
  6.2 5.9 %collective-permute-start.5 = (f32[16,1024]{1,0:T(8,128)}, f32[16,1024]{1,0:T(8,128)S(1)}, u32[]{:S(2)}, u32[]{:S(2)}) collective-permute-start(f32[16,1024]{1,0:T(8,128)} %own_hbm.1), channel_id=1, source_target_pairs={{0,8},{1,9},{2,10},{3,11},{4,12},{5,13},{6,14},{7,15},{8,0},{9,1},... | collective-permute-start | bytes 196616 | tf_op jit(solution)/shard_map/ppermute | solution.py:241
  12.1 9.1 %collective-permute-start.6 = (f32[64,1024]{1,0:T(8,128)S(1)}, f32[64,1024]{1,0:T(8,128)S(1)}, u32[]{:S(2)}, u32[]{:S(2)}) collective-permute-start(f32[64,1024]{1,0:T(8,128)S(1)} %constant_dynamic-update-slice_fusion.refs_0_), channel_id=1, source_target_pairs={{0,2},{1,5},{2,0},{3,7},{4,6},{5,1},{6,4},{7,3},{8,10},{9,13},{10,... | collective-permute-start | bytes 786440 | tf_op jit(solution)/shard_map/ppermute | solution.py:241
  13.6 9.2 %collective-permute-start.7 = (f32[64,1024]{1,0:T(8,128)S(1)}, f32[64,1024]{1,0:T(8,128)S(1)}, u32[]{:S(2)}, u32[]{:S(2)}) collective-permute-start(f32[64,1024]{1,0:T(8,128)S(1)} %constant_dynamic-update-slice_fusion.refs_0_), channel_id=1, source_target_pairs={{0,4},{1,3},{2,6},{3,1},{4,0},{5,7},{6,2},{7,5},{8,12},{9,11},{10,... | collective-permute-start | bytes 786440 | tf_op jit(solution)/shard_map/ppermute | solution.py:241
  15.1 9.9 %collective-permute-start.2 = (f32[64,1152]{1,0:T(8,128)S(1)}, f32[64,1152]{1,0:T(8,128)S(1)}, u32[]{:S(2)}, u32[]{:S(2)}) collective-permute-start(f32[64,1152]{1,0:T(8,128)S(1)} %get-tuple-element.33), channel_id=1, source_target_pairs={{0,2},{1,5},{2,0},{3,7},{4,6},{5,1},{6,4},{7,3},{8,10},{9,13},{10,... | collective-permute-start | bytes 884744 | tf_op jit(solution)/shard_map/ppermute | solution.py:241
  15.6 17.3 %collective-permute-start.1 = (f32[64,1152]{1,0:T(8,128)S(1)}, f32[64,1152]{1,0:T(8,128)S(1)}, u32[]{:S(2)}, u32[]{:S(2)}) collective-permute-start(f32[64,1152]{1,0:T(8,128)S(1)} %get-tuple-element.31), channel_id=1, source_target_pairs={{0,2},{1,5},{2,0},{3,7},{4,6},{5,1},{6,4},{7,3},{8,10},{9,13},{10,... | collective-permute-start | bytes 884744 | tf_op jit(solution)/shard_map/ppermute | solution.py:241
  22.8 6.4 %collective-permute-start.13 = (f32[64,1024]{1,0:T(8,128)S(1)}, f32[64,1024]{1,0:T(8,128)S(1)}, u32[]{:S(2)}, u32[]{:S(2)}) collective-permute-start(f32[64,1024]{1,0:T(8,128)S(1)} %collective-permute-done.6.refs_1_), channel_id=1, source_target_pairs={{0,4},{1,3},{2,6},{3,1},{4,0},{5,7},{6,2},{7,5},{8,12},{9,11},{10,... | collective-permute-start | bytes 786440 | tf_op jit(solution)/shard_map/ppermute | solution.py:241
  25.0 7.9 %collective-permute-start.8 = (f32[64,1152]{1,0:T(8,128)S(1)}, f32[64,1152]{1,0:T(8,128)S(1)}, u32[]{:S(2)}, u32[]{:S(2)}) collective-permute-start(f32[64,1152]{1,0:T(8,128)S(1)} %add.25), channel_id=1, source_target_pairs={{0,4},{1,3},{2,6},{3,1},{4,0},{5,7},{6,2},{7,5},{8,12},{9,11},{10,... | collective-permute-start | bytes 884744 | tf_op jit(solution)/shard_map/ppermute | solution.py:241
  30.2 1.3 %collective-permute-start.14 = (f32[8,256]{1,0:T(8,128)S(1)}, f32[8,256]{1,0:T(8,128)S(1)}, u32[]{:S(2)}, u32[]{:S(2)}) collective-permute-start(f32[8,256]{1,0:T(8,128)S(1)} %get-tuple-element.50), channel_id=1, source_target_pairs={{0,1},{1,0},{2,3},{3,2},{4,5},{5,4},{6,7},{7,6},{8,9},{9,8},{10,11... | collective-permute-start | bytes 24584 | tf_op jit(solution)/shard_map/ppermute | solution.py:248
  31.5 5.1 %collective-permute-start.15 = (f32[8,256]{1,0:T(8,128)S(1)}, f32[8,256]{1,0:T(8,128)S(1)}, u32[]{:S(2)}, u32[]{:S(2)}) collective-permute-start(f32[8,256]{1,0:T(8,128)S(1)} %add.30.a_ref), channel_id=1, source_target_pairs={{0,4},{1,3},{2,6},{3,1},{4,0},{5,7},{6,2},{7,5},{8,12},{9,11},{10,... | collective-permute-start | bytes 24584 | tf_op jit(solution)/shard_map/ppermute | solution.py:241
  33.0 10.1 %collective-permute-start.11 = (f32[16,1152]{1,0:T(8,128)S(1)}, f32[16,1152]{1,0:T(8,128)S(1)}, u32[]{:S(2)}, u32[]{:S(2)}) collective-permute-start(f32[16,1152]{1,0:T(8,128)S(1)} %get-tuple-element.58), channel_id=1, source_target_pairs={{0,16},{1,25},{2,18},{3,27},{4,20},{5,29},{6,22},{7,31},{8,24},{9,... | collective-permute-start | bytes 221192 | tf_op jit(solution)/shard_map/ppermute | solution.py:241
  35.1 8.7 %collective-permute-start.10 = (f32[16,1152]{1,0:T(8,128)S(1)}, f32[16,1152]{1,0:T(8,128)S(1)}, u32[]{:S(2)}, u32[]{:S(2)}) collective-permute-start(f32[16,1152]{1,0:T(8,128)S(1)} %get-tuple-element.59), channel_id=1, source_target_pairs={{0,24},{1,17},{2,26},{3,19},{4,28},{5,21},{6,30},{7,23},{8,16},{9,... | collective-permute-start | bytes 221192 | tf_op jit(solution)/shard_map/ppermute | solution.py:241
  36.4 8.8 %collective-permute-start.9 = (f32[16,1152]{1,0:T(8,128)S(1)}, f32[16,1152]{1,0:T(8,128)S(1)}, u32[]{:S(2)}, u32[]{:S(2)}) collective-permute-start(f32[16,1152]{1,0:T(8,128)S(1)} %get-tuple-element.57), channel_id=1, source_target_pairs={{0,8},{1,9},{2,10},{3,11},{4,12},{5,13},{6,14},{7,15},{8,0},{9,1},... | collective-permute-start | bytes 221192 | tf_op jit(solution)/shard_map/ppermute | solution.py:241
  36.6 3.7 %collective-permute-start.17 = (f32[8,256]{1,0:T(8,128)S(1)}, f32[8,256]{1,0:T(8,128)S(1)}, u32[]{:S(2)}, u32[]{:S(2)}) collective-permute-start(f32[8,256]{1,0:T(8,128)S(1)} %sum.1), channel_id=1, source_target_pairs={{0,2},{1,5},{2,0},{3,7},{4,6},{5,1},{6,4},{7,3},{8,10},{9,13},{10,... | collective-permute-start | bytes 24584 | tf_op jit(solution)/shard_map/ppermute | solution.py:241
  40.2 7.4 %collective-permute-start.16 = (f32[64,256]{1,0:T(8,128)S(1)}, f32[64,256]{1,0:T(8,128)S(1)}, u32[]{:S(2)}, u32[]{:S(2)}) collective-permute-start(f32[64,256]{1,0:T(8,128)S(1)} %get-tuple-element.53), channel_id=1, source_target_pairs={{0,1},{1,0},{2,3},{3,2},{4,5},{5,4},{6,7},{7,6},{8,9},{9,8},{10,11... | collective-permute-start | bytes 196616 | tf_op jit(solution)/shard_map/ppermute | solution.py:248
  40.3 5.5 %collective-permute-start.18 = (f32[8,256]{1,0:T(8,128)S(1)}, f32[8,256]{1,0:T(8,128)S(1)}, u32[]{:S(2)}, u32[]{:S(2)}) collective-permute-start(f32[8,256]{1,0:T(8,128)S(1)} %add.31.refs_8_), channel_id=1, source_target_pairs={{0,24},{1,25},{2,26},{3,27},{4,28},{5,29},{6,30},{7,31},{8,16},{9,... | collective-permute-start | bytes 24584 | tf_op jit(solution)/shard_map/ppermute | solution.py:241
  43.1 4.6 %collective-permute-start.19 = (f32[8,256]{1,0:T(8,128)S(1)}, f32[8,256]{1,0:T(8,128)S(1)}, u32[]{:S(2)}, u32[]{:S(2)}) collective-permute-start(f32[8,256]{1,0:T(8,128)S(1)} %add.31.refs_8_), channel_id=1, source_target_pairs={{0,16},{1,17},{2,18},{3,19},{4,20},{5,21},{6,22},{7,23},{8,24},{9,... | collective-permute-start | bytes 24584 | tf_op jit(solution)/shard_map/ppermute | solution.py:241
  43.8 3.9 %collective-permute-start.20 = (f32[8,256]{1,0:T(8,128)S(1)}, f32[8,256]{1,0:T(8,128)S(1)}, u32[]{:S(2)}, u32[]{:S(2)}) collective-permute-start(f32[8,256]{1,0:T(8,128)S(1)} %add.31.refs_8_), channel_id=1, source_target_pairs={{0,8},{1,9},{2,10},{3,11},{4,12},{5,13},{6,14},{7,15},{8,0},{9,1},... | collective-permute-start | bytes 24584 | tf_op jit(solution)/shard_map/ppermute | solution.py:241
  45.2 2.4 %collective-permute-start.12 = (f32[16,128]{1,0:T(8,128)S(1)}, f32[16,128]{1,0:T(8,128)S(1)}, u32[]{:S(2)}, u32[]{:S(2)}) collective-permute-start(f32[16,128]{1,0:T(8,128)S(1)} %slice.8.refs_0_), channel_id=1, source_target_pairs={{0,1},{1,0},{2,3},{3,2},{4,5},{5,4},{6,7},{7,6},{8,9},{9,8},{10,11... | collective-permute-start | bytes 24584 | tf_op jit(solution)/shard_map/ppermute | solution.py:248

commit v5 on v4

--- a/solution.py
+++ b/solution.py
@@ -48,7 +48,7 @@
 
 
 def early_kernel(n_line, rank_rows, width, t_hbm, a_hbm, c_hbm, own_hbm, other_ref, *refs):
-    *pay, slab_ref, high_ref, low_ref, gram_ref, block_ref, c_ref, own_ref, total, t_ref, a_ref, wide, sems = refs
+    *pay, slab_ref, high_ref, low_ref, gram_ref, block_ref, c_ref, own_ref, rows_ref, total, t_ref, a_ref, wide, sems = refs
     slices, rows, cols = t_hbm.shape
     group = slices // 2
     steps = slices // group
@@ -122,6 +122,15 @@
                 scale * slab[:, at : at + lanes] for scale, slab in zip(scales, slabs)
             )
 
+    c = c_ref[...]
+    chosen = lax.axis_index("row") * rank_rows
+    pick = lax.broadcasted_iota(jnp.int32, (rank_rows, rank), 1) == (
+        chosen + lax.broadcasted_iota(jnp.int32, (rank_rows, rank), 0)
+    )
+    exact = functools.partial(
+        lax.dot_general, precision=lax.Precision.HIGHEST, preferred_element_type=F32
+    )
+    rows_ref[...] = exact(exact(pick.astype(F32), c, NT), c, NN)
     last.wait()
     if len(pay) == 1:
         pay[0][...] = total[...]
@@ -214,17 +223,7 @@
         here = lax.axis_index("col") == 0
         pieces = [jnp.where(here, *pieces), jnp.where(here, *pieces[::-1])]
     gram_rows = jnp.concatenate(pieces, axis=1)
-    c = c_ref[...]
-    chosen = lax.axis_index("row") * rank_rows
-    rank = c.shape[1]
-    pick = lax.broadcasted_iota(jnp.int32, (rank_rows, rank), 1) == (
-        chosen + lax.broadcasted_iota(jnp.int32, (rank_rows, rank), 0)
-    )
-    exact = functools.partial(
-        lax.dot_general, precision=lax.Precision.HIGHEST, preferred_element_type=F32
-    )
-    c_mine = exact(pick.astype(F32), c, NT)
-    h_rows = gram_rows * exact(c_mine, c, NN)
+    h_rows = gram_rows * c_ref[...]
     out_ref[...] = dot3(split(h_rows), (high_ref[...], low_ref[...])) - m_ref[...]
 
 
@@ -279,13 +278,13 @@
     fixed = pltpu.with_memory_space_constraint
     hbm = pl.BlockSpec(memory_space=pltpu.HBM)
     vmem = pl.BlockSpec(memory_space=pltpu.VMEM)
-    *pay, slabs, high, low, gram, block_a, c_near, own = pl.pallas_call(
+    *pay, slabs, high, low, gram, block_a, c_near, own, c_rows = pl.pallas_call(
         kernel,
         in_specs=[hbm] * 4 + [vmem] * (len(a_parts) - 1),
         out_shape=[jax.ShapeDtypeStruct((n, cols + width), F32) for n in pay_rows]
         + [jax.ShapeDtypeStruct((slices, rank, cols), F32)]
         + [jax.ShapeDtypeStruct((slices * rows, cols), BF16)] * 2
-        + [jax.ShapeDtypeStruct(x, F32) for x in ((rank, rank), (rows, rank), (slices, rank), factor_bt.shape)],
+        + [jax.ShapeDtypeStruct(x, F32) for x in ((rank, rank), (rows, rank), (slices, rank), factor_bt.shape, (rank_rows, rank))],
         scratch_shapes=[
             pltpu.VMEM((rank, cols + width), F32),
             pltpu.VMEM((slices, rows, cols), F32),
@@ -363,7 +362,7 @@
     part_c = [part_c] + [move(part_c, lambda r, c, d=d: r ^ (4 * d)) for d in reversed(range(1, n_line))]
     gram_rows = total[:, cols:]
     grams = [gram_rows, swap(gram_rows)] if width < rank else [gram_rows]
-    operands = [*grams, c_near, total[:, :cols], bt_high, bt_low]
+    operands = [*grams, c_rows, total[:, :cols], bt_high, bt_low]
     shapes = [((rank_rows, cols), F32)]
     if pair:
         operands += [keep, swap(send[0]), *part_c]

time: 49 us -> 49 us (level)
  waiting for transfers between devices: 12.8 us -> 12.2 us
  starting transfers between devices: 25.6 us -> 26.1 us
    ppermute x17, waiting for transfers between devices: 12 us -> 11.4 us  [move(): lax.ppermute(x, ('row', 'col'), [(r * n_col + c, target(r, c) * n_col + c...]
    ppermute x17, starting transfers between devices: 24.5 us -> 25 us  [move(): lax.ppermute(x, ('row', 'col'), [(r * n_col + c, target(r, c) * n_col + c...]
  transfers between devices with their start and end apart: 21 -> 21, of which waited for: 8 -> 7; matrix products, arithmetic and copies ran while one was open for 0% -> 0% of each run, Pallas kernels for 17% -> 18%
where the time goes in v5:
time: 49 us; the launch traced here: 48.9 us
  starting transfers between devices  26.1 us (53%)
  waiting for transfers between devices  12.2 us (25%)
  Pallas kernels  9.6 us (20%)
  between operations  0.76 us (2%)
    ppermute x17, starting transfers between devices, move(): lax.ppermute(x, ('row', 'col'), [(r * n_col + c, target(r, c) * n_col + c...  25 us
    ppermute x17, waiting for transfers between devices, move(): lax.ppermute(x, ('row', 'col'), [(r * n_col + c, target(r, c) * n_col + c...  11.4 us
    pallas_call x1, Pallas kernels, local(): pl.pallas_call(kernel, in_specs=[hbm] * 4 + [vmem] * (len(a_parts) - 1),...  4.8 us
    pallas_call x1, Pallas kernels, local(): call(functools.partial(rows_kernel, pair), 'rows', work, [((half, rank),...  2.21 us
    ppermute x4, starting transfers between devices, swap(): return lax.ppermute(x, 'col', [(0, 1), (1, 0)])  1.09 us
    pallas_call x1, Pallas kernels, local(): call(functools.partial(ranks_kernel, n_line, rank_rows), 'ranks', WEIGHT...  0.98 us
  transfers between devices with their start and end apart: 21, of which 7 were waited for; matrix products, arithmetic and copies ran while one was open for 0% of the time, Pallas kernels for 18%

profile of v5, /device:TPU:0, one launch (start us, length us, event | category | flops | bytes accessed | tf_op | source)
XLA Modules:
  0.0 48.9 jit_solution(17547500353524752027)
XLA Ops:
  0.6 0.5 %collective-permute-start = (f32[64,256]{1,0:T(8,128)}, f32[64,256]{1,0:T(8,128)S(1)}, u32[]{:S(2)}, u32[]{:S(2)}) collective-permute-start(f32[64,256]{1,0:T(8,128)} %a_hbm.1), channel_id=1, source_target_pairs={{0,1},{1,0},{2,3},{3,2},{4,5},{5,4},{6,7},{7,6},{8,9},{9,8},{10,11... | collective-permute-start | bytes 196616 | tf_op jit(solution)/shard_map/ppermute | solution.py:247
  1.1 3.7 %collective-permute-start.3 = (f32[16,1024]{1,0:T(8,128)}, f32[16,1024]{1,0:T(8,128)S(1)}, u32[]{:S(2)}, u32[]{:S(2)}) collective-permute-start(f32[16,1024]{1,0:T(8,128)} %own_hbm.1), channel_id=1, source_target_pairs={{0,16},{1,25},{2,18},{3,27},{4,20},{5,29},{6,22},{7,31},{8,24},{9,... | collective-permute-start | bytes 196616 | tf_op jit(solution)/shard_map/ppermute | solution.py:240
  4.8 1.3 %collective-permute-start.4 = (f32[16,1024]{1,0:T(8,128)}, f32[16,1024]{1,0:T(8,128)S(1)}, u32[]{:S(2)}, u32[]{:S(2)}) collective-permute-start(f32[16,1024]{1,0:T(8,128)} %own_hbm.1), channel_id=1, source_target_pairs={{0,24},{1,17},{2,26},{3,19},{4,28},{5,21},{6,30},{7,23},{8,16},{9,... | collective-permute-start | bytes 196616 | tf_op jit(solution)/shard_map/ppermute | solution.py:240
  6.2 0.2 collective-permute-start.5
  6.4 0.0 collective-permute-done.other_ref
  6.4 4.8 %early.1 = (f32[64,1152]{1,0:T(8,128)S(1)}, f32[64,1152]{1,0:T(8,128)S(1)}, f32[64,1152]{1,0:T(8,128)S(1)}, f32[64,1152]{1,0:T(8,128)S(1)}, f32[8,256,1024]{2,1,...) custom-call(f32[8,128,1024]{2,1,0:T(8,128)} %t_hbm.1, ...), custom_call_target="tpu_custom_call" | custom-call | flops 536870912 | tf_op jit(solution)/shard_map/early/pallas_call | solution.py:281
  11.2 0.0 collective-permute-done.3
  11.2 0.1 collective-permute-done.4
  11.4 0.7 %collective-permute-done.5 = f32[16,1024]{1,0:T(8,128)S(1)} collective-permute-done((f32[16,1024]{1,0:T(8,128)}, f32[16,1024]{1,0:T(8,128)S(1)}, u32[]{:S(2)}, u32[]{:S(2)}) %collective-permute-start.5) | collective-permute-done | bytes 65568 | tf_op jit(solution)/shard_map/ppermute | solution.py:240
  12.1 1.5 %collective-permute-start.6 = (f32[64,1024]{1,0:T(8,128)S(1)}, f32[64,1024]{1,0:T(8,128)S(1)}, u32[]{:S(2)}, u32[]{:S(2)}) collective-permute-start(f32[64,1024]{1,0:T(8,128)S(1)} %constant_dynamic-update-slice_fusion.refs_0_), channel_id=1, source_target_pairs={{0,2},{1,5},{2,0},{3,7},{4,6},{5,1},{6,4},{7,3},{8,10},{9,13},{10,... | collective-permute-start | bytes 786440 | tf_op jit(solution)/shard_map/ppermute | solution.py:240
  13.6 1.5 %collective-permute-start.7 = (f32[64,1024]{1,0:T(8,128)S(1)}, f32[64,1024]{1,0:T(8,128)S(1)}, u32[]{:S(2)}, u32[]{:S(2)}) collective-permute-start(f32[64,1024]{1,0:T(8,128)S(1)} %constant_dynamic-update-slice_fusion.refs_0_), channel_id=1, source_target_pairs={{0,4},{1,3},{2,6},{3,1},{4,0},{5,7},{6,2},{7,5},{8,12},{9,11},{10,... | collective-permute-start | bytes 786440 | tf_op jit(solution)/shard_map/ppermute | solution.py:240
  15.1 0.5 %collective-permute-start.2 = (f32[64,1152]{1,0:T(8,128)S(1)}, f32[64,1152]{1,0:T(8,128)S(1)}, u32[]{:S(2)}, u32[]{:S(2)}) collective-permute-start(f32[64,1152]{1,0:T(8,128)S(1)} %get-tuple-element.34), channel_id=1, source_target_pairs={{0,2},{1,5},{2,0},{3,7},{4,6},{5,1},{6,4},{7,3},{8,10},{9,13},{10,... | collective-permute-start | bytes 884744 | tf_op jit(solution)/shard_map/ppermute | solution.py:240
  15.6 1.5 %collective-permute-start.1 = (f32[64,1152]{1,0:T(8,128)S(1)}, f32[64,1152]{1,0:T(8,128)S(1)}, u32[]{:S(2)}, u32[]{:S(2)}) collective-permute-start(f32[64,1152]{1,0:T(8,128)S(1)} %get-tuple-element.32), channel_id=1, source_target_pairs={{0,2},{1,5},{2,0},{3,7},{4,6},{5,1},{6,4},{7,3},{8,10},{9,13},{10,... | collective-permute-start | bytes 884744 | tf_op jit(solution)/shard_map/ppermute | solution.py:240
  17.1 4.1 %collective-permute-done.6.refs_1_ = f32[64,1024]{1,0:T(8,128)S(1)} collective-permute-done((f32[64,1024]{1,0:T(8,128)S(1)}, f32[64,1024]{1,0:T(8,128)S(1)}, u32[]{:S(2)}, u32[]{:S(2)}) %collective-permute-start.6) | collective-permute-done | bytes 262176 | tf_op jit(solution)/shard_map/ppermute | solution.py:240
  21.2 1.6 %collective-permute-done.7.refs_2_ = f32[64,1024]{1,0:T(8,128)S(1)} collective-permute-done((f32[64,1024]{1,0:T(8,128)S(1)}, f32[64,1024]{1,0:T(8,128)S(1)}, u32[]{:S(2)}, u32[]{:S(2)}) %collective-permute-start.7) | collective-permute-done | bytes 262176 | tf_op jit(solution)/shard_map/ppermute | solution.py:240
  22.8 1.5 %collective-permute-start.13 = (f32[64,1024]{1,0:T(8,128)S(1)}, f32[64,1024]{1,0:T(8,128)S(1)}, u32[]{:S(2)}, u32[]{:S(2)}) collective-permute-start(f32[64,1024]{1,0:T(8,128)S(1)} %collective-permute-done.6.refs_1_), channel_id=1, source_target_pairs={{0,4},{1,3},{2,6},{3,1},{4,0},{5,7},{6,2},{7,5},{8,12},{9,11},{10,... | collective-permute-start | bytes 786440 | tf_op jit(solution)/shard_map/ppermute | solution.py:240
  24.4 0.6 %near.1 = (bf16[256,1024]{1,0:T(8,128)(2,1)S(1)}, bf16[256,1024]{1,0:T(8,128)(2,1)S(1)}, f32[256,8]{1,0:T(8,128)S(1)}) custom-call(f32[8,256,1024]{2,1,0:T(8,128)S(1)} %get-tuple-element.35.slab_ref, f32[64,1024]{1,0:T(8,128)S(1)} %constant_dynamic-update-slice_fusion.refs_0_, f32[64,1024]{1,0:T(8,128)S(1)} %collective-permute-done.6.refs_1_, ...), custom_call_target="tpu_custom_call" | custom-call | flops 13421772800 | tf_op jit(solution)/shard_map/near/pallas_call | solution.py:319
  25.0 0.0 collective-permute-done.2
  25.0 1.4 %collective-permute-start.8 = (f32[64,1152]{1,0:T(8,128)S(1)}, f32[64,1152]{1,0:T(8,128)S(1)}, u32[]{:S(2)}, u32[]{:S(2)}) collective-permute-start(f32[64,1152]{1,0:T(8,128)S(1)} %add.25), channel_id=1, source_target_pairs={{0,4},{1,3},{2,6},{3,1},{4,0},{5,7},{6,2},{7,5},{8,12},{9,11},{10,... | collective-permute-start | bytes 884744 | tf_op jit(solution)/shard_map/ppermute | solution.py:240
  26.4 2.8 %collective-permute-done.13.buf_ref = f32[64,1024]{1,0:T(8,128)S(1)} collective-permute-done((f32[64,1024]{1,0:T(8,128)S(1)}, f32[64,1024]{1,0:T(8,128)S(1)}, u32[]{:S(2)}, u32[]{:S(2)}) %collective-permute-start.13) | collective-permute-done | bytes 262176 | tf_op jit(solution)/shard_map/ppermute | solution.py:240
  29.2 1.0 %ranks.1 = (bf16[256,1024]{1,0:T(8,128)(2,1)S(1)}, bf16[256,1024]{1,0:T(8,128)(2,1)S(1)}, f32[256,256]{1,0:T(8,128)S(1)}, f32[8,256]{1,0:T(8,128)S(1)}) custom-call(f32[8,256,1024]{2,1,0:T(8,128)S(1)} %get-tuple-element.35.slab_ref, f32[8,256]{1,0:T(8,128)S(1)} %get-tuple-element.42.c_ref, f32[256,256]{1,0:T(8,128)S(1)} %get-tuple-element.43.gram_ref, ...), custom_call_target="tpu_custom_call" | custom-call | flops 13421772800 | tf_op jit(solution)/shard_map/ranks/pallas_call | solution.py:332
  30.2 0.4 collective-permute-start.14
  30.7 0.8 %collective-permute-done.14 = f32[8,256]{1,0:T(8,128)S(1)} collective-permute-done((f32[8,256]{1,0:T(8,128)S(1)}, f32[8,256]{1,0:T(8,128)S(1)}, u32[]{:S(2)}, u32[]{:S(2)}) %collective-permute-start.14) | collective-permute-done | bytes 8224 | tf_op jit(solution)/shard_map/ppermute | solution.py:247
  31.5 1.4 %collective-permute-start.15 = (f32[8,256]{1,0:T(8,128)S(1)}, f32[8,256]{1,0:T(8,128)S(1)}, u32[]{:S(2)}, u32[]{:S(2)}) collective-permute-start(f32[8,256]{1,0:T(8,128)S(1)} %add.30.a_ref), channel_id=1, source_target_pairs={{0,4},{1,3},{2,6},{3,1},{4,0},{5,7},{6,2},{7,5},{8,12},{9,11},{10,... | collective-permute-start | bytes 24584 | tf_op jit(solution)/shard_map/ppermute | solution.py:240
  32.9 0.0 collective-permute-done.1
  32.9 0.0 collective-permute-done.8
  32.9 0.1 add_add_fusion
  33.0 2.1 %collective-permute-start.11 = (f32[16,1152]{1,0:T(8,128)S(1)}, f32[16,1152]{1,0:T(8,128)S(1)}, u32[]{:S(2)}, u32[]{:S(2)}) collective-permute-start(f32[16,1152]{1,0:T(8,128)S(1)} %get-tuple-element.60), channel_id=1, source_target_pairs={{0,16},{1,25},{2,18},{3,27},{4,20},{5,29},{6,22},{7,31},{8,24},{9,... | collective-permute-start | bytes 221192 | tf_op jit(solution)/shard_map/ppermute | solution.py:240
  35.1 1.3 %collective-permute-start.10 = (f32[16,1152]{1,0:T(8,128)S(1)}, f32[16,1152]{1,0:T(8,128)S(1)}, u32[]{:S(2)}, u32[]{:S(2)}) collective-permute-start(f32[16,1152]{1,0:T(8,128)S(1)} %get-tuple-element.61), channel_id=1, source_target_pairs={{0,24},{1,17},{2,26},{3,19},{4,28},{5,21},{6,30},{7,23},{8,16},{9,... | collective-permute-start | bytes 221192 | tf_op jit(solution)/shard_map/ppermute | solution.py:240
  36.5 0.1 collective-permute-start.9
  36.5 0.0 collective-permute-done.15.b_ref
  36.6 1.5 %collective-permute-start.17 = (f32[8,256]{1,0:T(8,128)S(1)}, f32[8,256]{1,0:T(8,128)S(1)}, u32[]{:S(2)}, u32[]{:S(2)}) collective-permute-start(f32[8,256]{1,0:T(8,128)S(1)} %sum.1), channel_id=1, source_target_pairs={{0,2},{1,5},{2,0},{3,7},{4,6},{5,1},{6,4},{7,3},{8,10},{9,13},{10,... | collective-permute-start | bytes 24584 | tf_op jit(solution)/shard_map/ppermute | solution.py:240
  38.0 2.2 %rows.1 = (f32[64,256]{1,0:T(8,128)S(1)}, f32[64,256]{1,0:T(8,128)S(1)}) custom-call(bf16[1024,1024]{1,0:T(8,128)(2,1)S(1)} %get-tuple-element.48.high_ref, bf16[1024,1024]{1,0:T(8,128)(2,1)S(1)} %get-tuple-element.49.low_ref, bf16[256,1024]{1,0:T(8,128)(2,1)S(1)} %get-tuple-element.46.bt_high.refs_4_, ...), custom_call_target="tpu_custom_call" | custom-call | flops 536870912 | tf_op jit(solution)/shard_map/rows/pallas_call | solution.py:355
  40.3 0.1 collective-permute-start.16
  40.3 0.0 collective-permute-done.17
  40.4 3.0 %collective-permute-start.18 = (f32[8,256]{1,0:T(8,128)S(1)}, f32[8,256]{1,0:T(8,128)S(1)}, u32[]{:S(2)}, u32[]{:S(2)}) collective-permute-start(f32[8,256]{1,0:T(8,128)S(1)} %add.31.refs_8_), channel_id=1, source_target_pairs={{0,24},{1,25},{2,26},{3,27},{4,28},{5,29},{6,30},{7,31},{8,16},{9,... | collective-permute-start | bytes 24584 | tf_op jit(solution)/shard_map/ppermute | solution.py:240
  43.3 0.0 collective-permute-done.11
  43.3 0.4 collective-permute-start.19
  43.8 0.0 collective-permute-done.10
  43.8 1.9 %collective-permute-start.20 = (f32[8,256]{1,0:T(8,128)S(1)}, f32[8,256]{1,0:T(8,128)S(1)}, u32[]{:S(2)}, u32[]{:S(2)}) collective-permute-start(f32[8,256]{1,0:T(8,128)S(1)} %add.31.refs_8_), channel_id=1, source_target_pairs={{0,8},{1,9},{2,10},{3,11},{4,12},{5,13},{6,14},{7,15},{8,0},{9,1},... | collective-permute-start | bytes 24584 | tf_op jit(solution)/shard_map/ppermute | solution.py:240
  45.7 0.0 collective-permute-done.9
  45.8 0.1 collective-permute-start.12
  45.8 0.0 collective-permute-done.18.refs_9_
  45.9 2.0 %collective-permute-done.19.refs_10_ = f32[8,256]{1,0:T(8,128)S(1)} collective-permute-done((f32[8,256]{1,0:T(8,128)S(1)}, f32[8,256]{1,0:T(8,128)S(1)}, u32[]{:S(2)}, u32[]{:S(2)}) %collective-permute-start.19) | collective-permute-done | bytes 8224 | tf_op jit(solution)/shard_map/ppermute | solution.py:240
  47.9 0.0 collective-permute-done.20.refs_11_
  47.9 0.0 collective-permute-done.16.refs_7_
  47.9 0.0 collective-permute-done.12.refs_1_
  47.9 1.0 %last.1 = (f32[16,1024]{1,0:T(8,128)}, f32[64,256]{1,0:T(8,128)}, f32[8,256]{1,0:T(8,128)}) custom-call(f32[16,128]{1,0:T(8,128)S(1)} %slice.8.refs_0_, f32[16,128]{1,0:T(8,128)S(1)} %collective-permute-done.12.refs_1_, f32[16,256]{1,0:T(8,128)S(1)} %get-tuple-element.41.refs_2_, f32[16,1024]{1,0:T(8,128)S(1)} %slice.9.refs_3_, ...), custom_call_target="tpu_custom_call" | custom-call | flops 4194304 | tf_op jit(solution)/shard_map/last/pallas_call | solution.py:370
  (12 shorter events, 0.1 us)
Async XLA Ops:
  0.6 5.8 %collective-permute-start = (f32[64,256]{1,0:T(8,128)}, f32[64,256]{1,0:T(8,128)S(1)}, u32[]{:S(2)}, u32[]{:S(2)}) collective-permute-start(f32[64,256]{1,0:T(8,128)} %a_hbm.1), channel_id=1, source_target_pairs={{0,1},{1,0},{2,3},{3,2},{4,5},{5,4},{6,7},{7,6},{8,9},{9,8},{10,11... | collective-permute-start | bytes 196616 | tf_op jit(solution)/shard_map/ppermute | solution.py:247
  1.1 10.1 %collective-permute-start.3 = (f32[16,1024]{1,0:T(8,128)}, f32[16,1024]{1,0:T(8,128)S(1)}, u32[]{:S(2)}, u32[]{:S(2)}) collective-permute-start(f32[16,1024]{1,0:T(8,128)} %own_hbm.1), channel_id=1, source_target_pairs={{0,16},{1,25},{2,18},{3,27},{4,20},{5,29},{6,22},{7,31},{8,24},{9,... | collective-permute-start | bytes 196616 | tf_op jit(solution)/shard_map/ppermute | solution.py:240
  4.8 6.6 %collective-permute-start.4 = (f32[16,1024]{1,0:T(8,128)}, f32[16,1024]{1,0:T(8,128)S(1)}, u32[]{:S(2)}, u32[]{:S(2)}) collective-permute-start(f32[16,1024]{1,0:T(8,128)} %own_hbm.1), channel_id=1, source_target_pairs={{0,24},{1,17},{2,26},{3,19},{4,28},{5,21},{6,30},{7,23},{8,16},{9,... | collective-permute-start | bytes 196616 | tf_op jit(solution)/shard_map/ppermute | solution.py:240
  6.2 5.9 %collective-permute-start.5 = (f32[16,1024]{1,0:T(8,128)}, f32[16,1024]{1,0:T(8,128)S(1)}, u32[]{:S(2)}, u32[]{:S(2)}) collective-permute-start(f32[16,1024]{1,0:T(8,128)} %own_hbm.1), channel_id=1, source_target_pairs={{0,8},{1,9},{2,10},{3,11},{4,12},{5,13},{6,14},{7,15},{8,0},{9,1},... | collective-permute-start | bytes 196616 | tf_op jit(solution)/shard_map/ppermute | solution.py:240
  12.1 9.1 %collective-permute-start.6 = (f32[64,1024]{1,0:T(8,128)S(1)}, f32[64,1024]{1,0:T(8,128)S(1)}, u32[]{:S(2)}, u32[]{:S(2)}) collective-permute-start(f32[64,1024]{1,0:T(8,128)S(1)} %constant_dynamic-update-slice_fusion.refs_0_), channel_id=1, source_target_pairs={{0,2},{1,5},{2,0},{3,7},{4,6},{5,1},{6,4},{7,3},{8,10},{9,13},{10,... | collective-permute-start | bytes 786440 | tf_op jit(solution)/shard_map/ppermute | solution.py:240
  13.6 9.2 %collective-permute-start.7 = (f32[64,1024]{1,0:T(8,128)S(1)}, f32[64,1024]{1,0:T(8,128)S(1)}, u32[]{:S(2)}, u32[]{:S(2)}) collective-permute-start(f32[64,1024]{1,0:T(8,128)S(1)} %constant_dynamic-update-slice_fusion.refs_0_), channel_id=1, source_target_pairs={{0,4},{1,3},{2,6},{3,1},{4,0},{5,7},{6,2},{7,5},{8,12},{9,11},{10,... | collective-permute-start | bytes 786440 | tf_op jit(solution)/shard_map/ppermute | solution.py:240
  15.1 9.9 %collective-permute-start.2 = (f32[64,1152]{1,0:T(8,128)S(1)}, f32[64,1152]{1,0:T(8,128)S(1)}, u32[]{:S(2)}, u32[]{:S(2)}) collective-permute-start(f32[64,1152]{1,0:T(8,128)S(1)} %get-tuple-element.34), channel_id=1, source_target_pairs={{0,2},{1,5},{2,0},{3,7},{4,6},{5,1},{6,4},{7,3},{8,10},{9,13},{10,... | collective-permute-start | bytes 884744 | tf_op jit(solution)/shard_map/ppermute | solution.py:240
  15.6 17.3 %collective-permute-start.1 = (f32[64,1152]{1,0:T(8,128)S(1)}, f32[64,1152]{1,0:T(8,128)S(1)}, u32[]{:S(2)}, u32[]{:S(2)}) collective-permute-start(f32[64,1152]{1,0:T(8,128)S(1)} %get-tuple-element.32), channel_id=1, source_target_pairs={{0,2},{1,5},{2,0},{3,7},{4,6},{5,1},{6,4},{7,3},{8,10},{9,13},{10,... | collective-permute-start | bytes 884744 | tf_op jit(solution)/shard_map/ppermute | solution.py:240
  22.8 6.4 %collective-permute-start.13 = (f32[64,1024]{1,0:T(8,128)S(1)}, f32[64,1024]{1,0:T(8,128)S(1)}, u32[]{:S(2)}, u32[]{:S(2)}) collective-permute-start(f32[64,1024]{1,0:T(8,128)S(1)} %collective-permute-done.6.refs_1_), channel_id=1, source_target_pairs={{0,4},{1,3},{2,6},{3,1},{4,0},{5,7},{6,2},{7,5},{8,12},{9,11},{10,... | collective-permute-start | bytes 786440 | tf_op jit(solution)/shard_map/ppermute | solution.py:240
  25.0 7.9 %collective-permute-start.8 = (f32[64,1152]{1,0:T(8,128)S(1)}, f32[64,1152]{1,0:T(8,128)S(1)}, u32[]{:S(2)}, u32[]{:S(2)}) collective-permute-start(f32[64,1152]{1,0:T(8,128)S(1)} %add.25), channel_id=1, source_target_pairs={{0,4},{1,3},{2,6},{3,1},{4,0},{5,7},{6,2},{7,5},{8,12},{9,11},{10,... | collective-permute-start | bytes 884744 | tf_op jit(solution)/shard_map/ppermute | solution.py:240
  30.2 1.3 %collective-permute-start.14 = (f32[8,256]{1,0:T(8,128)S(1)}, f32[8,256]{1,0:T(8,128)S(1)}, u32[]{:S(2)}, u32[]{:S(2)}) collective-permute-start(f32[8,256]{1,0:T(8,128)S(1)} %get-tuple-element.52), channel_id=1, source_target_pairs={{0,1},{1,0},{2,3},{3,2},{4,5},{5,4},{6,7},{7,6},{8,9},{9,8},{10,11... | collective-permute-start | bytes 24584 | tf_op jit(solution)/shard_map/ppermute | solution.py:247
  31.5 5.1 %collective-permute-start.15 = (f32[8,256]{1,0:T(8,128)S(1)}, f32[8,256]{1,0:T(8,128)S(1)}, u32[]{:S(2)}, u32[]{:S(2)}) collective-permute-start(f32[8,256]{1,0:T(8,128)S(1)} %add.30.a_ref), channel_id=1, source_target_pairs={{0,4},{1,3},{2,6},{3,1},{4,0},{5,7},{6,2},{7,5},{8,12},{9,11},{10,... | collective-permute-start | bytes 24584 | tf_op jit(solution)/shard_map/ppermute | solution.py:240
  33.0 10.3 %collective-permute-start.11 = (f32[16,1152]{1,0:T(8,128)S(1)}, f32[16,1152]{1,0:T(8,128)S(1)}, u32[]{:S(2)}, u32[]{:S(2)}) collective-permute-start(f32[16,1152]{1,0:T(8,128)S(1)} %get-tuple-element.60), channel_id=1, source_target_pairs={{0,16},{1,25},{2,18},{3,27},{4,20},{5,29},{6,22},{7,31},{8,24},{9,... | collective-permute-start | bytes 221192 | tf_op jit(solution)/shard_map/ppermute | solution.py:240
  35.1 8.6 %collective-permute-start.10 = (f32[16,1152]{1,0:T(8,128)S(1)}, f32[16,1152]{1,0:T(8,128)S(1)}, u32[]{:S(2)}, u32[]{:S(2)}) collective-permute-start(f32[16,1152]{1,0:T(8,128)S(1)} %get-tuple-element.61), channel_id=1, source_target_pairs={{0,24},{1,17},{2,26},{3,19},{4,28},{5,21},{6,30},{7,23},{8,16},{9,... | collective-permute-start | bytes 221192 | tf_op jit(solution)/shard_map/ppermute | solution.py:240
  36.5 9.2 %collective-permute-start.9 = (f32[16,1152]{1,0:T(8,128)S(1)}, f32[16,1152]{1,0:T(8,128)S(1)}, u32[]{:S(2)}, u32[]{:S(2)}) collective-permute-start(f32[16,1152]{1,0:T(8,128)S(1)} %get-tuple-element.59), channel_id=1, source_target_pairs={{0,8},{1,9},{2,10},{3,11},{4,12},{5,13},{6,14},{7,15},{8,0},{9,1},... | collective-permute-start | bytes 221192 | tf_op jit(solution)/shard_map/ppermute | solution.py:240
  36.6 3.8 %collective-permute-start.17 = (f32[8,256]{1,0:T(8,128)S(1)}, f32[8,256]{1,0:T(8,128)S(1)}, u32[]{:S(2)}, u32[]{:S(2)}) collective-permute-start(f32[8,256]{1,0:T(8,128)S(1)} %sum.1), channel_id=1, source_target_pairs={{0,2},{1,5},{2,0},{3,7},{4,6},{5,1},{6,4},{7,3},{8,10},{9,13},{10,... | collective-permute-start | bytes 24584 | tf_op jit(solution)/shard_map/ppermute | solution.py:240
  40.3 7.6 %collective-permute-start.16 = (f32[64,256]{1,0:T(8,128)S(1)}, f32[64,256]{1,0:T(8,128)S(1)}, u32[]{:S(2)}, u32[]{:S(2)}) collective-permute-start(f32[64,256]{1,0:T(8,128)S(1)} %get-tuple-element.55), channel_id=1, source_target_pairs={{0,1},{1,0},{2,3},{3,2},{4,5},{5,4},{6,7},{7,6},{8,9},{9,8},{10,11... | collective-permute-start | bytes 196616 | tf_op jit(solution)/shard_map/ppermute | solution.py:247
  40.4 5.5 %collective-permute-start.18 = (f32[8,256]{1,0:T(8,128)S(1)}, f32[8,256]{1,0:T(8,128)S(1)}, u32[]{:S(2)}, u32[]{:S(2)}) collective-permute-start(f32[8,256]{1,0:T(8,128)S(1)} %add.31.refs_8_), channel_id=1, source_target_pairs={{0,24},{1,25},{2,26},{3,27},{4,28},{5,29},{6,30},{7,31},{8,16},{9,... | collective-permute-start | bytes 24584 | tf_op jit(solution)/shard_map/ppermute | solution.py:240
  43.3 4.6 %collective-permute-start.19 = (f32[8,256]{1,0:T(8,128)S(1)}, f32[8,256]{1,0:T(8,128)S(1)}, u32[]{:S(2)}, u32[]{:S(2)}) collective-permute-start(f32[8,256]{1,0:T(8,128)S(1)} %add.31.refs_8_), channel_id=1, source_target_pairs={{0,16},{1,17},{2,18},{3,19},{4,20},{5,21},{6,22},{7,23},{8,24},{9,... | collective-permute-start | bytes 24584 | tf_op jit(solution)/shard_map/ppermute | solution.py:240
  43.8 4.1 %collective-permute-start.20 = (f32[8,256]{1,0:T(8,128)S(1)}, f32[8,256]{1,0:T(8,128)S(1)}, u32[]{:S(2)}, u32[]{:S(2)}) collective-permute-start(f32[8,256]{1,0:T(8,128)S(1)} %add.31.refs_8_), channel_id=1, source_target_pairs={{0,8},{1,9},{2,10},{3,11},{4,12},{5,13},{6,14},{7,15},{8,0},{9,1},... | collective-permute-start | bytes 24584 | tf_op jit(solution)/shard_map/ppermute | solution.py:240
  45.8 2.1 %collective-permute-start.12 = (f32[16,128]{1,0:T(8,128)S(1)}, f32[16,128]{1,0:T(8,128)S(1)}, u32[]{:S(2)}, u32[]{:S(2)}) collective-permute-start(f32[16,128]{1,0:T(8,128)S(1)} %slice.8.refs_0_), channel_id=1, source_target_pairs={{0,1},{1,0},{2,3},{3,2},{4,5},{5,4},{6,7},{7,6},{8,9},{9,8},{10,11... | collective-permute-start | bytes 24584 | tf_op jit(solution)/shard_map/ppermute | solution.py:247

commit v6 on v4

--- a/solution.py
+++ b/solution.py
@@ -267,7 +267,7 @@
     else:
         a_parts = [lax.all_gather(factor_a, "col", axis=0, tiled=True)]
     apart = [lambda r, c, d=d: r ^ (4 * distance(d, n_line, c % 2)) for d in range(n_line)]
-    got = [move(factor_bt, apart[d]) for d in range(1, n_line)]
+    got = [move(factor_bt, apart[d]) for d in reversed(range(1, n_line))][::-1]
 
     work = 2 * slices * rows * cols * rank
     pay_rows = [line_rows] * 4 if inside else [rank]

time: 49 us -> 49 us (level)
  no operation moved by 1% of the time
where the time goes in v6:
time: 49 us; the launch traced here: 48.9 us
  starting transfers between devices  25.6 us (52%)
  waiting for transfers between devices  12.8 us (26%)
  Pallas kernels  9.57 us (20%)
  between operations  0.76 us (2%)
    ppermute x17, starting transfers between devices, move(): lax.ppermute(x, ('row', 'col'), [(r * n_col + c, target(r, c) * n_col + c...  24.5 us
    ppermute x17, waiting for transfers between devices, move(): lax.ppermute(x, ('row', 'col'), [(r * n_col + c, target(r, c) * n_col + c...  12 us
    pallas_call x1, Pallas kernels, local(): pl.pallas_call(kernel, in_specs=[hbm] * 4 + [vmem] * (len(a_parts) - 1),...  4.48 us
    pallas_call x1, Pallas kernels, local(): call(functools.partial(rows_kernel, pair), 'rows', work, [((half, rank),...  2.2 us
    pallas_call x1, Pallas kernels, local(): call(functools.partial(last_kernel, pair, len(grams) - 1), 'last', rank_r...  1.26 us
    ppermute x4, starting transfers between devices, swap(): return lax.ppermute(x, 'col', [(0, 1), (1, 0)])  1.09 us
    pallas_call x1, Pallas kernels, local(): call(functools.partial(ranks_kernel, n_line, rank_rows), 'ranks', WEIGHT...  0.98 us
  transfers between devices with their start and end apart: 21, of which 8 were waited for; matrix products, arithmetic and copies ran while one was open for 0% of the time, Pallas kernels for 17%

profile of v6, /device:TPU:0, one launch (start us, length us, event | category | flops | bytes accessed | tf_op | source)
XLA Modules:
  0.0 48.9 jit_solution(14670948102602372888)
XLA Ops:
  0.6 0.5 %collective-permute-start = (f32[64,256]{1,0:T(8,128)}, f32[64,256]{1,0:T(8,128)S(1)}, u32[]{:S(2)}, u32[]{:S(2)}) collective-permute-start(f32[64,256]{1,0:T(8,128)} %a_hbm.1), channel_id=1, source_target_pairs={{0,1},{1,0},{2,3},{3,2},{4,5},{5,4},{6,7},{7,6},{8,9},{9,8},{10,11... | collective-permute-start | bytes 196616 | tf_op jit(solution)/shard_map/ppermute | solution.py:248
  1.1 3.7 %collective-permute-start.3 = (f32[16,1024]{1,0:T(8,128)}, f32[16,1024]{1,0:T(8,128)S(1)}, u32[]{:S(2)}, u32[]{:S(2)}) collective-permute-start(f32[16,1024]{1,0:T(8,128)} %own_hbm.1), channel_id=1, source_target_pairs={{0,16},{1,25},{2,18},{3,27},{4,20},{5,29},{6,22},{7,31},{8,24},{9,... | collective-permute-start | bytes 196616 | tf_op jit(solution)/shard_map/ppermute | solution.py:241
  4.8 1.3 %collective-permute-start.4 = (f32[16,1024]{1,0:T(8,128)}, f32[16,1024]{1,0:T(8,128)S(1)}, u32[]{:S(2)}, u32[]{:S(2)}) collective-permute-start(f32[16,1024]{1,0:T(8,128)} %own_hbm.1), channel_id=1, source_target_pairs={{0,24},{1,17},{2,26},{3,19},{4,28},{5,21},{6,30},{7,23},{8,16},{9,... | collective-permute-start | bytes 196616 | tf_op jit(solution)/shard_map/ppermute | solution.py:241
  6.2 0.2 collective-permute-start.5
  6.4 0.0 collective-permute-done.other_ref
  6.4 4.5 %early.1 = (f32[64,1152]{1,0:T(8,128)S(1)}, f32[64,1152]{1,0:T(8,128)S(1)}, f32[64,1152]{1,0:T(8,128)S(1)}, f32[64,1152]{1,0:T(8,128)S(1)}, f32[8,256,1024]{2,1,...) custom-call(f32[8,128,1024]{2,1,0:T(8,128)} %t_hbm.1, ...), custom_call_target="tpu_custom_call" | custom-call | flops 536870912 | tf_op jit(solution)/shard_map/early/pallas_call | solution.py:282
  10.9 0.0 collective-permute-done.3
  10.9 0.5 collective-permute-done.4
  11.4 0.7 %collective-permute-done.5 = f32[16,1024]{1,0:T(8,128)S(1)} collective-permute-done((f32[16,1024]{1,0:T(8,128)}, f32[16,1024]{1,0:T(8,128)S(1)}, u32[]{:S(2)}, u32[]{:S(2)}) %collective-permute-start.5) | collective-permute-done | bytes 65568 | tf_op jit(solution)/shard_map/ppermute | solution.py:241
  12.1 1.5 %collective-permute-start.6 = (f32[64,1024]{1,0:T(8,128)S(1)}, f32[64,1024]{1,0:T(8,128)S(1)}, u32[]{:S(2)}, u32[]{:S(2)}) collective-permute-start(f32[64,1024]{1,0:T(8,128)S(1)} %constant_dynamic-update-slice_fusion.refs_0_), channel_id=1, source_target_pairs={{0,2},{1,5},{2,0},{3,7},{4,6},{5,1},{6,4},{7,3},{8,10},{9,13},{10,... | collective-permute-start | bytes 786440 | tf_op jit(solution)/shard_map/ppermute | solution.py:241
  13.6 1.5 %collective-permute-start.7 = (f32[64,1024]{1,0:T(8,128)S(1)}, f32[64,1024]{1,0:T(8,128)S(1)}, u32[]{:S(2)}, u32[]{:S(2)}) collective-permute-start(f32[64,1024]{1,0:T(8,128)S(1)} %constant_dynamic-update-slice_fusion.refs_0_), channel_id=1, source_target_pairs={{0,4},{1,3},{2,6},{3,1},{4,0},{5,7},{6,2},{7,5},{8,12},{9,11},{10,... | collective-permute-start | bytes 786440 | tf_op jit(solution)/shard_map/ppermute | solution.py:241
  15.1 0.5 %collective-permute-start.2 = (f32[64,1152]{1,0:T(8,128)S(1)}, f32[64,1152]{1,0:T(8,128)S(1)}, u32[]{:S(2)}, u32[]{:S(2)}) collective-permute-start(f32[64,1152]{1,0:T(8,128)S(1)} %get-tuple-element.33), channel_id=1, source_target_pairs={{0,2},{1,5},{2,0},{3,7},{4,6},{5,1},{6,4},{7,3},{8,10},{9,13},{10,... | collective-permute-start | bytes 884744 | tf_op jit(solution)/shard_map/ppermute | solution.py:241
  15.6 1.5 %collective-permute-start.1 = (f32[64,1152]{1,0:T(8,128)S(1)}, f32[64,1152]{1,0:T(8,128)S(1)}, u32[]{:S(2)}, u32[]{:S(2)}) collective-permute-start(f32[64,1152]{1,0:T(8,128)S(1)} %get-tuple-element.31), channel_id=1, source_target_pairs={{0,2},{1,5},{2,0},{3,7},{4,6},{5,1},{6,4},{7,3},{8,10},{9,13},{10,... | collective-permute-start | bytes 884744 | tf_op jit(solution)/shard_map/ppermute | solution.py:241
  17.1 4.1 %collective-permute-done.6.refs_1_ = f32[64,1024]{1,0:T(8,128)S(1)} collective-permute-done((f32[64,1024]{1,0:T(8,128)S(1)}, f32[64,1024]{1,0:T(8,128)S(1)}, u32[]{:S(2)}, u32[]{:S(2)}) %collective-permute-start.6) | collective-permute-done | bytes 262176 | tf_op jit(solution)/shard_map/ppermute | solution.py:241
  21.2 1.6 %collective-permute-done.7.refs_2_ = f32[64,1024]{1,0:T(8,128)S(1)} collective-permute-done((f32[64,1024]{1,0:T(8,128)S(1)}, f32[64,1024]{1,0:T(8,128)S(1)}, u32[]{:S(2)}, u32[]{:S(2)}) %collective-permute-start.7) | collective-permute-done | bytes 262176 | tf_op jit(solution)/shard_map/ppermute | solution.py:241
  22.8 1.5 %collective-permute-start.13 = (f32[64,1024]{1,0:T(8,128)S(1)}, f32[64,1024]{1,0:T(8,128)S(1)}, u32[]{:S(2)}, u32[]{:S(2)}) collective-permute-start(f32[64,1024]{1,0:T(8,128)S(1)} %collective-permute-done.6.refs_1_), channel_id=1, source_target_pairs={{0,4},{1,3},{2,6},{3,1},{4,0},{5,7},{6,2},{7,5},{8,12},{9,11},{10,... | collective-permute-start | bytes 786440 | tf_op jit(solution)/shard_map/ppermute | solution.py:241
  24.4 0.6 %near.1 = (bf16[256,1024]{1,0:T(8,128)(2,1)S(1)}, bf16[256,1024]{1,0:T(8,128)(2,1)S(1)}, f32[256,8]{1,0:T(8,128)S(1)}) custom-call(f32[8,256,1024]{2,1,0:T(8,128)S(1)} %get-tuple-element.34.slab_ref, f32[64,1024]{1,0:T(8,128)S(1)} %constant_dynamic-update-slice_fusion.refs_0_, f32[64,1024]{1,0:T(8,128)S(1)} %collective-permute-done.6.refs_1_, ...), custom_call_target="tpu_custom_call" | custom-call | flops 13421772800 | tf_op jit(solution)/shard_map/near/pallas_call | solution.py:320
  25.0 0.0 collective-permute-done.2
  25.0 1.4 %collective-permute-start.8 = (f32[64,1152]{1,0:T(8,128)S(1)}, f32[64,1152]{1,0:T(8,128)S(1)}, u32[]{:S(2)}, u32[]{:S(2)}) collective-permute-start(f32[64,1152]{1,0:T(8,128)S(1)} %add.25), channel_id=1, source_target_pairs={{0,4},{1,3},{2,6},{3,1},{4,0},{5,7},{6,2},{7,5},{8,12},{9,11},{10,... | collective-permute-start | bytes 884744 | tf_op jit(solution)/shard_map/ppermute | solution.py:241
  26.4 2.8 %collective-permute-done.13.buf_ref = f32[64,1024]{1,0:T(8,128)S(1)} collective-permute-done((f32[64,1024]{1,0:T(8,128)S(1)}, f32[64,1024]{1,0:T(8,128)S(1)}, u32[]{:S(2)}, u32[]{:S(2)}) %collective-permute-start.13) | collective-permute-done | bytes 262176 | tf_op jit(solution)/shard_map/ppermute | solution.py:241
  29.2 1.0 %ranks.1 = (bf16[256,1024]{1,0:T(8,128)(2,1)S(1)}, bf16[256,1024]{1,0:T(8,128)(2,1)S(1)}, f32[256,256]{1,0:T(8,128)S(1)}, f32[8,256]{1,0:T(8,128)S(1)}) custom-call(f32[8,256,1024]{2,1,0:T(8,128)S(1)} %get-tuple-element.34.slab_ref, f32[8,256]{1,0:T(8,128)S(1)} %get-tuple-element.40.c_ref.refs_2_, f32[256,256]{1,0:T(8,128)S(1)} %get-tuple-element.41.gram_ref, ...), custom_call_target="tpu_custom_call" | custom-call | flops 13421772800 | tf_op jit(solution)/shard_map/ranks/pallas_call | solution.py:333
  30.2 0.4 collective-permute-start.14
  30.7 0.8 %collective-permute-done.14 = f32[8,256]{1,0:T(8,128)S(1)} collective-permute-done((f32[8,256]{1,0:T(8,128)S(1)}, f32[8,256]{1,0:T(8,128)S(1)}, u32[]{:S(2)}, u32[]{:S(2)}) %collective-permute-start.14) | collective-permute-done | bytes 8224 | tf_op jit(solution)/shard_map/ppermute | solution.py:248
  31.5 1.4 %collective-permute-start.15 = (f32[8,256]{1,0:T(8,128)S(1)}, f32[8,256]{1,0:T(8,128)S(1)}, u32[]{:S(2)}, u32[]{:S(2)}) collective-permute-start(f32[8,256]{1,0:T(8,128)S(1)} %add.30.a_ref), channel_id=1, source_target_pairs={{0,4},{1,3},{2,6},{3,1},{4,0},{5,7},{6,2},{7,5},{8,12},{9,11},{10,... | collective-permute-start | bytes 24584 | tf_op jit(solution)/shard_map/ppermute | solution.py:241
  32.9 0.0 collective-permute-done.1
  32.9 0.0 collective-permute-done.8
  32.9 0.1 add_add_fusion
  33.0 2.1 %collective-permute-start.11 = (f32[16,1152]{1,0:T(8,128)S(1)}, f32[16,1152]{1,0:T(8,128)S(1)}, u32[]{:S(2)}, u32[]{:S(2)}) collective-permute-start(f32[16,1152]{1,0:T(8,128)S(1)} %get-tuple-element.58), channel_id=1, source_target_pairs={{0,16},{1,25},{2,18},{3,27},{4,20},{5,29},{6,22},{7,31},{8,24},{9,... | collective-permute-start | bytes 221192 | tf_op jit(solution)/shard_map/ppermute | solution.py:241
  35.1 1.3 %collective-permute-start.10 = (f32[16,1152]{1,0:T(8,128)S(1)}, f32[16,1152]{1,0:T(8,128)S(1)}, u32[]{:S(2)}, u32[]{:S(2)}) collective-permute-start(f32[16,1152]{1,0:T(8,128)S(1)} %get-tuple-element.59), channel_id=1, source_target_pairs={{0,24},{1,17},{2,26},{3,19},{4,28},{5,21},{6,30},{7,23},{8,16},{9,... | collective-permute-start | bytes 221192 | tf_op jit(solution)/shard_map/ppermute | solution.py:241
  36.4 0.2 collective-permute-start.9
  36.5 0.0 collective-permute-done.15.b_ref
  36.6 1.4 %collective-permute-start.17 = (f32[8,256]{1,0:T(8,128)S(1)}, f32[8,256]{1,0:T(8,128)S(1)}, u32[]{:S(2)}, u32[]{:S(2)}) collective-permute-start(f32[8,256]{1,0:T(8,128)S(1)} %sum.1), channel_id=1, source_target_pairs={{0,2},{1,5},{2,0},{3,7},{4,6},{5,1},{6,4},{7,3},{8,10},{9,13},{10,... | collective-permute-start | bytes 24584 | tf_op jit(solution)/shard_map/ppermute | solution.py:241
  38.0 2.2 %rows.1 = (f32[64,256]{1,0:T(8,128)S(1)}, f32[64,256]{1,0:T(8,128)S(1)}) custom-call(bf16[1024,1024]{1,0:T(8,128)(2,1)S(1)} %get-tuple-element.46.high_ref, bf16[1024,1024]{1,0:T(8,128)(2,1)S(1)} %get-tuple-element.47.low_ref, bf16[256,1024]{1,0:T(8,128)(2,1)S(1)} %get-tuple-element.44.bt_high.refs_4_, ...), custom_call_target="tpu_custom_call" | custom-call | flops 536870912 | tf_op jit(solution)/shard_map/rows/pallas_call | solution.py:356
  40.2 0.1 collective-permute-start.16
  40.3 0.0 collective-permute-done.17
  40.3 2.8 %collective-permute-start.18 = (f32[8,256]{1,0:T(8,128)S(1)}, f32[8,256]{1,0:T(8,128)S(1)}, u32[]{:S(2)}, u32[]{:S(2)}) collective-permute-start(f32[8,256]{1,0:T(8,128)S(1)} %add.31.refs_8_), channel_id=1, source_target_pairs={{0,24},{1,25},{2,26},{3,27},{4,28},{5,29},{6,30},{7,31},{8,16},{9,... | collective-permute-start | bytes 24584 | tf_op jit(solution)/shard_map/ppermute | solution.py:241
  43.1 0.0 collective-permute-done.11
  43.1 0.7 %collective-permute-start.19 = (f32[8,256]{1,0:T(8,128)S(1)}, f32[8,256]{1,0:T(8,128)S(1)}, u32[]{:S(2)}, u32[]{:S(2)}) collective-permute-start(f32[8,256]{1,0:T(8,128)S(1)} %add.31.refs_8_), channel_id=1, source_target_pairs={{0,16},{1,17},{2,18},{3,19},{4,20},{5,21},{6,22},{7,23},{8,24},{9,... | collective-permute-start | bytes 24584 | tf_op jit(solution)/shard_map/ppermute | solution.py:241
  43.8 0.0 collective-permute-done.10
  43.8 1.4 %collective-permute-start.20 = (f32[8,256]{1,0:T(8,128)S(1)}, f32[8,256]{1,0:T(8,128)S(1)}, u32[]{:S(2)}, u32[]{:S(2)}) collective-permute-start(f32[8,256]{1,0:T(8,128)S(1)} %add.31.refs_8_), channel_id=1, source_target_pairs={{0,8},{1,9},{2,10},{3,11},{4,12},{5,13},{6,14},{7,15},{8,0},{9,1},... | collective-permute-start | bytes 24584 | tf_op jit(solution)/shard_map/ppermute | solution.py:241
  45.2 0.0 collective-permute-done.9
  45.2 0.1 collective-permute-start.12
  45.3 0.5 %collective-permute-done.18.refs_9_ = f32[8,256]{1,0:T(8,128)S(1)} collective-permute-done((f32[8,256]{1,0:T(8,128)S(1)}, f32[8,256]{1,0:T(8,128)S(1)}, u32[]{:S(2)}, u32[]{:S(2)}) %collective-permute-start.18) | collective-permute-done | bytes 8224 | tf_op jit(solution)/shard_map/ppermute | solution.py:241
  45.8 1.8 %collective-permute-done.19.refs_10_ = f32[8,256]{1,0:T(8,128)S(1)} collective-permute-done((f32[8,256]{1,0:T(8,128)S(1)}, f32[8,256]{1,0:T(8,128)S(1)}, u32[]{:S(2)}, u32[]{:S(2)}) %collective-permute-start.19) | collective-permute-done | bytes 8224 | tf_op jit(solution)/shard_map/ppermute | solution.py:241
  47.6 0.0 collective-permute-done.20.refs_11_
  47.6 0.0 collective-permute-done.16.refs_7_
  47.6 0.0 collective-permute-done.12.refs_1_
  47.6 1.3 %last.1 = (f32[16,1024]{1,0:T(8,128)}, f32[64,256]{1,0:T(8,128)}, f32[8,256]{1,0:T(8,128)}) custom-call(f32[16,128]{1,0:T(8,128)S(1)} %slice.8.refs_0_, f32[16,128]{1,0:T(8,128)S(1)} %collective-permute-done.12.refs_1_, f32[8,256]{1,0:T(8,128)S(1)} %get-tuple-element.40.c_ref.refs_2_, f32[16,1024]{1,0:T(8,128)S(1)} %slice.9.refs_3_, ...), custom_call_target="tpu_custom_call" | custom-call | flops 4194304 | tf_op jit(solution)/shard_map/last/pallas_call | solution.py:371
  (12 shorter events, 0.1 us)
Async XLA Ops:
  0.6 5.8 %collective-permute-start = (f32[64,256]{1,0:T(8,128)}, f32[64,256]{1,0:T(8,128)S(1)}, u32[]{:S(2)}, u32[]{:S(2)}) collective-permute-start(f32[64,256]{1,0:T(8,128)} %a_hbm.1), channel_id=1, source_target_pairs={{0,1},{1,0},{2,3},{3,2},{4,5},{5,4},{6,7},{7,6},{8,9},{9,8},{10,11... | collective-permute-start | bytes 196616 | tf_op jit(solution)/shard_map/ppermute | solution.py:248
  1.1 9.8 %collective-permute-start.3 = (f32[16,1024]{1,0:T(8,128)}, f32[16,1024]{1,0:T(8,128)S(1)}, u32[]{:S(2)}, u32[]{:S(2)}) collective-permute-start(f32[16,1024]{1,0:T(8,128)} %own_hbm.1), channel_id=1, source_target_pairs={{0,16},{1,25},{2,18},{3,27},{4,20},{5,29},{6,22},{7,31},{8,24},{9,... | collective-permute-start | bytes 196616 | tf_op jit(solution)/shard_map/ppermute | solution.py:241
  4.8 6.6 %collective-permute-start.4 = (f32[16,1024]{1,0:T(8,128)}, f32[16,1024]{1,0:T(8,128)S(1)}, u32[]{:S(2)}, u32[]{:S(2)}) collective-permute-start(f32[16,1024]{1,0:T(8,128)} %own_hbm.1), channel_id=1, source_target_pairs={{0,24},{1,17},{2,26},{3,19},{4,28},{5,21},{6,30},{7,23},{8,16},{9,... | collective-permute-start | bytes 196616 | tf_op jit(solution)/shard_map/ppermute | solution.py:241
  6.2 5.9 %collective-permute-start.5 = (f32[16,1024]{1,0:T(8,128)}, f32[16,1024]{1,0:T(8,128)S(1)}, u32[]{:S(2)}, u32[]{:S(2)}) collective-permute-start(f32[16,1024]{1,0:T(8,128)} %own_hbm.1), channel_id=1, source_target_pairs={{0,8},{1,9},{2,10},{3,11},{4,12},{5,13},{6,14},{7,15},{8,0},{9,1},... | collective-permute-start | bytes 196616 | tf_op jit(solution)/shard_map/ppermute | solution.py:241
  12.1 9.1 %collective-permute-start.6 = (f32[64,1024]{1,0:T(8,128)S(1)}, f32[64,1024]{1,0:T(8,128)S(1)}, u32[]{:S(2)}, u32[]{:S(2)}) collective-permute-start(f32[64,1024]{1,0:T(8,128)S(1)} %constant_dynamic-update-slice_fusion.refs_0_), channel_id=1, source_target_pairs={{0,2},{1,5},{2,0},{3,7},{4,6},{5,1},{6,4},{7,3},{8,10},{9,13},{10,... | collective-permute-start | bytes 786440 | tf_op jit(solution)/shard_map/ppermute | solution.py:241
  13.6 9.2 %collective-permute-start.7 = (f32[64,1024]{1,0:T(8,128)S(1)}, f32[64,1024]{1,0:T(8,128)S(1)}, u32[]{:S(2)}, u32[]{:S(2)}) collective-permute-start(f32[64,1024]{1,0:T(8,128)S(1)} %constant_dynamic-update-slice_fusion.refs_0_), channel_id=1, source_target_pairs={{0,4},{1,3},{2,6},{3,1},{4,0},{5,7},{6,2},{7,5},{8,12},{9,11},{10,... | collective-permute-start | bytes 786440 | tf_op jit(solution)/shard_map/ppermute | solution.py:241
  15.1 9.9 %collective-permute-start.2 = (f32[64,1152]{1,0:T(8,128)S(1)}, f32[64,1152]{1,0:T(8,128)S(1)}, u32[]{:S(2)}, u32[]{:S(2)}) collective-permute-start(f32[64,1152]{1,0:T(8,128)S(1)} %get-tuple-element.33), channel_id=1, source_target_pairs={{0,2},{1,5},{2,0},{3,7},{4,6},{5,1},{6,4},{7,3},{8,10},{9,13},{10,... | collective-permute-start | bytes 884744 | tf_op jit(solution)/shard_map/ppermute | solution.py:241
  15.6 17.3 %collective-permute-start.1 = (f32[64,1152]{1,0:T(8,128)S(1)}, f32[64,1152]{1,0:T(8,128)S(1)}, u32[]{:S(2)}, u32[]{:S(2)}) collective-permute-start(f32[64,1152]{1,0:T(8,128)S(1)} %get-tuple-element.31), channel_id=1, source_target_pairs={{0,2},{1,5},{2,0},{3,7},{4,6},{5,1},{6,4},{7,3},{8,10},{9,13},{10,... | collective-permute-start | bytes 884744 | tf_op jit(solution)/shard_map/ppermute | solution.py:241
  22.8 6.4 %collective-permute-start.13 = (f32[64,1024]{1,0:T(8,128)S(1)}, f32[64,1024]{1,0:T(8,128)S(1)}, u32[]{:S(2)}, u32[]{:S(2)}) collective-permute-start(f32[64,1024]{1,0:T(8,128)S(1)} %collective-permute-done.6.refs_1_), channel_id=1, source_target_pairs={{0,4},{1,3},{2,6},{3,1},{4,0},{5,7},{6,2},{7,5},{8,12},{9,11},{10,... | collective-permute-start | bytes 786440 | tf_op jit(solution)/shard_map/ppermute | solution.py:241
  25.0 7.9 %collective-permute-start.8 = (f32[64,1152]{1,0:T(8,128)S(1)}, f32[64,1152]{1,0:T(8,128)S(1)}, u32[]{:S(2)}, u32[]{:S(2)}) collective-permute-start(f32[64,1152]{1,0:T(8,128)S(1)} %add.25), channel_id=1, source_target_pairs={{0,4},{1,3},{2,6},{3,1},{4,0},{5,7},{6,2},{7,5},{8,12},{9,11},{10,... | collective-permute-start | bytes 884744 | tf_op jit(solution)/shard_map/ppermute | solution.py:241
  30.2 1.3 %collective-permute-start.14 = (f32[8,256]{1,0:T(8,128)S(1)}, f32[8,256]{1,0:T(8,128)S(1)}, u32[]{:S(2)}, u32[]{:S(2)}) collective-permute-start(f32[8,256]{1,0:T(8,128)S(1)} %get-tuple-element.50), channel_id=1, source_target_pairs={{0,1},{1,0},{2,3},{3,2},{4,5},{5,4},{6,7},{7,6},{8,9},{9,8},{10,11... | collective-permute-start | bytes 24584 | tf_op jit(solution)/shard_map/ppermute | solution.py:248
  31.5 5.1 %collective-permute-start.15 = (f32[8,256]{1,0:T(8,128)S(1)}, f32[8,256]{1,0:T(8,128)S(1)}, u32[]{:S(2)}, u32[]{:S(2)}) collective-permute-start(f32[8,256]{1,0:T(8,128)S(1)} %add.30.a_ref), channel_id=1, source_target_pairs={{0,4},{1,3},{2,6},{3,1},{4,0},{5,7},{6,2},{7,5},{8,12},{9,11},{10,... | collective-permute-start | bytes 24584 | tf_op jit(solution)/shard_map/ppermute | solution.py:241
  33.0 10.1 %collective-permute-start.11 = (f32[16,1152]{1,0:T(8,128)S(1)}, f32[16,1152]{1,0:T(8,128)S(1)}, u32[]{:S(2)}, u32[]{:S(2)}) collective-permute-start(f32[16,1152]{1,0:T(8,128)S(1)} %get-tuple-element.58), channel_id=1, source_target_pairs={{0,16},{1,25},{2,18},{3,27},{4,20},{5,29},{6,22},{7,31},{8,24},{9,... | collective-permute-start | bytes 221192 | tf_op jit(solution)/shard_map/ppermute | solution.py:241
  35.1 8.7 %collective-permute-start.10 = (f32[16,1152]{1,0:T(8,128)S(1)}, f32[16,1152]{1,0:T(8,128)S(1)}, u32[]{:S(2)}, u32[]{:S(2)}) collective-permute-start(f32[16,1152]{1,0:T(8,128)S(1)} %get-tuple-element.59), channel_id=1, source_target_pairs={{0,24},{1,17},{2,26},{3,19},{4,28},{5,21},{6,30},{7,23},{8,16},{9,... | collective-permute-start | bytes 221192 | tf_op jit(solution)/shard_map/ppermute | solution.py:241
  36.4 8.8 %collective-permute-start.9 = (f32[16,1152]{1,0:T(8,128)S(1)}, f32[16,1152]{1,0:T(8,128)S(1)}, u32[]{:S(2)}, u32[]{:S(2)}) collective-permute-start(f32[16,1152]{1,0:T(8,128)S(1)} %get-tuple-element.57), channel_id=1, source_target_pairs={{0,8},{1,9},{2,10},{3,11},{4,12},{5,13},{6,14},{7,15},{8,0},{9,1},... | collective-permute-start | bytes 221192 | tf_op jit(solution)/shard_map/ppermute | solution.py:241
  36.6 3.7 %collective-permute-start.17 = (f32[8,256]{1,0:T(8,128)S(1)}, f32[8,256]{1,0:T(8,128)S(1)}, u32[]{:S(2)}, u32[]{:S(2)}) collective-permute-start(f32[8,256]{1,0:T(8,128)S(1)} %sum.1), channel_id=1, source_target_pairs={{0,2},{1,5},{2,0},{3,7},{4,6},{5,1},{6,4},{7,3},{8,10},{9,13},{10,... | collective-permute-start | bytes 24584 | tf_op jit(solution)/shard_map/ppermute | solution.py:241
  40.2 7.4 %collective-permute-start.16 = (f32[64,256]{1,0:T(8,128)S(1)}, f32[64,256]{1,0:T(8,128)S(1)}, u32[]{:S(2)}, u32[]{:S(2)}) collective-permute-start(f32[64,256]{1,0:T(8,128)S(1)} %get-tuple-element.53), channel_id=1, source_target_pairs={{0,1},{1,0},{2,3},{3,2},{4,5},{5,4},{6,7},{7,6},{8,9},{9,8},{10,11... | collective-permute-start | bytes 196616 | tf_op jit(solution)/shard_map/ppermute | solution.py:248
  40.3 5.5 %collective-permute-start.18 = (f32[8,256]{1,0:T(8,128)S(1)}, f32[8,256]{1,0:T(8,128)S(1)}, u32[]{:S(2)}, u32[]{:S(2)}) collective-permute-start(f32[8,256]{1,0:T(8,128)S(1)} %add.31.refs_8_), channel_id=1, source_target_pairs={{0,24},{1,25},{2,26},{3,27},{4,28},{5,29},{6,30},{7,31},{8,16},{9,... | collective-permute-start | bytes 24584 | tf_op jit(solution)/shard_map/ppermute | solution.py:241
  43.1 4.6 %collective-permute-start.19 = (f32[8,256]{1,0:T(8,128)S(1)}, f32[8,256]{1,0:T(8,128)S(1)}, u32[]{:S(2)}, u32[]{:S(2)}) collective-permute-start(f32[8,256]{1,0:T(8,128)S(1)} %add.31.refs_8_), channel_id=1, source_target_pairs={{0,16},{1,17},{2,18},{3,19},{4,20},{5,21},{6,22},{7,23},{8,24},{9,... | collective-permute-start | bytes 24584 | tf_op jit(solution)/shard_map/ppermute | solution.py:241
  43.8 3.9 %collective-permute-start.20 = (f32[8,256]{1,0:T(8,128)S(1)}, f32[8,256]{1,0:T(8,128)S(1)}, u32[]{:S(2)}, u32[]{:S(2)}) collective-permute-start(f32[8,256]{1,0:T(8,128)S(1)} %add.31.refs_8_), channel_id=1, source_target_pairs={{0,8},{1,9},{2,10},{3,11},{4,12},{5,13},{6,14},{7,15},{8,0},{9,1},... | collective-permute-start | bytes 24584 | tf_op jit(solution)/shard_map/ppermute | solution.py:241
  45.2 2.4 %collective-permute-start.12 = (f32[16,128]{1,0:T(8,128)S(1)}, f32[16,128]{1,0:T(8,128)S(1)}, u32[]{:S(2)}, u32[]{:S(2)}) collective-permute-start(f32[16,128]{1,0:T(8,128)S(1)} %slice.8.refs_0_), channel_id=1, source_target_pairs={{0,1},{1,0},{2,3},{3,2},{4,5},{5,4},{6,7},{7,6},{8,9},{9,8},{10,11... | collective-permute-start | bytes 24584 | tf_op jit(solution)/shard_map/ppermute | solution.py:248
